TPU v7x, 32 devices: a whole 2x2x4 slice. The times are simulated.
32 devices in a mesh: dp: 8 (over z, y), section: 4 (over x, core).
Axes of the slice: x: 2, y: 2, z: 4, core: 2. Of those that a mesh axis runs over, the one named last changes fastest.
Arguments:
- word_embed: bfloat16 [8192, 768], P(('dp', 'section')), may hold values from -6 to 6
- boxes: int32 [4, 8192], P(None, 'dp'), may hold values from 0 to 1023
- mask_pos: int32 [16, 96], P('dp'), may hold values from -1 to 511, as said below
- replace_ids: int32 [16, 96], P('dp'), may hold values from -1 to 16383, as said below
- cotangent: bfloat16 [8192, 768], P(('dp', 'section')), may hold values from -14 to 14
- layout_table: bfloat16 [2, 1024, 768], replicated, may hold values from -3 to 3
- vocab_table: bfloat16 [16384, 768], P('dp'), may hold values from -6 to 6
- embed_gain: float32 [768], replicated, may hold values from 0.5 to 1.5
- embed_shift: float32 [768], replicated, may hold values from -4 to 4
- qkv_weight: bfloat16 [4, 768, 1152], P('section'), may hold values from -0.21875 to 0.21875
- qv_bias: float32 [4, 2, 384], P('section'), may hold values from -3 to 3
- out_weight: bfloat16 [4, 384, 768], P('section'), may hold values from -1.75 to 1.75
- up_weight: bfloat16 [4, 768, 1536], P('section'), may hold values from -0.21875 to 0.21875
- up_bias: float32 [4, 1536], P('section'), may hold values from -3 to 3
- down_weight: bfloat16 [4, 1536, 768], P('section'), may hold values from -0.109375 to 0.109375
- layer_gains: float32 [2, 2, 768], replicated, may hold values from 0.5 to 1.5
- layer_biases: float32 [2, 4, 768], replicated, may hold values from -3 to 3
Outputs:
- activations: float32 [8192, 768], P(('dp', 'section'))
- input_grad: float32 [8192, 768], P(('dp', 'section'))
- layout_table_grad: float32 [2, 1024, 768], P(None, ('dp', 'section'))
- vocab_table_grad: float32 [16384, 768], P(('dp', 'section'))
- embed_gain_grad: float32 [768], replicated
- embed_shift_grad: float32 [768], replicated
- qkv_weight_grad: float32 [4, 768, 1152], P('section')
- qv_bias_grad: float32 [4, 2, 384], P('section')
- out_weight_grad: float32 [4, 384, 768], P('section')
- up_weight_grad: float32 [4, 768, 1536], P('section')
- up_bias_grad: float32 [4, 1536], P('section')
- down_weight_grad: float32 [4, 1536, 768], P('section')
- layer_gains_grad: float32 [2, 2, 768], replicated
- layer_biases_grad: float32 [2, 4, 768], replicated
Inputs may be any that keep to these rules, and one draw needn't show every extreme that they name: `mask_pos`: each row lists distinct positions of its page first and -1 after them; a row uses between half of 96 and 96 entries, and the first row uses all. `replace_ids`: an entry is -1 exactly where mask_pos is -1, else an id of the table.
All inputs are finite; a program needn't handle non-finite values.
Results may differ from a plain program's by a relative error of at most 0.017.
Values may be sent and summed in bfloat16 or wider, within the bound.
A program may use at most 192 MiB of HBM per device.

v0:
```python
import jax
import jax.numpy as jnp
from jax import lax
from jax.sharding import PartitionSpec as P

HEAD_DIM = 64


EPS = 1e-12
ROOT_HALF = 0.7071067811865476
INV_ROOT_TWO_PI = 0.3989422804014327


def from_partner(block, axis, distance):
    count = lax.axis_size(axis)
    route = []
    for low in range(count):
        high = low | 1 << distance
        if high != low and high < count:
            route += [(low, high), (high, low)]
    return lax.ppermute(block, axis, route)


def from_behind(block, axis, distance):
    devices = range(lax.axis_size(axis))
    route = [(i - distance, i) for i in devices if i - distance in devices]
    return lax.ppermute(block, axis, route)


def passed_along(block, axis, distance):
    devices = range(lax.axis_size(axis))
    route = [((i - distance) % len(devices), i) for i in devices]
    return lax.ppermute(block, axis, route)


def normalize(values, gain, shift):
    center = values - jnp.mean(values, -1, keepdims=True)
    spread = jnp.mean(center * center, -1, keepdims=True)
    inverse = lax.rsqrt(spread + EPS)
    normed = center * inverse
    return (normed * gain + shift, normed, inverse)


def normalize_back(grad, normed, inverse, gain):
    scaled = grad * gain
    centered = (
        scaled
        - jnp.mean(scaled, -1, keepdims=True)
        - normed * jnp.mean(scaled * normed, -1, keepdims=True)
    )
    return (inverse * centered, jnp.sum(grad * normed, 0), jnp.sum(grad, 0))


def gelu_exact(values):
    return 0.5 * values * (1.0 + jax.scipy.special.erf(values * ROOT_HALF))


def gelu_slope(values):
    return (
        0.5 * (1.0 + jax.scipy.special.erf(values * ROOT_HALF))
        + values * jnp.exp(-0.5 * values * values) * INV_ROOT_TWO_PI
    )


def matmul(left, right):
    return jnp.dot(left, right, preferred_element_type=jnp.float32)


def matmul_left_t(left, right):
    return jnp.einsum("pa,pb->ab", left, right, preferred_element_type=jnp.float32)


def matmul_right_t(left, right):
    return jnp.einsum("pa,ba->pb", left, right, preferred_element_type=jnp.float32)


def pair_forward(partial_value):
    return partial_value + from_partner(partial_value, "section", 0)


def pair_backward(partial_value):
    return partial_value + from_partner(partial_value, "section", 0)


def layer_forward(rows, weights):
    w_qkv, b_qv, w_out, w_up, b_up, w_down, gains, shifts = weights
    width = w_out.shape[0]
    heads = width // HEAD_DIM
    length = rows.shape[0]
    scale = HEAD_DIM ** (-0.5)
    rows_low = rows.astype(jnp.bfloat16)
    joined = matmul(rows_low, w_qkv)
    queries = (joined[:, :width] + b_qv[0]).astype(jnp.bfloat16).reshape(length, heads, HEAD_DIM)
    key_rows = joined[:, width : 2 * width].astype(jnp.bfloat16).reshape(length, heads, HEAD_DIM)
    value_rows = (
        (joined[:, 2 * width :] + b_qv[1]).astype(jnp.bfloat16).reshape(length, heads, HEAD_DIM)
    )
    scores = (
        jnp.einsum("qhd,khd->hqk", queries, key_rows, preferred_element_type=jnp.float32) * scale
    )
    highest = jnp.max(scores, -1, keepdims=True)
    expo = jnp.exp(scores - highest)
    probs = expo / jnp.sum(expo, -1, keepdims=True)
    probs_low = probs.astype(jnp.bfloat16)
    context = jnp.einsum("hqk,khd->qhd", probs_low, value_rows, preferred_element_type=jnp.float32)
    context = context.reshape(length, width).astype(jnp.bfloat16)
    attended = pair_forward(matmul(context, w_out)) + shifts[0]
    hidden, normed_one, inverse_one = normalize(rows + attended, gains[0], shifts[1])
    hidden_low = hidden.astype(jnp.bfloat16)
    upper = matmul(hidden_low, w_up) + b_up
    active = gelu_exact(upper).astype(jnp.bfloat16)
    mixed = pair_forward(matmul(active, w_down)) + shifts[2]
    output, normed_two, inverse_two = normalize(hidden + mixed, gains[1], shifts[3])
    kept = (
        rows_low,
        queries,
        key_rows,
        value_rows,
        probs,
        probs_low,
        context,
        normed_one,
        inverse_one,
        hidden_low,
        upper,
        active,
        normed_two,
        inverse_two,
    )
    return (output, kept)


def layer_backward(rows, grad_out, weights):
    w_qkv, b_qv, w_out, w_up, b_up, w_down, gains, shifts = weights
    width = w_out.shape[0]
    heads = width // HEAD_DIM
    length = rows.shape[0]
    scale = HEAD_DIM ** (-0.5)
    recomputed, kept = layer_forward(rows, weights)
    (
        rows_low,
        queries,
        key_rows,
        value_rows,
        probs,
        probs_low,
        context,
        normed_one,
        inverse_one,
        hidden_low,
        upper,
        active,
        normed_two,
        inverse_two,
    ) = kept
    grad_two, gain_two, shift_two = normalize_back(grad_out, normed_two, inverse_two, gains[1])
    grad_mixed = grad_two.astype(jnp.bfloat16)
    shift_down = jnp.sum(grad_mixed.astype(jnp.float32), 0)
    down_grad = matmul_left_t(active, grad_mixed)
    grad_active = matmul_right_t(grad_mixed, w_down)
    grad_upper = (grad_active * gelu_slope(upper)).astype(jnp.bfloat16)
    up_bias_grad = jnp.sum(grad_upper.astype(jnp.float32), 0)
    up_grad = matmul_left_t(hidden_low, grad_upper)
    grad_hidden = grad_two + pair_backward(matmul_right_t(grad_upper, w_up))
    grad_one, gain_one, shift_one = normalize_back(grad_hidden, normed_one, inverse_one, gains[0])
    grad_attended = grad_one.astype(jnp.bfloat16)
    shift_out = jnp.sum(grad_attended.astype(jnp.float32), 0)
    out_grad = matmul_left_t(context, grad_attended)
    grad_context = (
        matmul_right_t(grad_attended, w_out).astype(jnp.bfloat16).reshape(length, heads, HEAD_DIM)
    )
    grad_probs = jnp.einsum(
        "qhd,khd->hqk", grad_context, value_rows, preferred_element_type=jnp.float32
    )
    grad_scores = (probs * (grad_probs - jnp.sum(probs * grad_probs, -1, keepdims=True))).astype(
        jnp.bfloat16
    )
    grad_queries = (
        jnp.einsum("hqk,khd->qhd", grad_scores, key_rows, preferred_element_type=jnp.float32)
        * scale
    ).astype(jnp.bfloat16)
    grad_keys = (
        jnp.einsum("hqk,qhd->khd", grad_scores, queries, preferred_element_type=jnp.float32) * scale
    ).astype(jnp.bfloat16)
    grad_values = jnp.einsum(
        "hqk,qhd->khd", probs_low, grad_context, preferred_element_type=jnp.float32
    ).astype(jnp.bfloat16)
    grad_queries = grad_queries.reshape(length, width)
    grad_values = grad_values.reshape(length, width)
    grad_joined = jnp.concatenate([grad_queries, grad_keys.reshape(length, width), grad_values], 1)
    bias_grad = jnp.stack(
        [jnp.sum(grad_queries.astype(jnp.float32), 0), jnp.sum(grad_values.astype(jnp.float32), 0)]
    )
    joined_grad = matmul_left_t(rows_low, grad_joined)
    grad_rows = grad_one + pair_backward(matmul_right_t(grad_joined, w_qkv))
    gains_grad = jnp.stack([gain_one, gain_two])
    shifts_grad = jnp.stack([shift_out, shift_one, shift_down, shift_two])
    return (
        grad_rows,
        (joined_grad, bias_grad, out_grad, up_grad, up_bias_grad, down_grad),
        (gains_grad, shifts_grad),
    )


def embed_forward(words, boxes, mask_pos, fetched, table, gain, shift_vec, index, page):
    word_rows = lax.dynamic_slice_in_dim(words, index * page, page, 0).astype(jnp.float32)
    box_rows = lax.dynamic_slice_in_dim(boxes, index * page, page, 1)
    listed = lax.dynamic_index_in_dim(mask_pos, index, 0, keepdims=False)
    slot_rows = lax.dynamic_index_in_dim(fetched, index, 0, keepdims=False)
    places = jnp.arange(page, dtype=jnp.int32)
    chosen = (listed[:, None] == places[None, :]).astype(jnp.bfloat16)
    marked = jnp.any(listed[:, None] == places[None, :], axis=0)
    replaced = matmul_left_t(chosen, slot_rows)
    coords = jnp.arange(table.shape[1], dtype=jnp.int32)
    one_x = (box_rows[0][:, None] == coords[None, :]).astype(jnp.bfloat16) + (
        box_rows[2][:, None] == coords[None, :]
    ).astype(jnp.bfloat16)
    one_y = (box_rows[1][:, None] == coords[None, :]).astype(jnp.bfloat16) + (
        box_rows[3][:, None] == coords[None, :]
    ).astype(jnp.bfloat16)
    summed = (
        jnp.where(marked[:, None], replaced, word_rows)
        + matmul(one_x, table[0])
        + matmul(one_y, table[1])
    )
    hidden, normed, inverse = normalize(summed, gain, shift_vec)
    return (hidden, (marked, chosen, one_x, one_y, normed, inverse))


def embed_backward(grad_rows, kept, gain):
    marked, chosen, one_x, one_y, normed, inverse = kept
    grad_summed, gain_grad, shift_grad = normalize_back(grad_rows, normed, inverse, gain)
    grad_low = grad_summed.astype(jnp.bfloat16)
    grad_float = grad_low.astype(jnp.float32)
    word_grad = jnp.where(marked[:, None], 0.0, grad_float)
    slot_grad = matmul(chosen, grad_low).astype(jnp.bfloat16)
    table_grad = jnp.stack([matmul_left_t(one_x, grad_low), matmul_left_t(one_y, grad_low)])
    return (word_grad, table_grad, gain_grad, shift_grad, slot_grad)


def on_device(
    word_embed,
    boxes,
    mask_pos,
    replace_ids,
    cotangent,
    layout_table,
    vocab_table,
    embed_gain,
    embed_shift,
    qkv_weight,
    qv_bias,
    out_weight,
    up_weight,
    up_bias,
    down_weight,
    layer_gains,
    layer_biases,
):
    section = lax.axis_index("section")
    layer = section // 2
    is_first = layer == 0
    words, grads_in = (
        lax.all_gather(word_embed, "section", axis=0, tiled=True),
        lax.all_gather(cotangent, "section", axis=0, tiled=True),
    )
    micro = mask_pos.shape[0]
    slots = mask_pos.shape[1]
    page = words.shape[0] // micro
    width = words.shape[1]
    flat_ids = replace_ids.reshape(-1)
    piece = lax.all_gather(vocab_table, "dp", axis=0, tiled=True)
    columns = jnp.arange(piece.shape[0], dtype=jnp.int32)
    picked = (flat_ids[:, None] == columns[None, :]).astype(jnp.bfloat16)
    fetched = matmul(picked, piece)
    fetched = fetched.astype(jnp.bfloat16).reshape(micro, slots, width)
    weights = (
        qkv_weight[0],
        qv_bias[0],
        out_weight[0],
        up_weight[0],
        up_bias[0],
        down_weight[0],
        lax.dynamic_index_in_dim(layer_gains, layer, 0, keepdims=False),
        lax.dynamic_index_in_dim(layer_biases, layer, 0, keepdims=False),
    )
    grad_shapes = [
        qkv_weight.shape[1:],
        qv_bias.shape[1:],
        out_weight.shape[1:],
        up_weight.shape[1:],
        up_bias.shape[1:],
        down_weight.shape[1:],
    ]

    def embedded(index):
        return embed_forward(
            words, boxes, mask_pos, fetched, layout_table, embed_gain, embed_shift, index, page
        )

    def forward_tick(carry, tick):
        received, stash, finals = carry
        index = tick - layer
        valid = (index >= 0) & (index < micro)
        index = jnp.clip(index, 0, micro - 1)
        first_rows, unused_kept = embedded(index)
        rows = jnp.where(is_first, first_rows, received.astype(jnp.float32))
        output, layer_kept = layer_forward(rows, weights)
        stash = jnp.where(valid, lax.dynamic_update_index_in_dim(stash, rows, index, 0), stash)
        finals = jnp.where(valid, lax.dynamic_update_index_in_dim(finals, output, index, 0), finals)
        received = from_behind(output.astype(jnp.bfloat16), "section", 2)
        return ((received, stash, finals), None)

    blank = jnp.zeros((micro, page, width), jnp.float32)
    ticks = jnp.arange(micro + 1, dtype=jnp.int32)
    start = (jnp.zeros((page, width), jnp.bfloat16), blank, blank)
    (unused_received, stash, finals), unused_out = lax.scan(forward_tick, start, ticks)
    layer_start = tuple((jnp.zeros(shape, jnp.float32) for shape in grad_shapes))
    small_start = (
        jnp.zeros((2, width), jnp.float32),
        jnp.zeros((4, width), jnp.float32),
        jnp.zeros((width,), jnp.float32),
        jnp.zeros((width,), jnp.float32),
    )
    table_start = jnp.zeros(layout_table.shape, jnp.float32)
    slot_start = jnp.zeros((micro, slots, width), jnp.bfloat16)

    def backward_tick(carry, tick):
        received, word_grads, slot_grads, layer_acc, small_acc, table_acc = carry
        index = micro - 1 - tick + (1 - layer)
        valid = (index >= 0) & (index < micro)
        index = jnp.clip(index, 0, micro - 1)
        rows = lax.dynamic_index_in_dim(stash, index, 0, keepdims=False)
        given = lax.dynamic_slice_in_dim(grads_in, index * page, page, 0).astype(jnp.float32)
        grad_out = jnp.where(is_first, received.astype(jnp.float32), given)
        grad_rows, layer_terms, small_terms = layer_backward(rows, grad_out, weights)
        unused_rows, embed_kept = embedded(index)
        word_grad, table_grad, emb_gain_grad, emb_shift_grad, slot_grad = embed_backward(
            grad_rows, embed_kept, embed_gain
        )
        weight_valid = valid.astype(jnp.float32)
        embed_valid = (valid & is_first).astype(jnp.float32)
        word_grads = jnp.where(
            valid & is_first,
            lax.dynamic_update_index_in_dim(word_grads, word_grad, index, 0),
            word_grads,
        )
        slot_grads = jnp.where(
            valid & is_first,
            lax.dynamic_update_index_in_dim(slot_grads, slot_grad, index, 0),
            slot_grads,
        )
        layer_acc = tuple(
            (total + term * weight_valid for total, term in zip(layer_acc, layer_terms))
        )
        small_acc = (
            small_acc[0] + small_terms[0] * weight_valid,
            small_acc[1] + small_terms[1] * weight_valid,
            small_acc[2] + emb_gain_grad * embed_valid,
            small_acc[3] + emb_shift_grad * embed_valid,
        )
        table_acc = table_acc + table_grad * embed_valid
        received = from_behind(grad_rows.astype(jnp.bfloat16), "section", -2)
        return ((received, word_grads, slot_grads, layer_acc, small_acc, table_acc), None)

    start = (
        jnp.zeros((page, width), jnp.bfloat16),
        blank,
        slot_start,
        layer_start,
        small_start,
        table_start,
    )
    (unused_received, word_grads, slot_grads, layer_acc, small_acc, table_acc), unused_out = (
        lax.scan(backward_tick, start, ticks)
    )
    layer_sums = lax.psum(layer_acc, "dp")
    slot = (jnp.arange(2, dtype=jnp.int32) == layer).astype(jnp.float32) * 0.5
    pair_share = is_first.astype(jnp.float32) * 0.5
    first_owner = (section == 0).astype(jnp.float32)
    gains_term = slot[:, None, None] * small_acc[0][None]
    shifts_term = slot[:, None, None] * small_acc[1][None]
    small_sums = lax.psum(
        (gains_term, shifts_term, small_acc[2] * pair_share, small_acc[3] * pair_share),
        ("dp", "section"),
    )
    table_part = lax.psum_scatter(
        table_acc * first_owner, ("dp", "section"), scatter_dimension=1, tiled=True
    )
    slot_rows = slot_grads.reshape(micro * slots, width)
    owner_ids = jnp.where(section == 0, flat_ids, -1)
    rows_here = jnp.arange(
        vocab_table.shape[0] // lax.axis_size("section") * lax.axis_size(("dp", "section")),
        dtype=jnp.int32,
    )
    picked = (rows_here[:, None] == owner_ids[None, :]).astype(jnp.bfloat16)
    vocab_part = lax.psum_scatter(
        matmul(picked, slot_rows), ("dp", "section"), scatter_dimension=0, tiled=True
    )
    mine = jnp.where(layer == 1, finals, word_grads).reshape(micro * page, width)
    quarter = micro * page // lax.axis_size("section")
    target = (section + 2) % lax.axis_size("section")
    sending = lax.dynamic_slice_in_dim(mine, target * quarter, quarter, 0)
    keeping = lax.dynamic_slice_in_dim(mine, section * quarter, quarter, 0)
    arriving = passed_along(sending.astype(jnp.bfloat16), "section", 2).astype(sending.dtype)
    activations = jnp.where(layer == 1, keeping, arriving)
    input_grad = jnp.where(layer == 0, keeping, arriving)
    return (
        activations,
        input_grad,
        table_part,
        vocab_part,
        small_sums[2],
        small_sums[3],
        layer_sums[0][None],
        layer_sums[1][None],
        layer_sums[2][None],
        layer_sums[3][None],
        layer_sums[4][None],
        layer_sums[5][None],
        small_sums[0],
        small_sums[1],
    )


def solution(mesh):
    placed = (
        P(("dp", "section"), None),
        P(None, "dp"),
        P("dp", None),
        P("dp", None),
        P(("dp", "section"), None),
        P(),
        P("dp", None),
        P(),
        P(),
        P("section", None, None),
        P("section", None, None),
        P("section", None, None),
        P("section", None, None),
        P("section", None),
        P("section", None, None),
        P(),
        P(),
    )
    return jax.shard_map(
        on_device,
        mesh=mesh,
        in_specs=placed,
        out_specs=(
            P(("dp", "section"), None),
            P(("dp", "section"), None),
            P(None, ("dp", "section"), None),
            P(("dp", "section"), None),
            P(),
            P(),
            P("section", None, None),
            P("section", None, None),
            P("section", None, None),
            P("section", None, None),
            P("section", None),
            P("section", None, None),
            P(),
            P(),
        ),
        check_vma=False,
    )
```

profile of v0, /device:TPU:0, one launch (start us, length us, event | category | flops | bytes accessed | tf_op | source)
XLA Modules:
  0.0 2135.9 jit_solution(14654825014709779081)
XLA Ops:
  9.7 483.0 %all-gather.4.cloned.1.call-done = bf16[16384,768]{1,0:T(8,128)(2,1)} async-done(((bf16[2048,768]{1,0:T(8,128)(2,1)}), bf16[16384,768]{1,0:T(8,128)(2,1)}) %all-gather.4.cloned.1.call-update) | async-done | bytes 25165840 | tf_op jit(solution)/shard_map/all_gather | solution.py:272
  492.8 11.1 fusion.143
  503.9 10.1 all-gather.6.cloned.1.call-done
  514.0 21.3 all-gather.8.cloned.1.call-done
  539.1 191.0 %while.53 = (s32[]{:T(128)}, bf16[512,768]{1,0:T(8,128)(2,1)S(1)}, f32[2,512,768]{2,1,0:T(8,128)}, f32[2,512,768]{2,1,0:T(8,128)}, pred[]{:T(512)}, /*index=5*/s...) while((s32[]{:T(128)}, bf16[512,768]{1,0:T(8,128)(2,1)S(1)}, ...), condition=%wide.region_10.11_spmd, body=%wide.region_0.10_spmd.sunk | while | flops 5758731776 | bytes 158854064 | solution.py:317
  550.7 4.8 fusion.310
  555.5 3.5 fusion.311
  566.4 6.6 fusion.314
  573.3 3.4 collective-permute-done.1
  583.9 3.4 fusion.317
  587.9 12.6 collective-permute-done.2
  612.9 4.8 fusion.310
  617.7 3.5 fusion.311
  622.0 3.4 collective-permute-done
  628.6 6.6 fusion.314
  635.3 3.5 collective-permute-done.1
  642.9 5.3 collective-permute-start.2
  648.2 3.4 fusion.317
  652.2 12.5 collective-permute-done.2
  677.1 4.8 fusion.310
  681.9 3.5 fusion.311
  686.2 3.4 collective-permute-done
  692.8 6.6 fusion.314
  699.6 3.5 collective-permute-done.1
  707.1 5.3 collective-permute-start.2
  712.4 3.4 fusion.317
  716.4 12.5 collective-permute-done.2
  733.7 378.3 %while.54 = (s32[]{:T(128)}, bf16[512,768]{1,0:T(8,128)(2,1)}, f32[2,512,768]{2,1,0:T(8,128)}, bf16[2,96,768]{2,1,0:T(8,128)(2,1)}, f32[768,1152]{1,0:T(8,128)},...) while((s32[]{:T(128)}, bf16[512,768]{1,0:T(8,128)(2,1)}, ...), condition=%wide.region_39.40_spmd.clone, body=%wide.region_11.39_spmd.clone.sunk | while | flops 15574935552 | bytes 575732480 | solution.py:375
  762.2 4.8 fusion.364
  767.0 3.5 fusion.365
  771.2 3.4 collective-permute-done.3
  795.9 3.2 convert_reduce_fusion.11
  804.2 5.2 select_add_fusion.11
  811.9 4.6 multiply_reduce_fusion.34
  826.1 4.0 fusion.372
  835.2 4.1 fusion.375
  839.4 4.1 multiply_reduce_fusion.36
  853.1 18.2 collective-permute-done.7
  877.5 4.8 fusion.364
  882.3 3.5 fusion.365
  886.6 3.4 collective-permute-done.3
  919.5 6.6 select_add_fusion.11
  928.6 4.6 multiply_reduce_fusion.34
  942.9 4.0 fusion.372
  952.7 4.1 fusion.375
  956.9 4.1 multiply_reduce_fusion.36
  970.5 18.1 collective-permute-done.7
  994.8 4.8 fusion.364
  999.6 3.5 fusion.365
  1003.9 3.4 collective-permute-done.3
  1036.8 6.6 select_add_fusion.11
  1045.9 4.6 multiply_reduce_fusion.34
  1060.2 4.0 fusion.372
  1070.0 4.1 fusion.375
  1074.2 4.1 multiply_reduce_fusion.36
  1087.8 18.1 collective-permute-done.7
  1112.0 5.8 broadcast_multiply_fusion.12
  1118.8 21.9 %fusion.140 = f32[16384,768]{1,0:T(8,128)} fusion(bf16[192,768]{1,0:T(8,128)(2,1)S(1)} %bitcast.328, s32[192]{0:T(256)S(1)} %broadcast_select_fusion.1), kind=kOutput, calls=%fused_computation.247 | convolution fusion | flops 4834983936 | bytes 50627328 | tf_op jit(solution)/shard_map/dot_general | solution.py:66
  1147.0 44.6 %all-reduce = (f32[768]{0:T(1024)}, f32[768]{0:T(1024)}, f32[2,2,768]{2,1,0:T(2,128)}, f32[2,4,768]{2,1,0:T(4,128)}) all-reduce(f32[768]{0:T(1024)S(1)} %get-tuple-element.843, f32[768]{0:T(1024)S(1)} %get-tuple-element.842, f32[2,2,768]{2,1,0:T(2,128)S(1)} %broadcast_multiply_fusion.14, ...), channel_id=1, replica_groups=mesh['dp'=8,'section'=4] {'dp','section'}, use_global_device_ids=true, to_apply=%region_42.43 | all-reduce | flops 10752 | bytes 86016 | tf_op jit(solution)/shard_map/psum | solution.py:383
  1191.6 21.8 %all-reduce.1 = (f32[1,2,384]{2,1,0:T(2,128)}, f32[1,1536]{1,0:T(1,128)}) all-reduce(f32[1,2,384]{2,1,0:T(2,128)S(1)} %bitcast.334, f32[1,1536]{1,0:T(1,128)S(1)} %broadcast_in_dim.168), channel_id=1, replica_groups=mesh['dp'=8,'section'=4] {'dp'}, use_global_device_ids=true, to_apply=%region_45.46 | all-reduce | flops 2304 | bytes 18432 | tf_op jit(solution)/shard_map/psum | solution.py:377
  1215.8 17.8 reduce-scatter.3.cloned.1.call-done
  1233.5 445.8 %all-reduce.5.cloned.1.call-done = (f32[1,768,1152]{2,1,0:T(8,128)}, f32[1,384,768]{2,1,0:T(8,128)}, f32[1,768,1536]{2,1,0:T(8,128)}, f32[1,1536,768]{2,1,0:T(8,128)}) async-done(((f32[1,768,1152]{2,1,0:T(8,128)}, f32[1,384,768]{2,1,0:T(8,128)}, f32[1,768,1536]{2,1,0:T(8,128)}, f32[1,1536,768]{2,1,0:T(8,128)}), (f32[1,768,1152]{2,1,0:T(8,128)}, f32[1,384,768]{2,1,0:T(8,128)}, f32[1,768,1536]{2,1,0:T(8,128)}, ...) | async-done | bytes 14155792 | tf_op jit(solution)/shard_map/psum | solution.py:377
  1679.4 438.7 %reduce-scatter.5.cloned.1.call-done = f32[512,768]{1,0:T(8,128)} async-done(((f32[16384,768]{1,0:T(8,128)}), f32[512,768]{1,0:T(8,128)}) %reduce-scatter.5.cloned.1.call-update) | async-done | bytes 1572880 | tf_op jit(solution)/shard_map/reduce_scatter | solution.py:397
  2118.1 4.2 copy.150
  (922 shorter events, 277.0 us)
Async XLA Ops:
  7.2 485.5 %all-gather.4.cloned.1.call-start = ((), (), s32[]{:S(2)}) async-start(), calls=%async_computation.2 | async-start | bytes 28311552 | tf_op jit(solution)/shard_map/all_gather | solution.py:272
  8.0 506.0 %all-gather.6.cloned.1.call-start = ((), (), s32[]{:S(2)}) async-start(), calls=%async_computation.3 | async-start | bytes 1966080 | tf_op jit(solution)/shard_map/all_gather | solution.py:264
  8.7 526.5 %all-gather.8.cloned.1.call-start = ((), (), s32[]{:S(2)}) async-start(), calls=%async_computation.4 | async-start | bytes 1966080 | tf_op jit(solution)/shard_map/all_gather | solution.py:265
  9.4 1224.1 %reduce-scatter.3.cloned.1.call-start = ((), (), s32[]{:S(2)}) async-start(), calls=%async_computation.5 | async-start | bytes 6488064 | tf_op jit(solution)/shard_map/reduce_scatter | solution.py:387
  9.7 494.2 %copy-start.84 = (s32[192]{0:T(256)}, s32[192]{0:T(256)S(1)}, u32[]{:S(2)}) copy-start(s32[192]{0:T(256)S(1)} %eq.248) | copy-start | bytes 2308
  539.5 7.5 copy-start.18
  559.7 3.6 collective-permute-start
  566.1 7.0 copy-start.4
  573.1 3.6 collective-permute-start.1
  580.8 19.7 collective-permute-start.2
  587.9 13.7 copy-start.23
  601.6 7.5 copy-start.18
  621.8 3.6 collective-permute-start
  635.2 3.6 collective-permute-start.1
  642.9 21.8 %collective-permute-start.2 = (bf16[512,768]{1,0:T(8,128)(2,1)}, bf16[512,768]{1,0:T(8,128)(2,1)}, u32[]{:S(2)}, u32[]{:S(2)}) collective-permute-start(bf16[512,768]{1,0:T(8,128)(2,1)} %fusion.316), channel_id=1, source_target_pairs={{0,2},{1,3},{4,6},{5,7},{8,10},{9,11},{12,14},{13,15},{16,18},{17,... | collective-permute-start | bytes 2359304 | tf_op jit(solution)/shard_map/while/body/eval_jaxpr/ppermute | solution.py:27
  652.2 13.6 copy-start.23
  665.8 7.5 copy-start.18
  686.1 3.6 collective-permute-start
  699.4 3.6 collective-permute-start.1
  707.1 21.8 %collective-permute-start.2 = (bf16[512,768]{1,0:T(8,128)(2,1)}, bf16[512,768]{1,0:T(8,128)(2,1)}, u32[]{:S(2)}, u32[]{:S(2)}) collective-permute-start(bf16[512,768]{1,0:T(8,128)(2,1)} %fusion.316), channel_id=1, source_target_pairs={{0,2},{1,3},{4,6},{5,7},{8,10},{9,11},{12,14},{13,15},{16,18},{17,... | collective-permute-start | bytes 2359304 | tf_op jit(solution)/shard_map/while/body/eval_jaxpr/ppermute | solution.py:27
  716.4 13.6 copy-start.23
  771.1 3.6 collective-permute-start.3
  783.3 5.4 collective-permute-start.4
  788.6 13.4 copy-start.2
  801.7 10.2 collective-permute-start.5
  802.1 7.3 slice-start.2
  809.4 9.2 slice-start.4
  830.1 9.3 collective-permute-start.6
  849.5 21.8 %collective-permute-start.7 = (bf16[512,768]{1,0:T(8,128)(2,1)S(1)}, bf16[512,768]{1,0:T(8,128)(2,1)S(1)}, u32[]{:S(2)}, u32[]{:S(2)}) collective-permute-start(bf16[512,768]{1,0:T(8,128)(2,1)S(1)} %convert_element_type.540), channel_id=1, source_target_pairs={{2,0},{3,1},{6,4},{7,5},{10,8},{11,9},{14,12},{15,13},{18,16},{19,... | collective-permute-start | bytes 2359304 | tf_op jit(solution)/shard_map/while/body/eval_jaxpr/ppermute | solution.py:27
  851.2 21.0 copy-start.14
  851.2 21.0 copy-start.96
  853.1 18.2 copy-start.7
  886.4 3.6 collective-permute-start.3
  898.6 5.4 collective-permute-start.4
  904.0 13.4 copy-start.2
  917.0 11.6 collective-permute-start.5
  917.4 8.7 slice-start.2
  926.1 9.2 slice-start.4
  942.8 7.5 copy-start.56
  942.8 7.5 copy-start.58
  942.8 7.5 copy-start.24
  946.8 10.0 collective-permute-start.6
  966.9 21.7 %collective-permute-start.7 = (bf16[512,768]{1,0:T(8,128)(2,1)S(1)}, bf16[512,768]{1,0:T(8,128)(2,1)S(1)}, u32[]{:S(2)}, u32[]{:S(2)}) collective-permute-start(bf16[512,768]{1,0:T(8,128)(2,1)S(1)} %convert_element_type.540), channel_id=1, source_target_pairs={{2,0},{3,1},{6,4},{7,5},{10,8},{11,9},{14,12},{15,13},{18,16},{19,... | collective-permute-start | bytes 2359304 | tf_op jit(solution)/shard_map/while/body/eval_jaxpr/ppermute | solution.py:27
  968.6 20.9 copy-start.14
  968.6 20.9 copy-start.96
  970.5 18.1 copy-start.7
  1003.7 3.6 collective-permute-start.3
  1015.9 5.4 collective-permute-start.4
  1021.3 13.4 copy-start.2
  1034.4 11.6 collective-permute-start.5
  1034.7 8.7 slice-start.2
  1043.4 9.2 slice-start.4
  1060.2 7.5 copy-start.56
  1060.2 7.5 copy-start.58
  1060.2 7.5 copy-start.24
  1064.1 10.0 collective-permute-start.6
  1084.2 21.7 %collective-permute-start.7 = (bf16[512,768]{1,0:T(8,128)(2,1)S(1)}, bf16[512,768]{1,0:T(8,128)(2,1)S(1)}, u32[]{:S(2)}, u32[]{:S(2)}) collective-permute-start(bf16[512,768]{1,0:T(8,128)(2,1)S(1)} %convert_element_type.540), channel_id=1, source_target_pairs={{2,0},{3,1},{6,4},{7,5},{10,8},{11,9},{14,12},{15,13},{18,16},{19,... | collective-permute-start | bytes 2359304 | tf_op jit(solution)/shard_map/while/body/eval_jaxpr/ppermute | solution.py:27
  1085.9 20.9 copy-start.14
  1086.0 20.9 copy-start.96
  1087.8 18.1 copy-start.7
  1117.8 561.6 %all-reduce.5.cloned.1.call-start = ((), (), s32[]{:S(2)}) async-start(), calls=%async_computation.7 | async-start | bytes 28311552 | tf_op jit(solution)/shard_map/psum | solution.py:377
  1118.4 999.7 %reduce-scatter.5.cloned.1.call-start = ((), (), s32[]{:S(2)}) async-start(), calls=%async_computation.6 | async-start | bytes 51904512 | tf_op jit(solution)/shard_map/reduce_scatter | solution.py:397
  1142.7 48.9 %copy-start.70 = (f32[2,384]{1,0:T(2,128)S(1)}, f32[2,384]{1,0:T(2,128)}, u32[]{:S(2)}) copy-start(f32[2,384]{1,0:T(2,128)} %get-tuple-element.1602) | copy-start | bytes 9220
  1145.2 68.2 %collective-permute-start.8 = (bf16[256,768]{1,0:T(8,128)(2,1)S(1)}, bf16[256,768]{1,0:T(8,128)(2,1)S(1)}, u32[]{:S(2)}, u32[]{:S(2)}) collective-permute-start(bf16[256,768]{1,0:T(8,128)(2,1)S(1)} %dynamic-slice_convert_fusion), channel_id=1, source_target_pairs={{2,0},{3,1},{0,2},{1,3},{6,4},{7,5},{4,6},{5,7},{10,8},{11,9},{8,1... | collective-permute-start | bytes 1179656 | tf_op jit(solution)/shard_map/ppermute | solution.py:33
  (235 other events, 751.2 us)
Sparse Core Ops, SparseCore 0:
  9.6 483.1 all-gather.3
  494.3 19.6 all-gather.5
  515.5 19.6 all-gather.7
  1117.9 115.5 reduce-scatter.2
  1239.9 439.3 all-reduce.4
  1687.3 430.6 reduce-scatter.4
where the time goes:
time: 2140 us
  waiting for transfers between devices  1540 us (72%)
  matrix products  272 us (13%)
  other arithmetic  118 us (6%)
  blocking collectives  66.4 us (3%)
  local copies, waits for them, and re-layouts  64.3 us (3%)
  loops' own time  36.3 us (2%)
  starting transfers between devices  22.5 us (1%)
    all_gather x1, waiting for transfers between devices, on_device(): piece = lax.all_gather(vocab_table, 'dp', axis=0, tiled=True)  483 us
    psum x1, waiting for transfers between devices, on_device(): layer_sums = lax.psum(layer_acc, 'dp')  446 us
    reduce_scatter x1, waiting for transfers between devices, on_device(): lax.psum_scatter(matmul(picked, slot_rows), ('dp', 'section'), scatter_di...  439 us
    dot_general x38, matrix products, matmul(): return jnp.dot(left, right, preferred_element_type=jnp.float32)  117 us
    ppermute x6, waiting for transfers between devices, from_behind(): return lax.ppermute(block, axis, route)  92 us
    dot_general x24, matrix products, matmul_left_t(): jnp.einsum('pa,pb->ab', left, right, preferred_element_type=jnp.float32)  55.5 us
    psum x1, blocking collectives, on_device(): lax.psum((gains_term, shifts_term, small_acc[2] * pair_share, small_acc[3...  44.6 us
  transfers between devices with their start and end apart: 31, of which 21 were waited for; matrix products, arithmetic and copies ran while one was open for 6% of the time, Pallas kernels for 0%

commit v1 on v0

v1 whole, which is shorter than its diff:
```python
import functools

import jax
import jax.numpy as jnp
from jax import lax
from jax.experimental import pallas as pl
from jax.experimental.pallas import tpu as pltpu
from jax.sharding import PartitionSpec as P

HEAD_DIM = 64
EPS = 1e-12
ROOT_HALF = 0.7071067811865476
INV_ROOT_TWO_PI = 0.3989422804014327
BF = jnp.bfloat16
F32 = jnp.float32


def routed(block, route):
    return lax.ppermute(block, "section", route)


SWAP = [(0, 1), (1, 0), (2, 3), (3, 2)]


def swapped(block):
    return routed(block, SWAP)


def normalize(values, gain, shift):
    center = values - jnp.mean(values, -1, keepdims=True)
    spread = jnp.mean(center * center, -1, keepdims=True)
    inverse = lax.rsqrt(spread + EPS)
    normed = center * inverse
    return (normed * gain + shift, normed, inverse)


def normalize_back(grad, normed, inverse, gain):
    scaled = grad * gain
    centered = (
        scaled
        - jnp.mean(scaled, -1, keepdims=True)
        - normed * jnp.mean(scaled * normed, -1, keepdims=True)
    )
    return (inverse * centered, jnp.sum(grad * normed, 0), jnp.sum(grad, 0))


def gelu_exact(values):
    return 0.5 * values * (1.0 + lax.erf(values * ROOT_HALF))


def gelu_slope(values):
    return (
        0.5 * (1.0 + lax.erf(values * ROOT_HALF))
        + values * jnp.exp(-0.5 * values * values) * INV_ROOT_TWO_PI
    )


def matmul(left, right):
    return jnp.dot(left, right, preferred_element_type=F32)


def matmul_left_t(left, right):
    return jnp.einsum("pa,pb->ab", left, right, preferred_element_type=F32)


def matmul_right_t(left, right):
    return jnp.einsum("pa,ba->pb", left, right, preferred_element_type=F32)


def layer_forward(rows, weights):
    w_q, w_k, w_v, b_q, b_v, w_out, w_up, b_up, w_down, gains, shifts = weights
    width = w_out.shape[0]
    heads = width // HEAD_DIM
    length = rows.shape[0]
    scale = HEAD_DIM ** (-0.5)
    rows_low = rows.astype(BF)
    queries = (matmul(rows_low, w_q) + b_q).astype(BF).reshape(length, heads, HEAD_DIM)
    key_rows = matmul(rows_low, w_k).astype(BF).reshape(length, heads, HEAD_DIM)
    value_rows = (matmul(rows_low, w_v) + b_v).astype(BF).reshape(length, heads, HEAD_DIM)
    scores = jnp.einsum("qhd,khd->hqk", queries, key_rows, preferred_element_type=F32) * scale
    highest = jnp.max(scores, -1, keepdims=True)
    expo = jnp.exp(scores - highest)
    probs = expo / jnp.sum(expo, -1, keepdims=True)
    probs_low = probs.astype(BF)
    context = jnp.einsum("hqk,khd->qhd", probs_low, value_rows, preferred_element_type=F32)
    context = context.reshape(length, width).astype(BF)
    attended = matmul(context, w_out) + shifts[0]
    hidden, normed_one, inverse_one = normalize(rows + attended, gains[0], shifts[1])
    hidden_low = hidden.astype(BF)
    upper = matmul(hidden_low, w_up) + b_up
    active = gelu_exact(upper).astype(BF)
    mixed = matmul(active, w_down) + shifts[2]
    output, normed_two, inverse_two = normalize(hidden + mixed, gains[1], shifts[3])
    kept = (
        rows_low, queries, key_rows, value_rows, probs, probs_low, context, normed_one,
        inverse_one, hidden_low, upper, active, normed_two, inverse_two,
    )
    return (output, kept)


def layer_backward(kept, grad_out, weights):
    w_q, w_k, w_v, b_q, b_v, w_out, w_up, b_up, w_down, gains, shifts = weights
    (
        rows_low, queries, key_rows, value_rows, probs, probs_low, context, normed_one,
        inverse_one, hidden_low, upper, active, normed_two, inverse_two,
    ) = kept
    width = w_out.shape[0]
    heads = width // HEAD_DIM
    length = rows_low.shape[0]
    scale = HEAD_DIM ** (-0.5)
    grad_two, gain_two, shift_two = normalize_back(grad_out, normed_two, inverse_two, gains[1])
    grad_mixed = grad_two.astype(BF)
    shift_down = jnp.sum(grad_mixed.astype(F32), 0)
    grad_active = matmul_right_t(grad_mixed, w_down)
    grad_upper = (grad_active * gelu_slope(upper)).astype(BF)
    grad_hidden = grad_two + matmul_right_t(grad_upper, w_up)
    grad_one, gain_one, shift_one = normalize_back(grad_hidden, normed_one, inverse_one, gains[0])
    grad_attended = grad_one.astype(BF)
    shift_out = jnp.sum(grad_attended.astype(F32), 0)
    grad_context = matmul_right_t(grad_attended, w_out).astype(BF).reshape(length, heads, HEAD_DIM)
    grad_probs = jnp.einsum("qhd,khd->hqk", grad_context, value_rows, preferred_element_type=F32)
    grad_scores = (probs * (grad_probs - jnp.sum(probs * grad_probs, -1, keepdims=True))).astype(BF)
    grad_q = (
        jnp.einsum("hqk,khd->qhd", grad_scores, key_rows, preferred_element_type=F32) * scale
    ).astype(BF).reshape(length, width)
    grad_k = (
        jnp.einsum("hqk,qhd->khd", grad_scores, queries, preferred_element_type=F32) * scale
    ).astype(BF).reshape(length, width)
    grad_v = jnp.einsum(
        "hqk,qhd->khd", probs_low, grad_context, preferred_element_type=F32
    ).astype(BF).reshape(length, width)
    grad_rows = (
        grad_one
        + matmul_right_t(grad_q, w_q)
        + matmul_right_t(grad_k, w_k)
        + matmul_right_t(grad_v, w_v)
    )
    gains_grad = jnp.stack([gain_one, gain_two])
    shifts_grad = jnp.stack([shift_out, shift_one, shift_down, shift_two])
    whole = (rows_low, grad_attended, hidden_low, grad_mixed)
    split = (grad_q, grad_k, grad_v, context, grad_upper, active)
    return (grad_rows, whole, split, gains_grad, shifts_grad)


GROUP = 8
BLOCK = 128
HOP = 4
DEPTH = 3


def tree_of(k):
    turn = k % 8
    return turn < 4, 1 + turn % 2, (turn // 2) % 2


def reduce_kernel(
    counts, a_ref, b_ref, small_ref, out_ref, gathered_ref, buf, total, gathered, send, recv,
    out_sem, g_send, g_recv, g_out,
):
    me = lax.axis_index("dp")
    section = lax.axis_index("section")
    z = (me % GROUP) // 2
    y = me % 2
    chunks = buf.shape[1]
    side = buf.shape[3]
    n_q, n_o, n_u, n_d = counts
    mesh_id = pl.DeviceIdType.MESH
    deltas = (-2, 2, 1 - 2 * y)
    exists = (z > 0, z < GROUP // 2 - 1, y >= 0)
    n_sections = lax.axis_size("section")

    barrier = pltpu.get_barrier_semaphore()
    for d in range(3):

        @pl.when(exists[d])
        def _():
            pl.semaphore_signal(
                barrier, inc=1, device_id=(me + deltas[d], section), device_id_type=mesh_id
            )

    for step in range(1, n_sections):
        pl.semaphore_signal(
            barrier, inc=1, device_id=(me, (section + step) % n_sections), device_id_type=mesh_id
        )
    pl.semaphore_wait(
        barrier,
        n_sections + jnp.where(exists[0], 1, 0) + jnp.where(exists[1], 1, 0),
    )

    def roles(k):
        comb, root_z, root_y = tree_of(k)
        along = jnp.logical_or(jnp.logical_not(comb), y == root_y)
        across = jnp.logical_or(comb, z == root_z)
        child = (
            exists[0] & along & (z <= root_z),
            exists[1] & along & (z >= root_z),
            across & (y == root_y),
        )
        up_z = along & (z != root_z)
        up_y = across & (y != root_y)
        parent = jnp.where(up_z, jnp.where(z < root_z, 1, 0), jnp.where(up_y, 2, 3))
        depth = jnp.abs(z - root_z) + jnp.abs(y - root_y)
        return child, parent, depth

    def transfer(k, d, source):
        delta = jnp.where(d == 0, deltas[0], jnp.where(d == 1, deltas[1], deltas[2]))
        there = jnp.where(d == 2, 2, 1 - d)
        return pltpu.make_async_remote_copy(
            src_ref=buf.at[source, k],
            dst_ref=buf.at[there, k],
            send_sem=send.at[d, k],
            recv_sem=recv.at[there, k],
            device_id=(me + delta, section),
            device_id_type=mesh_id,
        )

    def arrived(k, d):
        pltpu.make_async_remote_copy(
            src_ref=buf.at[3, k],
            dst_ref=buf.at[d, k],
            send_sem=send.at[0, k],
            recv_sem=recv.at[d, k],
            device_id=(me, section),
            device_id_type=mesh_id,
        ).wait_recv()

    def result(k, source):
        return pltpu.make_async_copy(buf.at[source, k], out_ref.at[k], out_sem.at[k])

    def product(k):
        kk = k - 1
        in_d = kk < n_d[0] * n_d[1]
        ku = kk - n_d[0] * n_d[1]
        in_u = ku < n_u[0] * n_u[1]
        ko = ku - n_u[0] * n_u[1]
        in_o = ko < n_o[0] * n_o[1]
        kq = ko - n_o[0] * n_o[1]
        a_at = jnp.where(
            in_d,
            n_q[0] + n_o[0] + n_u[0] + kk // n_d[1],
            jnp.where(
                in_u,
                n_q[0] + n_o[0] + ku // n_u[1],
                jnp.where(in_o, n_q[0] + ko // n_o[1], kq // n_q[1]),
            ),
        )
        b_at = jnp.where(
            in_d,
            n_q[1] + n_o[1] + n_u[1] + kk % n_d[1],
            jnp.where(
                in_u,
                n_q[1] + n_o[1] + ku % n_u[1],
                jnp.where(in_o, n_q[1] + ko % n_o[1], kq % n_q[1]),
            ),
        )
        left = a_ref[:, pl.ds(pl.multiple_of(a_at * BLOCK, BLOCK), BLOCK)]
        right = b_ref[:, pl.ds(pl.multiple_of(b_at * side, BLOCK), side)]
        total[...] = lax.dot_general(
            left, right, (((0,), (0,)), ((), ())), preferred_element_type=F32
        )

    def climb(k, level):
        child, parent, depth = roles(k)

        @pl.when((k >= 0) & (k < chunks) & (depth == DEPTH - level))
        def _():
            @pl.when(k == 0)
            def _():
                total[...] = small_ref[...]

            @pl.when(k > 0)
            def _():
                product(k)

            if level > 0:
                for d in range(3):

                    @pl.when(child[d])
                    def _():
                        arrived(k, d)
                        total[...] += buf[d, k].astype(F32)

            buf[3, k] = total[...].astype(BF)
            if level < DEPTH:
                transfer(k, parent, 3).start()
            else:
                for d in range(3):

                    @pl.when(child[d])
                    def _():
                        transfer(k, d, 3).start()

                result(k, 3).start()

    def descend(k, level):
        child, parent, depth = roles(k)

        @pl.when((k >= 0) & (k < chunks) & (depth == level))
        def _():
            arrived(k, parent)
            for d in range(3):

                @pl.when(child[d])
                def _():
                    transfer(k, d, parent).start()

            result(k, parent).start()

    def settle(k):
        child, parent, depth = roles(k)
        for d in range(3):

            @pl.when(child[d] | (parent == d))
            def _():
                transfer(k, d, 3).wait_send()

        result(k, 3).wait()

    def loop(low, high, body):
        def step(k, carry):
            body(k)
            return carry

        lax.fori_loop(low, high, step, 0)

    def advance(t):
        for level in range(DEPTH + 1):
            climb(t - level * HOP, level)
        for level in range(1, DEPTH + 1):
            descend(t - (DEPTH + level) * HOP, level)

    def handed(step):
        return pltpu.make_async_remote_copy(
            src_ref=gathered.at[0],
            dst_ref=gathered.at[step],
            send_sem=g_send.at[step],
            recv_sem=g_recv.at[step],
            device_id=(me, (section + n_sections - step) % n_sections),
            device_id_type=mesh_id,
        )

    last = 2 * DEPTH * HOP
    loop(0, last + HOP, advance)
    mine = roles(0)[1]
    rows = gathered.shape[1]
    gathered[0] = buf[mine, 0, :rows]
    for step in range(1, n_sections):
        handed(step).start()
    loop(last + HOP, chunks + last, advance)
    for step in range(1, n_sections):
        handed(step).wait()
    to_out = pltpu.make_async_copy(gathered, gathered_ref, g_out)
    to_out.start()
    loop(0, chunks, settle)
    to_out.wait()


def reduced(a, b, small, counts, side):
    chunks = 1 + sum(rows * columns for rows, columns in counts)
    n_sections = lax.axis_size("section")
    kept = 32
    any_space = pl.BlockSpec(memory_space=pl.ANY)
    in_vmem = pl.BlockSpec(memory_space=pltpu.VMEM)
    flops = 2 * a.shape[0] * BLOCK * side * chunks
    return pl.pallas_call(
        functools.partial(reduce_kernel, counts),
        out_shape=(
            jax.ShapeDtypeStruct((chunks, BLOCK, side), BF),
            jax.ShapeDtypeStruct((n_sections, kept, side), BF),
        ),
        in_specs=[in_vmem] * 3,
        out_specs=(any_space, any_space),
        scratch_shapes=[
            pltpu.VMEM((4, chunks, BLOCK, side), BF),
            pltpu.VMEM((BLOCK, side), F32),
            pltpu.VMEM((n_sections, kept, side), BF),
            pltpu.SemaphoreType.DMA((3, chunks)),
            pltpu.SemaphoreType.DMA((3, chunks)),
            pltpu.SemaphoreType.DMA((chunks,)),
            pltpu.SemaphoreType.DMA((n_sections,)),
            pltpu.SemaphoreType.DMA((n_sections,)),
            pltpu.SemaphoreType.DMA,
        ],
        compiler_params=pltpu.CompilerParams(
            collective_id=0, has_side_effects=True, vmem_limit_bytes=60 << 20
        ),
        cost_estimate=pl.CostEstimate(
            flops=flops, bytes_accessed=400 << 20, transcendentals=0
        ),
        name="gradient_sums",
    )(a, b, small)


def on_device(
    word_embed, boxes, mask_pos, replace_ids, cotangent, layout_table, vocab_table, embed_gain,
    embed_shift, qkv_weight, qv_bias, out_weight, up_weight, up_bias, down_weight, layer_gains,
    layer_biases,
):
    section = lax.axis_index("section")
    layer = section // 2
    half = section % 2
    is_first = layer == 0
    quarter, width = word_embed.shape
    page = 2 * quarter
    side = qkv_weight.shape[2] // 3

    words_a = routed(word_embed, [(1, 0), (2, 1)])
    words_b = routed(word_embed, [(3, 1)])
    given_a = routed(cotangent, [(0, 2), (2, 3)])
    given_b = routed(cotangent, [(1, 2)])
    words = jnp.concatenate(
        [jnp.where(half == 0, word_embed, words_a), jnp.where(half == 0, words_a, words_b)], 0
    )
    given = jnp.concatenate(
        [given_a, jnp.where(half == 0, given_b, cotangent)], 0
    ).astype(F32)

    qkv_other, out_other, up_other, down_other, qvb_other, upb_other = (
        swapped(array[0])
        for array in (qkv_weight, out_weight, up_weight, down_weight, qv_bias, up_bias)
    )
    qkv_own = qkv_weight[0]
    weights = (
        jnp.concatenate([qkv_own[:, :side], qkv_other[:, :side]], 1),
        jnp.concatenate([qkv_own[:, side : 2 * side], qkv_other[:, side : 2 * side]], 1),
        jnp.concatenate([qkv_own[:, 2 * side :], qkv_other[:, 2 * side :]], 1),
        jnp.concatenate([qv_bias[0, 0], qvb_other[0]]),
        jnp.concatenate([qv_bias[0, 1], qvb_other[1]]),
        jnp.concatenate([out_weight[0], out_other], 0),
        jnp.concatenate([up_weight[0], up_other], 1),
        jnp.concatenate([up_bias[0], upb_other]),
        jnp.concatenate([down_weight[0], down_other], 0),
        lax.dynamic_index_in_dim(layer_gains, layer, 0, keepdims=False),
        lax.dynamic_index_in_dim(layer_biases, layer, 0, keepdims=False),
    )

    listed = lax.dynamic_index_in_dim(mask_pos, half, 0, keepdims=False)
    ids = lax.dynamic_index_in_dim(replace_ids, half, 0, keepdims=False)
    slots = ids.shape[0]
    rows_held = vocab_table.shape[0]
    asked = lax.all_gather(ids, "dp", axis=0, tiled=True)
    held = jnp.arange(rows_held, dtype=jnp.int32) + lax.axis_index("dp") * rows_held
    picked = (asked[:, None] == held[None, :]).astype(BF)
    slot_rows = lax.psum_scatter(
        matmul(picked, vocab_table).astype(BF), "dp", scatter_dimension=0, tiled=True
    )

    places = jnp.arange(page, dtype=jnp.int32)
    chosen = (listed[:, None] == places[None, :]).astype(BF)
    marked = jnp.any(listed[:, None] == places[None, :], axis=0)
    replaced = matmul_left_t(chosen, slot_rows)
    box_rows = lax.dynamic_slice_in_dim(boxes, half * page, page, 1)
    coords = jnp.arange(layout_table.shape[1], dtype=jnp.int32)
    one_x, one_y = (
        (box_rows[a][:, None] == coords[None, :]).astype(BF)
        + (box_rows[a + 2][:, None] == coords[None, :]).astype(BF)
        for a in (0, 1)
    )
    summed = (
        jnp.where(marked[:, None], replaced, words.astype(F32))
        + matmul(one_x, layout_table[0])
        + matmul(one_y, layout_table[1])
    )
    hidden_in, normed_in, inverse_in = normalize(summed, embed_gain, embed_shift)

    first_out, unused_kept = layer_forward(hidden_in, weights)
    second_in = routed(first_out.astype(BF), [(0, 2), (1, 3)])
    rows = jnp.where(is_first, hidden_in, second_in.astype(F32))
    output, kept = layer_forward(rows, weights)
    second_grad = layer_backward(kept, given, weights)[0]
    first_grad = routed(second_grad.astype(BF), [(2, 0), (3, 1)])
    grad_out = jnp.where(is_first, first_grad.astype(F32), given)
    grad_rows, whole, split, gains_grad, shifts_grad = layer_backward(kept, grad_out, weights)

    grad_summed, eg_grad, es_grad = normalize_back(grad_rows, normed_in, inverse_in, embed_gain)
    grad_low = jnp.where(is_first, grad_summed, 0.0).astype(BF)
    word_grad = jnp.where(marked[:, None], 0.0, grad_low.astype(F32))
    slot_grad = matmul(chosen, grad_low).astype(BF)
    table_grad = jnp.stack([matmul_left_t(one_x, grad_low), matmul_left_t(one_y, grad_low)])
    table_part = lax.psum_scatter(
        table_grad.astype(BF), ("dp", "section"), scatter_dimension=1, tiled=True
    ).astype(F32)

    mine = jnp.where(
        is_first,
        slot_grad[: slots // 2],
        routed(slot_grad[slots // 2 :], [(0, 2), (1, 3)]),
    )
    my_ids = jnp.where(is_first, ids[: slots // 2], ids[slots // 2 :])
    all_rows = lax.all_gather(mine, ("dp", "section"), axis=0, tiled=True)
    all_ids = lax.all_gather(my_ids, ("dp", "section"), axis=0, tiled=True)
    count = rows_held // lax.axis_size("section")
    base = (lax.axis_index("dp") * lax.axis_size("section") + section) * count
    rows_here = jnp.arange(count, dtype=jnp.int32) + base
    vocab_part = matmul((rows_here[:, None] == all_ids[None, :]).astype(BF), all_rows)

    def both(array, columns):
        return jnp.concatenate([array[:, :columns], swapped(array[:, columns:])], 0)

    rows_low, grad_attended, hidden_low, grad_mixed = (
        jnp.concatenate([array, swapped(array)], 0) for array in whole
    )
    grad_q, grad_k, grad_v, context, grad_upper, active = (
        both(array, array.shape[1] // 2) for array in split
    )
    left = jnp.concatenate([rows_low, context, hidden_low, active], 1)
    right = jnp.concatenate([grad_q, grad_k, grad_v, grad_attended, grad_upper, grad_mixed], 1)
    hidden_units = grad_upper.shape[1]
    counts = (
        (width // BLOCK, 3),
        (side // BLOCK, width // side),
        (width // BLOCK, hidden_units // side),
        (hidden_units // BLOCK, width // side),
    )
    flat = jnp.concatenate(
        [
            jnp.sum(grad_q.astype(F32), 0), jnp.sum(grad_v.astype(F32), 0),
            jnp.sum(grad_upper.astype(F32), 0), gains_grad.reshape(-1), shifts_grad.reshape(-1),
            eg_grad, es_grad,
        ]
    ).reshape(-1, side)
    small_in = jnp.pad(flat, ((0, BLOCK - flat.shape[0]), (0, 0)))
    chunked, gathered = reduced(left, right, small_in, counts, side)
    outer = lax.axis_size("dp") // GROUP
    if outer > 1:
        groups = [[i + GROUP * g for g in range(outer)] for i in range(GROUP)]
        chunked, gathered = lax.psum((chunked, gathered), "dp", axis_index_groups=groups)
    chunked = chunked[1:]

    def laid(start, count):
        rows_of, columns_of = count
        part = chunked[start : start + rows_of * columns_of].astype(F32)
        part = part.reshape(rows_of, columns_of, BLOCK, side).transpose(0, 2, 1, 3)
        return part.reshape(1, rows_of * BLOCK, columns_of * side)

    n_q, n_o, n_u, n_d = (rows_of * columns_of for rows_of, columns_of in counts)
    sums = (
        laid(n_d + n_u + n_o, counts[0]), laid(n_d + n_u, counts[1]), laid(n_d, counts[2]),
        laid(0, counts[3]),
    )
    parts = gathered.astype(F32)[:, : flat.shape[0]].reshape(4, -1)
    own = parts[0]
    in_order = jnp.stack(
        [parts[0] + parts[jnp.where(half == 0, 1, 3)], parts[2] + parts[jnp.where(half == 0, 3, 1)]]
    )
    low_edge = 2 * side + hidden_units
    by_layer = jnp.where(layer == 0, in_order, in_order[::-1])[:, low_edge:]
    small = (
        by_layer[:, : 2 * width].reshape(2, 2, width),
        by_layer[:, 2 * width : 6 * width].reshape(2, 4, width),
        by_layer[0, 6 * width : 7 * width],
        by_layer[0, 7 * width :],
        own[: 2 * side].reshape(1, 2, side),
        own[2 * side : low_edge].reshape(1, hidden_units),
    )

    out_first = output[:quarter].astype(BF)
    out_second = output[quarter:].astype(BF)
    act_a = routed(out_first, [(2, 0), (3, 2)])
    act_b = routed(out_second, [(2, 1)])
    grad_first = word_grad[:quarter].astype(BF)
    grad_second = word_grad[quarter:].astype(BF)
    ing_a = routed(grad_second, [(0, 1), (1, 3)])
    ing_b = routed(grad_first, [(1, 2)])
    activations = jnp.where(
        section == 3,
        output[quarter:],
        jnp.where(section == 1, act_b, act_a).astype(F32),
    )
    input_grad = jnp.where(
        section == 0,
        word_grad[:quarter],
        jnp.where(section == 2, ing_b, ing_a).astype(F32),
    )
    return (
        activations, input_grad, table_part, vocab_part, small[2], small[3],
        sums[0],
        small[4],
        sums[1], sums[2],
        small[5],
        sums[3], small[0], small[1],
    )


def solution(mesh):
    both = ("dp", "section")
    by_section = P("section", None, None)
    return jax.shard_map(
        on_device,
        mesh=mesh,
        in_specs=(
            P(both, None), P(None, "dp"), P("dp", None), P("dp", None), P(both, None), P(),
            P("dp", None), P(), P(), by_section, by_section, by_section, by_section,
            P("section", None), by_section, P(), P(),
        ),
        out_specs=(
            P(both, None), P(both, None), P(None, both, None), P(both, None), P(), P(),
            by_section, by_section, by_section, by_section, P("section", None), by_section,
            P(), P(),
        ),
        check_vma=False,
    )
```

time: 2140 us -> 733 us (0.34)
  waiting for transfers between devices: 1540 us -> 85.2 us
  Pallas kernels: 0 us -> 151 us
  matrix products: 272 us -> 167 us
  local copies, waits for them, and re-layouts: 64.3 us -> 127 us
  loops' own time: 36.3 us -> 0 us
  other arithmetic: 118 us -> 93.2 us
    all_gather x3 -> x1, waiting for transfers between devices: 514 us -> 0.01 us  [on_device(): all_rows = lax.all_gather(mine, ('dp', 'section'), axis=0, tiled=True)]
    psum x1 -> x0, waiting for transfers between devices: 446 us -> none  [on_device(): layer_sums = lax.psum(layer_acc, 'dp')]
    reduce_scatter x2, waiting for transfers between devices: 456 us -> 43.7 us  [the longest x1 43.7 us: on_device(): lax.psum_scatter(matmul(picked, vocab_table).astype(BF), 'dp', scatter_di...]
    pallas_call x0 -> x1, Pallas kernels: none -> 151 us  [reduced(): pl.pallas_call(functools.partial(reduce_kernel, counts), out_shape=(jax.S...]
    dot_general x77 -> x32, matrix products: 210 us -> 105 us  [the longest x16 53.7 us: matmul(): return jnp.dot(left, right, preferred_element_type=F32)]
    ppermute x25 -> x27, waiting for transfers between devices: 123 us -> 41.5 us  [routed(): return lax.ppermute(block, 'section', route)]
    psum x2 -> x0, blocking collectives: 66.4 us -> none  [the longest x1 44.6 us: on_device(): lax.psum((gains_term, shifts_term, small_acc[2] * pair_share, small_acc[3...]
    unnamed x0 -> x2, blocking collectives: none -> 52.1 us
  transfers between devices with their start and end apart: 31 -> 30, of which waited for: 21 -> 6; matrix products, arithmetic and copies ran while one was open for 6% -> 32% of each run, Pallas kernels for 0% -> 21%
where the time goes in v1:
time: 733 us; the launch traced here: 723 us
  matrix products  167 us (23%)
  Pallas kernels  151 us (21%)
  local copies, waits for them, and re-layouts  127 us (17%)
  other arithmetic  93.2 us (13%)
  waiting for transfers between devices  85.2 us (12%)
  blocking collectives  52.1 us (7%)
  starting transfers between devices  30.3 us (4%)
  between operations  17 us (2%)
    pallas_call x1, Pallas kernels, reduced(): pl.pallas_call(functools.partial(reduce_kernel, counts), out_shape=(jax.S...  151 us
    dot_general x16, matrix products, matmul(): return jnp.dot(left, right, preferred_element_type=F32)  53.7 us
    unnamed x2, blocking collectives  52.1 us
    reduce_scatter x1, waiting for transfers between devices, on_device(): lax.psum_scatter(matmul(picked, vocab_table).astype(BF), 'dp', scatter_di...  43.7 us
    dot_general x11, matrix products, matmul_right_t(): return jnp.einsum('pa,ba->pb', left, right, preferred_element_type=F32)  42.4 us
    ppermute x27, waiting for transfers between devices, routed(): return lax.ppermute(block, 'section', route)  41.5 us
    unnamed x348, local copies, waits for them, and re-layouts  39.9 us
    concatenate x1, other arithmetic, on_device(): left = jnp.concatenate([rows_low, context, hidden_low, active], 1)  38 us
  transfers between devices with their start and end apart: 30, of which 6 were waited for; matrix products, arithmetic and copies ran while one was open for 32% of the time, Pallas kernels for 21%

profile of v1, /device:TPU:0, one launch (start us, length us, event | category | flops | bytes accessed | tf_op | source)
XLA Modules:
  0.0 722.8 jit_solution(6267876706875171916)
XLA Ops:
  10.5 13.6 %all-reduce.1 = s32[768]{0:T(1024)} all-reduce(s32[768]{0:T(1024)S(1)} %get-tuple-element.80), channel_id=2, replica_groups=mesh['dp'=8,'section'=4] {'dp'}, use_global_device_ids=true, to_apply=%add.1 | all-reduce | flops 768 | bytes 6144
  24.2 4.4 fusion.40
  33.9 2.9 fusion.130
  36.8 2.4 fusion.32
  39.2 2.4 fusion.34
  44.8 2.7 fusion.131
  47.5 43.7 %reduce-scatter.3.cloned.1.call-done = bf16[96,768]{1,0:T(8,128)(2,1)} async-done(((bf16[768,768]{1,0:T(8,128)(2,1)}), bf16[96,768]{1,0:T(8,128)(2,1)}) %reduce-scatter.3.cloned.1.call-update) | async-done | bytes 147472 | tf_op jit(solution)/shard_map/reduce_scatter | solution.py:444
  91.2 2.6 fusion.138
  97.3 2.3 copy.93
  99.6 3.1 convolution_convert_fusion.5
  102.8 2.3 copy.94
  105.1 2.8 add_convert_fusion.5
  107.9 2.4 copy.92
  110.3 7.3 %fusion.139 = (f32[12,512]{1,0:T(8,128)S(1)}, f32[12,512,512]{1,2,0:T(8,128)}) fusion(bf16[512,12,64]{0,2,1:T(8,128)(2,1)S(1)} %bitcast.168, bf16[512,12,64]{0,2,1:T(8,128)(2,1)S(1)} %bitcast.169), kind=kOutput, calls=%fused_computation.281 | convolution fusion | flops 412090880 | bytes 14180352 | tf_op jit(solution)/shard_map/sub | solution.py:82
  117.6 6.1 fusion.49
  127.0 10.0 %fusion.141 = (f32[512]{0:T(512)S(1)}, f32[512,768]{1,0:T(8,128)S(1)}) fusion(f32[768]{0:T(1024)S(1)} %copy-done.120, bf16[1536,768]{1,0:T(8,128)(2,1)} %collective-permute-done.7, bf16[1536,768]{1,0:T(8,128)(2,1)} %bitcast.190, f32[3072]{0:T(1024)S(1)} %copy-done.109, f32[512,768]{1,0:T(8,128)} %copy-done.42, f32[768]{0:T(1024)S(1)} %copy-done.102, ...), kind=kOutput, calls=%fused_computation.283 | convolution fusion | flops 4864867840 | bytes 12610560 | tf_op jit(solution)/shard_map/dot_general | solution.py:59
  138.9 3.5 collective-permute-start.8
  143.1 2.8 collective-permute-start.11
  146.0 14.7 %collective-permute-done.8 = bf16[512,768]{1,0:T(8,128)(2,1)S(1)} collective-permute-done((bf16[512,768]{1,0:T(8,128)(2,1)}, bf16[512,768]{1,0:T(8,128)(2,1)S(1)}, u32[]{:S(2)}, u32[]{:S(2)}) %collective-permute-start.8) | collective-permute-done | bytes 786464 | tf_op jit(solution)/shard_map/ppermute | solution.py:19
  170.0 2.6 copy.96
  172.6 7.7 %fusion.144 = (f32[12,512]{1,0:T(8,128)}, f32[12,512,512]{1,2,0:T(8,128)}) fusion(bf16[512,12,64]{0,2,1:T(8,128)(2,1)S(1)} %bitcast.149, bf16[512,12,64]{0,2,1:T(8,128)(2,1)S(1)} %bitcast.143), kind=kOutput, calls=%fused_computation.284 | convolution fusion | flops 412090880 | bytes 14180352 | tf_op jit(solution)/shard_map/sub | solution.py:82
  180.3 6.0 convolution_convert_fusion.8
  186.4 2.4 fusion.145
  190.9 5.9 multiply_convert_fusion.4
  196.9 5.6 fusion.146
  205.8 14.2 %fusion.124 = (f32[512]{0:T(512)}, f32[512]{0:T(512)}, f32[512,768]{1,0:T(8,128)}) fusion(f32[512]{0:T(512)} %copy-done.89, f32[512,768]{1,0:T(8,128)S(1)} %get-tuple-element.128, f32[512]{0:T(512)S(1)} %broadcast_multiply_fusion.11, f32[768]{0:T(1024)} %copy-done.83, bf16[768,1536]{1,0:T(8,128)(2,1)} %collective-permute-done.5, ...), kind=kOutput, calls=%fused_computation.268 | convolution fusion | flops 4879809536 | bytes 21268480 | tf_op jit(solution)/shard_map/pa,ba->pb/dot_general | solution.py:67
  222.0 3.6 convolution_convert_fusion.3
  225.6 2.3 copy.100
  227.9 6.9 convolution_convert_fusion.7
  234.8 8.9 %multiply_reduce_fusion.1 = (f32[12,512]{1,0:T(8,128)S(1)}, f32[12,512,512]{1,2,0:T(8,128)}) fusion(f32[12,512,512]{1,2,0:T(8,128)} %get-tuple-element.126, f32[12,512]{1,0:T(8,128)S(1)} %copy-done.78, bf16[512,12,64]{0,2,1:T(8,128)(2,1)S(1)} %bitcast.174, bf16[512,12,64]{0,2,1:T(8,128)(2,1)S(1)} %bitcast.166), kind=kOutput, calls=%fused_computation.5 | convolution fusion | flops 412084224 | bytes 26787840 | tf_op jit(solution)/shard_map/qhd,khd->hqk/dot_general | solution.py:121
  243.8 6.8 multiply_convert_fusion.1
  259.5 23.6 %collective-permute-done.13 = bf16[512,768]{1,0:T(8,128)(2,1)S(1)} collective-permute-done((bf16[512,768]{1,0:T(8,128)(2,1)S(1)}, bf16[512,768]{1,0:T(8,128)(2,1)S(1)}, u32[]{:S(2)}, u32[]{:S(2)}) %collective-permute-start.13) | collective-permute-done | bytes 786464 | tf_op jit(solution)/shard_map/ppermute | solution.py:19
  283.1 2.4 multiply_reduce_fusion.5
  285.5 3.9 convert_reduce_fusion.1
  289.4 7.9 %multiply_convert_fusion.2 = bf16[512,3072]{1,0:T(8,128)(2,1)S(1)} fusion(bf16[512,768]{1,0:T(8,128)(2,1)} %get-tuple-element.77, f32[512,3072]{1,0:T(8,128)S(1)} %bitcast.206, f32[3072]{0:T(1024)S(1)} %copy-done.111, bf16[1536,768]{1,0:T(8,128)(2,1)} %collective-permute-done.7, bf16[1536,768]{1,0:T(8,128)(2,1)S(1)} %bitcast.193), kind=kOutput, calls=%fused_computation.20 | convolution fusion | flops 2442657792 | bytes 14954496 | tf_op jit(solution)/shard_map/pa,ba->pb/dot_general | solution.py:67
  297.3 6.9 multiply_reduce_fusion.6
  306.3 2.8 convolution_convert_fusion.2
  309.1 2.3 copy.104
  311.4 7.0 convolution_convert_fusion.6
  318.5 9.2 %multiply_reduce_fusion = (f32[12,512]{1,0:T(8,128)S(1)}, f32[12,512,512]{1,2,0:T(8,128)}) fusion(f32[12,512,512]{1,2,0:T(8,128)} %get-tuple-element.126, f32[12,512]{1,0:T(8,128)S(1)} %copy-done.79, bf16[512,12,64]{0,2,1:T(8,128)(2,1)S(1)} %bitcast.172, bf16[512,12,64]{0,2,1:T(8,128)(2,1)S(1)} %bitcast.167), kind=kOutput, calls=%fused_computation.3 | convolution fusion | flops 412084224 | bytes 26787840 | tf_op jit(solution)/shard_map/qhd,khd->hqk/dot_general | solution.py:121
  327.7 7.2 multiply_convert_fusion
  341.4 2.5 multiply_reduce_fusion.4
  351.3 38.4 %all-reduce.2 = s32[1536]{0:T(1024)} all-reduce(s32[1536]{0:T(1024)S(1)} %fusion.102), channel_id=3, replica_groups=mesh['dp'=8,'section'=4] {'dp','section'}, use_global_device_ids=true, to_apply=%add.2 | all-reduce | flops 1536 | bytes 12288
  390.3 3.3 fusion.129
  409.2 4.8 collective-permute-start.16
  414.9 3.3 fusion.128
  424.2 2.4 collective-permute-start.15
  436.3 2.6 collective-permute-done.10
  441.8 4.3 collective-permute-start.18
  447.9 2.8 copy-done.81
  450.8 38.0 %maximum_maximum_fusion.a_ref = bf16[1024,3456]{1,0:T(8,128)(2,1)} fusion(bf16[512,1536]{1,0:T(8,128)(2,1)} %collective-permute-done.20, bf16[512,1536]{1,0:T(8,128)(2,1)S(1)} %get-tuple-element.86, bf16[512,768]{1,0:T(8,128)(2,1)S(1)} %collective-permute-done.19, bf16[512,768]{1,0:T(8,128)(2,1)S(1)} %copy-done.35, ...), kind=kLoop, calls=%fused_computation.14 | loop fusion | flops 56623104 | bytes 14155776 | tf_op jit(solution)/shard_map/concatenate | solution.py:506
  497.9 3.3 fusion.25
  501.2 2.7 maximum_dynamic-update-slice_fusion.b_ref
  503.9 151.1 %gradient_sums.1 = (bf16[73,128,384]{2,1,0:T(8,128)(2,1)}, bf16[4,32,384]{2,1,0:T(8,128)(2,1)}) custom-call(bf16[1024,3456]{1,0:T(8,128)(2,1)} %maximum_maximum_fusion.a_ref, bf16[1024,4224]{1,0:T(8,128)(2,1)} %maximum_dynamic-update-slice_fusion.b_ref, f32[128,384]{1,0:T(8,128)} %pad.4.small_ref), custom_call_target="tpu_custom_call" | custom-call | flops 7348420608 | bytes 419430400 | tf_op jit(solution)/shard_map/gradient_sums/pallas_call | solution.py:365
  655.0 3.0 slice.253
  661.8 3.1 fusion.127
  665.5 5.2 copy.118
  670.7 6.6 reshape.328
  677.8 5.8 copy.119
  683.7 7.3 %reshape.330 = f32[1,1536,768]{2,1,0:T(8,128)} reshape(f32[12,128,2,384]{3,2,1,0:T(2,128)} %copy.119) | data formatting | bytes 9437184 | tf_op jit(solution)/shard_map/reshape | solution.py:534
  691.0 3.2 copy.116
  694.2 5.0 reshape.324
  699.2 5.2 copy.120
  711.4 4.4 fusion.19
  (521 shorter events, 119.4 us)
Async XLA Ops:
  7.2 17.0 %copy-start = (bf16[2048,768]{1,0:T(8,128)(2,1)S(1)}, bf16[2048,768]{1,0:T(8,128)(2,1)}, u32[]{:S(2)}) copy-start(bf16[2048,768]{1,0:T(8,128)(2,1)} %param.23) | copy-start | bytes 9437188
  7.2 84.0 %reduce-scatter.3.cloned.1.call-start = ((), (), s32[]{:S(2)}) async-start(), calls=%async_computation.2 | async-start | bytes 1327104 | tf_op jit(solution)/shard_map/reduce_scatter | solution.py:444
  24.2 8.8 %copy-start.126 = (s32[4,1024]{1,0:T(4,128)S(1)}, s32[4,1024]{1,0:T(4,128)}, u32[]{:S(2)}) copy-start(s32[4,1024]{1,0:T(4,128)} %param.18) | copy-start | bytes 49156
  28.6 681.2 %reduce-scatter.5.cloned.1.call-start = ((), (), s32[]{:S(2)}) async-start(), calls=%async_computation.3 | async-start | bytes 3244032 | tf_op jit(solution)/shard_map/reduce_scatter | solution.py:480
  28.7 15.7 %collective-permute-start = (bf16[256,768]{1,0:T(8,128)(2,1)S(1)}, bf16[256,768]{1,0:T(8,128)(2,1)S(1)}, u32[]{:S(2)}, u32[]{:S(2)}) collective-permute-start(bf16[256,768]{1,0:T(8,128)(2,1)S(1)} %copy-done.72), channel_id=1, source_target_pairs={{1,0},{2,1},{5,4},{6,5},{9,8},{10,9},{13,12},{14,13},{17,16},{18,1... | collective-permute-start | bytes 1179656 | tf_op jit(solution)/shard_map/ppermute | solution.py:19
  30.0 14.7 %collective-permute-start.1 = (bf16[256,768]{1,0:T(8,128)(2,1)S(1)}, bf16[256,768]{1,0:T(8,128)(2,1)S(1)}, u32[]{:S(2)}, u32[]{:S(2)}) collective-permute-start(bf16[256,768]{1,0:T(8,128)(2,1)S(1)} %copy-done.72), channel_id=1, source_target_pairs={{3,1},{7,5},{11,9},{15,13},{19,17},{23,21},{27,25},{31,29}} | collective-permute-start | bytes 1179656 | tf_op jit(solution)/shard_map/ppermute | solution.py:19
  30.7 14.1 %collective-permute-start.2 = (bf16[768,1152]{1,0:T(8,128)(2,1)}, bf16[768,1152]{1,0:T(8,128)(2,1)}, u32[]{:S(2)}, u32[]{:S(2)}) collective-permute-start(bf16[768,1152]{1,0:T(8,128)(2,1)} %bitcast.160), channel_id=1, source_target_pairs={{0,1},{1,0},{2,3},{3,2},{4,5},{5,4},{6,7},{7,6},{8,9},{9,8},{10,11... | collective-permute-start | bytes 5308424 | tf_op jit(solution)/shard_map/ppermute | solution.py:19
  32.5 10.0 %collective-permute-start.3 = (f32[2,384]{1,0:T(2,128)}, f32[2,384]{1,0:T(2,128)S(1)}, u32[]{:S(2)}, u32[]{:S(2)}) collective-permute-start(f32[2,384]{1,0:T(2,128)} %bitcast.180), channel_id=1, source_target_pairs={{0,1},{1,0},{2,3},{3,2},{4,5},{5,4},{6,7},{7,6},{8,9},{9,8},{10,11... | collective-permute-start | bytes 9224 | tf_op jit(solution)/shard_map/ppermute | solution.py:19
  32.6 91.2 %collective-permute-start.4 = (bf16[384,768]{1,0:T(8,128)(2,1)}, bf16[384,768]{1,0:T(8,128)(2,1)}, u32[]{:S(2)}, u32[]{:S(2)}) collective-permute-start(bf16[384,768]{1,0:T(8,128)(2,1)} %bitcast.199), channel_id=1, source_target_pairs={{0,1},{1,0},{2,3},{3,2},{4,5},{5,4},{6,7},{7,6},{8,9},{9,8},{10,11... | collective-permute-start | bytes 1769480 | tf_op jit(solution)/shard_map/ppermute | solution.py:19
  33.8 57.4 %copy-start.133 = (s32[96]{0:T(128)}, s32[96]{0:T(128)S(1)}, u32[]{:S(2)}) copy-start(s32[96]{0:T(128)S(1)} %fusion.103) | copy-start | bytes 1156
  33.9 57.3 %copy-start.143 = (pred[512]{0:T(512)(128)(4,1)}, pred[512]{0:T(512)(128)(4,1)S(1)}, u32[]{:S(2)}) copy-start(pred[512]{0:T(512)(128)(4,1)S(1)} %fusion.97) | copy-start | bytes 1540
  36.8 68.3 %copy-start.20 = (bf16[768,384]{1,0:T(8,128)(2,1)}, bf16[768,384]{1,0:T(8,128)(2,1)S(1)}, u32[]{:S(2)}) copy-start(bf16[768,384]{1,0:T(8,128)(2,1)S(1)} %get-tuple-element.90) | copy-start | bytes 1769476
  41.8 85.2 %copy-start.83 = (f32[768]{0:T(1024)}, f32[768]{0:T(1024)S(1)}, u32[]{:S(2)}) copy-start(f32[768]{0:T(1024)S(1)} %get-tuple-element.68) | copy-start | bytes 9220
  42.4 1.2 collective-permute-start.6
  43.6 82.6 %collective-permute-start.5 = (bf16[768,1536]{1,0:T(8,128)(2,1)}, bf16[768,1536]{1,0:T(8,128)(2,1)}, u32[]{:S(2)}, u32[]{:S(2)}) collective-permute-start(bf16[768,1536]{1,0:T(8,128)(2,1)} %bitcast.194), channel_id=1, source_target_pairs={{0,1},{1,0},{2,3},{3,2},{4,5},{5,4},{6,7},{7,6},{8,9},{9,8},{10,11... | collective-permute-start | bytes 7077896 | tf_op jit(solution)/shard_map/ppermute | solution.py:19
  44.4 81.8 %collective-permute-start.7 = (bf16[1536,768]{1,0:T(8,128)(2,1)}, bf16[1536,768]{1,0:T(8,128)(2,1)}, u32[]{:S(2)}, u32[]{:S(2)}) collective-permute-start(bf16[1536,768]{1,0:T(8,128)(2,1)} %bitcast.189), channel_id=1, source_target_pairs={{0,1},{1,0},{2,3},{3,2},{4,5},{5,4},{6,7},{7,6},{8,9},{9,8},{10,11... | collective-permute-start | bytes 7077896 | tf_op jit(solution)/shard_map/ppermute | solution.py:19
  47.5 57.6 %copy-start.24 = (bf16[768,384]{1,0:T(8,128)(2,1)}, bf16[768,384]{1,0:T(8,128)(2,1)S(1)}, u32[]{:S(2)}) copy-start(bf16[768,384]{1,0:T(8,128)(2,1)S(1)} %get-tuple-element.93) | copy-start | bytes 1769476
  94.5 29.2 %copy-start.92 = (f32[512]{0:T(512)}, f32[512]{0:T(512)S(1)}, u32[]{:S(2)}) copy-start(f32[512]{0:T(512)S(1)} %add_rsqrt_fusion.4) | copy-start | bytes 6148
  137.7 22.9 %copy-start.93 = (f32[512]{0:T(512)S(1)}, f32[512]{0:T(512)}, u32[]{:S(2)}) copy-start(f32[512]{0:T(512)} %copy-done.92) | copy-start | bytes 6148
  138.9 21.7 %collective-permute-start.8 = (bf16[512,768]{1,0:T(8,128)(2,1)}, bf16[512,768]{1,0:T(8,128)(2,1)S(1)}, u32[]{:S(2)}, u32[]{:S(2)}) collective-permute-start(bf16[512,768]{1,0:T(8,128)(2,1)} %add_convert_fusion.3), channel_id=1, source_target_pairs={{0,2},{1,3},{4,6},{5,7},{8,10},{9,11},{12,14},{13,15},{16,18},{17,... | collective-permute-start | bytes 2359304 | tf_op jit(solution)/shard_map/ppermute | solution.py:19
  142.4 3.5 collective-permute-start.12
  143.1 59.7 %collective-permute-start.11 = (bf16[256,768]{1,0:T(8,128)(2,1)}, bf16[256,768]{1,0:T(8,128)(2,1)}, u32[]{:S(2)}, u32[]{:S(2)}) collective-permute-start(bf16[256,768]{1,0:T(8,128)(2,1)} %param.21), channel_id=1, source_target_pairs={{0,2},{2,3},{4,6},{6,7},{8,10},{10,11},{12,14},{14,15},{16,18},{18... | collective-permute-start | bytes 1179656 | tf_op jit(solution)/shard_map/ppermute | solution.py:19
  146.0 15.8 %copy-start.56 = (bf16[768,384]{1,0:T(8,128)(2,1)S(1)}, bf16[768,384]{1,0:T(8,128)(2,1)}, u32[]{:S(2)}) copy-start(bf16[768,384]{1,0:T(8,128)(2,1)} %get-tuple-element.88) | copy-start | bytes 1769476
  146.0 15.8 %copy-start.63 = (bf16[768,384]{1,0:T(8,128)(2,1)S(1)}, bf16[768,384]{1,0:T(8,128)(2,1)}, u32[]{:S(2)}) copy-start(bf16[768,384]{1,0:T(8,128)(2,1)} %get-tuple-element.91) | copy-start | bytes 1769476
  170.0 10.3 %copy-start.8 = (bf16[512,768]{0,1:T(8,128)(2,1)}, bf16[512,768]{0,1:T(8,128)(2,1)S(1)}, u32[]{:S(2)}) copy-start(bf16[512,768]{0,1:T(8,128)(2,1)S(1)} %copy.97) | copy-start | bytes 2359300
  227.9 15.8 %slice-start = ((s8[12582912]{0:T(1024)(128)(4,1)}), s8[4194304]{0:T(1024)(128)(4,1)S(1)}, s32[]{:S(2)}) async-start(s8[12582912]{0:T(1024)(128)(4,1)} %bitcast.138), calls=%async_computation.5 | async-start | bytes 8388608
  227.9 15.8 %slice-start.1 = ((s8[12582912]{0:T(1024)(128)(4,1)}), s8[4194304]{0:T(1024)(128)(4,1)S(1)}, s32[]{:S(2)}) async-start(s8[12582912]{0:T(1024)(128)(4,1)} %bitcast.138), calls=%async_computation.6 | async-start | bytes 8388608
  234.8 8.9 %slice-start.2 = ((s8[12582912]{0:T(1024)(128)(4,1)}), s8[4194304]{0:T(1024)(128)(4,1)S(1)}, s32[]{:S(2)}) async-start(s8[12582912]{0:T(1024)(128)(4,1)} %bitcast.138), calls=%async_computation.7 | async-start | bytes 8388608
  255.1 34.3 %slice-start.8 = ((s8[6291456]{0:T(1024)(128)(4,1)}), s8[4194304]{0:T(1024)(128)(4,1)S(1)}, s32[]{:S(2)}) async-start(s8[6291456]{0:T(1024)(128)(4,1)} %bitcast.205), calls=%async_computation.13 | async-start | bytes 8388608
  256.8 26.3 %copy-start.3 = (f32[512,768]{1,0:T(8,128)S(1)}, f32[512,768]{1,0:T(8,128)}, u32[]{:S(2)}) copy-start(f32[512,768]{1,0:T(8,128)} %copy-done.2) | copy-start | bytes 4718596
  256.8 26.2 %copy-start.88 = (f32[512]{0:T(512)S(1)}, f32[512]{0:T(512)}, u32[]{:S(2)}) copy-start(f32[512]{0:T(512)} %copy-done.87) | copy-start | bytes 6148
  256.8 26.2 %copy-start.98 = (f32[512]{0:T(512)S(1)}, f32[512]{0:T(512)}, u32[]{:S(2)}) copy-start(f32[512]{0:T(512)} %copy-done.97) | copy-start | bytes 6148
  256.8 32.6 %slice-start.9 = ((s8[6291456]{0:T(1024)(128)(4,1)}), s8[2097152]{0:T(1024)(128)(4,1)S(1)}, s32[]{:S(2)}) async-start(s8[6291456]{0:T(1024)(128)(4,1)} %bitcast.205), calls=%async_computation.14 | async-start | bytes 4194304
  258.2 27.3 %copy-start.96 = (f32[768]{0:T(1024)S(1)}, f32[768]{0:T(1024)}, u32[]{:S(2)}) copy-start(f32[768]{0:T(1024)} %get-tuple-element.67) | copy-start | bytes 9220
  258.2 24.9 %collective-permute-start.13 = (bf16[512,768]{1,0:T(8,128)(2,1)S(1)}, bf16[512,768]{1,0:T(8,128)(2,1)S(1)}, u32[]{:S(2)}, u32[]{:S(2)}) collective-permute-start(bf16[512,768]{1,0:T(8,128)(2,1)S(1)} %add_convert_fusion), channel_id=1, source_target_pairs={{2,0},{3,1},{6,4},{7,5},{10,8},{11,9},{14,12},{15,13},{18,16},{19,... | collective-permute-start | bytes 2359304 | tf_op jit(solution)/shard_map/ppermute | solution.py:19
  289.4 7.9 %copy-start.85 = (f32[768]{0:T(1024)S(1)}, f32[768]{0:T(1024)}, u32[]{:S(2)}) copy-start(f32[768]{0:T(1024)} %copy-done.83) | copy-start | bytes 9220
  289.4 7.9 %copy-start.149 = (bf16[1,768,1536]{2,1,0:T(8,128)(2,1)S(1)}, bf16[1,768,1536]{2,1,0:T(8,128)(2,1)}, u32[]{:S(2)}) copy-start(bf16[1,768,1536]{2,1,0:T(8,128)(2,1)} %param.29) | copy-start | bytes 7077892
  311.4 16.3 %slice-start.3 = ((s8[12582912]{0:T(1024)(128)(4,1)}), s8[4194304]{0:T(1024)(128)(4,1)S(1)}, s32[]{:S(2)}) async-start(s8[12582912]{0:T(1024)(128)(4,1)} %bitcast.140), calls=%async_computation.8 | async-start | bytes 8388608
  311.4 16.3 %slice-start.4 = ((s8[12582912]{0:T(1024)(128)(4,1)}), s8[4194304]{0:T(1024)(128)(4,1)S(1)}, s32[]{:S(2)}) async-start(s8[12582912]{0:T(1024)(128)(4,1)} %bitcast.140), calls=%async_computation.9 | async-start | bytes 8388608
  318.5 22.1 %copy-start.28 = (bf16[12,64,512]{2,1,0:T(8,128)(2,1)}, bf16[12,64,512]{2,1,0:T(8,128)(2,1)S(1)}, u32[]{:S(2)}) copy-start(bf16[12,64,512]{2,1,0:T(8,128)(2,1)S(1)} %convolution_convert_fusion.6) | copy-start | bytes 2359300
  318.5 9.2 %slice-start.5 = ((s8[12582912]{0:T(1024)(128)(4,1)}), s8[4194304]{0:T(1024)(128)(4,1)S(1)}, s32[]{:S(2)}) async-start(s8[12582912]{0:T(1024)(128)(4,1)} %bitcast.140), calls=%async_computation.10 | async-start | bytes 8388608
  350.6 360.8 %all-gather.4.cloned.1.call-start = ((), (), s32[]{:S(2)}) async-start(), calls=%async_computation.4 | async-start | bytes 2433024 | tf_op jit(solution)/shard_map/all_gather | solution.py:490
  393.7 57.1 %collective-permute-start.20 = (bf16[512,1536]{1,0:T(8,128)(2,1)}, bf16[512,1536]{1,0:T(8,128)(2,1)}, u32[]{:S(2)}, u32[]{:S(2)}) collective-permute-start(bf16[512,1536]{1,0:T(8,128)(2,1)} %get-tuple-element.87), channel_id=1, source_target_pairs={{0,1},{1,0},{2,3},{3,2},{4,5},{5,4},{6,7},{7,6},{8,9},{9,8},{10,11... | collective-permute-start | bytes 4718600 | tf_op jit(solution)/shard_map/ppermute | solution.py:19
  397.5 31.7 %collective-permute-start.23 = (bf16[512,384]{1,0:T(8,128)(2,1)}, bf16[512,384]{1,0:T(8,128)(2,1)}, u32[]{:S(2)}, u32[]{:S(2)}) collective-permute-start(bf16[512,384]{1,0:T(8,128)(2,1)} %copy.136), channel_id=1, source_target_pairs={{0,1},{1,0},{2,3},{3,2},{4,5},{5,4},{6,7},{7,6},{8,9},{9,8},{10,11... | collective-permute-start | bytes 1179656 | tf_op jit(solution)/shard_map/ppermute | solution.py:19
  400.2 23.9 %collective-permute-start.21 = (bf16[512,384]{1,0:T(8,128)(2,1)}, bf16[512,384]{1,0:T(8,128)(2,1)}, u32[]{:S(2)}, u32[]{:S(2)}) collective-permute-start(bf16[512,384]{1,0:T(8,128)(2,1)} %copy.132), channel_id=1, source_target_pairs={{0,1},{1,0},{2,3},{3,2},{4,5},{5,4},{6,7},{7,6},{8,9},{9,8},{10,11... | collective-permute-start | bytes 1179656 | tf_op jit(solution)/shard_map/ppermute | solution.py:19
  401.8 12.1 %copy-start.16 = (f32[512,768]{1,0:T(8,128)S(1)}, f32[512,768]{1,0:T(8,128)}, u32[]{:S(2)}) copy-start(f32[512,768]{1,0:T(8,128)} %get-tuple-element.78) | copy-start | bytes 4718596
  405.9 25.8 %collective-permute-start.22 = (bf16[512,384]{1,0:T(8,128)(2,1)}, bf16[512,384]{1,0:T(8,128)(2,1)}, u32[]{:S(2)}, u32[]{:S(2)}) collective-permute-start(bf16[512,384]{1,0:T(8,128)(2,1)} %copy.134), channel_id=1, source_target_pairs={{0,1},{1,0},{2,3},{3,2},{4,5},{5,4},{6,7},{7,6},{8,9},{9,8},{10,11... | collective-permute-start | bytes 1179656 | tf_op jit(solution)/shard_map/ppermute | solution.py:19
  409.2 12.0 %collective-permute-start.16 = (bf16[48,768]{1,0:T(8,128)(2,1)}, bf16[48,768]{1,0:T(8,128)(2,1)}, u32[]{:S(2)}, u32[]{:S(2)}) collective-permute-start(bf16[48,768]{1,0:T(8,128)(2,1)} %slice.274), channel_id=1, source_target_pairs={{0,2},{1,3},{4,6},{5,7},{8,10},{9,11},{12,14},{13,15},{16,18},{17,... | collective-permute-start | bytes 221192 | tf_op jit(solution)/shard_map/ppermute | solution.py:19
  421.2 14.6 %collective-permute-start.14 = (bf16[256,768]{1,0:T(8,128)(2,1)}, bf16[256,768]{1,0:T(8,128)(2,1)}, u32[]{:S(2)}, u32[]{:S(2)}) collective-permute-start(bf16[256,768]{1,0:T(8,128)(2,1)} %get-tuple-element.96), channel_id=1, source_target_pairs={{1,2},{5,6},{9,10},{13,14},{17,18},{21,22},{25,26},{29,30}} | collective-permute-start | bytes 1179656 | tf_op jit(solution)/shard_map/ppermute | solution.py:19
  424.2 7.6 %copy-start.38 = (bf16[512,768]{1,0:T(8,128)(2,1)S(1)}, bf16[512,768]{1,0:T(8,128)(2,1)}, u32[]{:S(2)}) copy-start(bf16[512,768]{1,0:T(8,128)(2,1)} %copy-done.37) | copy-start | bytes 2359300
  424.2 7.6 %copy-start.43 = (bf16[512,384]{1,0:T(8,128)(2,1)S(1)}, bf16[512,384]{1,0:T(8,128)(2,1)}, u32[]{:S(2)}) copy-start(bf16[512,384]{1,0:T(8,128)(2,1)} %copy.133) | copy-start | bytes 1179652
  424.2 11.9 %collective-permute-start.15 = (bf16[256,768]{1,0:T(8,128)(2,1)}, bf16[256,768]{1,0:T(8,128)(2,1)S(1)}, u32[]{:S(2)}, u32[]{:S(2)}) collective-permute-start(bf16[256,768]{1,0:T(8,128)(2,1)} %get-tuple-element.95), channel_id=1, source_target_pairs={{0,1},{1,3},{4,5},{5,7},{8,9},{9,11},{12,13},{13,15},{16,17},{17,1... | collective-permute-start | bytes 1179656 | tf_op jit(solution)/shard_map/ppermute | solution.py:19
  429.2 9.7 %collective-permute-start.10 = (bf16[256,768]{1,0:T(8,128)(2,1)S(1)}, bf16[256,768]{1,0:T(8,128)(2,1)S(1)}, u32[]{:S(2)}, u32[]{:S(2)}) collective-permute-start(bf16[256,768]{1,0:T(8,128)(2,1)S(1)} %copy-done.75), channel_id=1, source_target_pairs={{2,0},{3,2},{6,4},{7,6},{10,8},{11,10},{14,12},{15,14},{18,16},{19... | collective-permute-start | bytes 1179656 | tf_op jit(solution)/shard_map/ppermute | solution.py:19
  430.5 8.4 %copy-start.74 = (bf16[256,768]{1,0:T(8,128)(2,1)S(1)}, bf16[256,768]{1,0:T(8,128)(2,1)}, u32[]{:S(2)}) copy-start(bf16[256,768]{1,0:T(8,128)(2,1)} %get-tuple-element.98) | copy-start | bytes 1179652
  431.7 9.1 %copy-start.17 = (f32[512,768]{1,0:T(8,128)S(1)}, f32[512,768]{1,0:T(8,128)}, u32[]{:S(2)}) copy-start(f32[512,768]{1,0:T(8,128)} %get-tuple-element.78) | copy-start | bytes 4718596
  431.7 15.4 %collective-permute-start.24 = (bf16[512,768]{1,0:T(8,128)(2,1)S(1)}, bf16[512,768]{1,0:T(8,128)(2,1)S(1)}, u32[]{:S(2)}, u32[]{:S(2)}) collective-permute-start(bf16[512,768]{1,0:T(8,128)(2,1)S(1)} %copy-done.38), channel_id=1, source_target_pairs={{0,1},{1,0},{2,3},{3,2},{4,5},{5,4},{6,7},{7,6},{8,9},{9,8},{10,11... | collective-permute-start | bytes 2359304 | tf_op jit(solution)/shard_map/ppermute | solution.py:19
  434.3 7.5 %copy-start.71 = (bf16[512,384]{1,0:T(8,128)(2,1)S(1)}, bf16[512,384]{1,0:T(8,128)(2,1)}, u32[]{:S(2)}) copy-start(bf16[512,384]{1,0:T(8,128)(2,1)} %copy.130) | copy-start | bytes 1179652
  434.3 11.9 %copy-start.15 = (f32[512,768]{1,0:T(8,128)S(1)}, f32[512,768]{1,0:T(8,128)}, u32[]{:S(2)}) copy-start(f32[512,768]{1,0:T(8,128)} %get-tuple-element.94) | copy-start | bytes 4718596
  435.7 12.2 %collective-permute-start.19 = (bf16[512,768]{1,0:T(8,128)(2,1)S(1)}, bf16[512,768]{1,0:T(8,128)(2,1)S(1)}, u32[]{:S(2)}, u32[]{:S(2)}) collective-permute-start(bf16[512,768]{1,0:T(8,128)(2,1)S(1)} %copy-done.35), channel_id=1, source_target_pairs={{0,1},{1,0},{2,3},{3,2},{4,5},{5,4},{6,7},{7,6},{8,9},{9,8},{10,11... | collective-permute-start | bytes 2359304 | tf_op jit(solution)/shard_map/ppermute | solution.py:19
  436.1 11.8 %collective-permute-start.17 = (bf16[512,768]{1,0:T(8,128)(2,1)S(1)}, bf16[512,768]{1,0:T(8,128)(2,1)S(1)}, u32[]{:S(2)}, u32[]{:S(2)}) collective-permute-start(bf16[512,768]{1,0:T(8,128)(2,1)S(1)} %copy-done.33), channel_id=1, source_target_pairs={{0,1},{1,0},{2,3},{3,2},{4,5},{5,4},{6,7},{7,6},{8,9},{9,8},{10,11... | collective-permute-start | bytes 2359304 | tf_op jit(solution)/shard_map/ppermute | solution.py:19
  438.8 3.0 collective-permute-start.9
  441.8 5.7 collective-permute-start.18
  447.1 41.6 %collective-permute-start.25 = (bf16[512,1536]{1,0:T(8,128)(2,1)S(1)}, bf16[512,1536]{1,0:T(8,128)(2,1)S(1)}, u32[]{:S(2)}, u32[]{:S(2)}) collective-permute-start(bf16[512,1536]{1,0:T(8,128)(2,1)S(1)} %copy-done.44), channel_id=1, source_target_pairs={{0,1},{1,0},{2,3},{3,2},{4,5},{5,4},{6,7},{7,6},{8,9},{9,8},{10,11... | collective-permute-start | bytes 4718600 | tf_op jit(solution)/shard_map/ppermute | solution.py:19
  447.5 53.7 %collective-permute-start.26 = (bf16[512,768]{1,0:T(8,128)(2,1)}, bf16[512,768]{1,0:T(8,128)(2,1)}, u32[]{:S(2)}, u32[]{:S(2)}) collective-permute-start(bf16[512,768]{1,0:T(8,128)(2,1)} %get-tuple-element.77), channel_id=1, source_target_pairs={{0,1},{1,0},{2,3},{3,2},{4,5},{5,4},{6,7},{7,6},{8,9},{9,8},{10,11... | collective-permute-start | bytes 2359304 | tf_op jit(solution)/shard_map/ppermute | solution.py:19
  (129 other events, 384.8 us)
Sparse Core Ops, SparseCore 0:
  28.7 62.3 reduce-scatter.2
  350.7 99.6 reduce-scatter.4
  453.4 56.1 all-gather.3

commit v2 on v1

v2 whole, which is shorter than its diff:
```python
import functools

import jax
import jax.numpy as jnp
from jax import lax
from jax.experimental import pallas as pl
from jax.experimental.pallas import tpu as pltpu
from jax.sharding import PartitionSpec as P

HEAD_DIM = 64
EPS = 1e-12
ROOT_HALF = 0.7071067811865476
INV_ROOT_TWO_PI = 0.3989422804014327
BF = jnp.bfloat16
F32 = jnp.float32


def routed(block, route):
    return lax.ppermute(block, "section", route)


SWAP = [(0, 1), (1, 0), (2, 3), (3, 2)]


def swapped(block):
    return routed(block, SWAP)


def normalize(values, gain, shift):
    center = values - jnp.mean(values, -1, keepdims=True)
    spread = jnp.mean(center * center, -1, keepdims=True)
    inverse = lax.rsqrt(spread + EPS)
    normed = center * inverse
    return (normed * gain + shift, normed, inverse)


def normalize_back(grad, normed, inverse, gain):
    scaled = grad * gain
    centered = (
        scaled
        - jnp.mean(scaled, -1, keepdims=True)
        - normed * jnp.mean(scaled * normed, -1, keepdims=True)
    )
    return (inverse * centered, jnp.sum(grad * normed, 0), jnp.sum(grad, 0))


def matmul(left, right):
    return jnp.dot(left, right, preferred_element_type=F32)


def matmul_left_t(left, right):
    return jnp.einsum("pa,pb->ab", left, right, preferred_element_type=F32)


GROUP = 8
BLOCK = 128
HOP = 4
DEPTH = 3
EXTRA = 20


def tree_of(k):
    turn = k % 8
    return turn < 4, 1 + turn % 2, (turn // 2) % 2


def rooted_at(c):
    return (c // 2) % 2 == 0, c // 2, c % 2


def loop(low, high, body):
    def step(k, carry):
        body(k)
        return carry

    lax.fori_loop(low, high, step, 0)


def reduce_kernel(
    counts, a_ref, b_ref, small_ref, edge_ref, box_ref, listed_ref,
    q_ref, o_ref, u_ref, d_ref, gathered_ref, rows_ref, table_ref,
    buf, total, gathered, edge, rows, table, piece,
    send, recv, out_sem, g_send, g_recv, e_send, e_recv, r_send, r_recv, t_send, t_recv,
    f_send, f_recv, last_sem,
):
    me = lax.axis_index("dp")
    section = lax.axis_index("section")
    n_sections = lax.axis_size("section")
    layer = section // 2
    half = section % 2
    other_core = section + 1 - 2 * half
    other_layer = (section + 2) % n_sections
    place = me % GROUP
    z = place // 2
    y = place % 2
    chunks = buf.shape[1]
    side = buf.shape[3]
    slots = rows.shape[2]
    n_q, n_o, n_u, n_d = counts
    ends = (n_d[0] * n_d[1],)
    ends += (ends[0] + n_u[0] * n_u[1],)
    ends += (ends[1] + n_o[0] * n_o[1],)
    mesh_id = pl.DeviceIdType.MESH
    deltas = (-2, 2, 1 - 2 * y)
    exists = (z > 0, z < GROUP // 2 - 1, y >= 0)

    barrier = pltpu.get_barrier_semaphore()
    for d in range(3):

        @pl.when(exists[d])
        def _():
            pl.semaphore_signal(
                barrier, inc=1, device_id=(me + deltas[d], section), device_id_type=mesh_id
            )

    for step in range(1, n_sections):
        pl.semaphore_signal(
            barrier, inc=1, device_id=(me, (section + step) % n_sections), device_id_type=mesh_id
        )
    pl.semaphore_wait(
        barrier,
        n_sections + jnp.where(exists[0], 1, 0) + jnp.where(exists[1], 1, 0),
    )

    def remote(source, target, sent, got, device):
        return pltpu.make_async_remote_copy(
            src_ref=source, dst_ref=target, send_sem=sent, recv_sem=got, device_id=device,
            device_id_type=mesh_id,
        )

    def edge_across():
        return remote(
            edge_ref.at[1], edge.at[0], e_send.at[0], e_recv.at[0], (me, other_layer)
        )

    def edge_beside(source):
        return remote(source, edge.at[1], e_send.at[1], e_recv.at[1], (me, other_core))

    @pl.when(layer == 0)
    def _():
        edge_across().start()
        edge_beside(edge_ref.at[0]).start()
        edge[0] = edge_ref[0]

    def roles(tree):
        comb, root_z, root_y = tree
        along = jnp.logical_or(jnp.logical_not(comb), y == root_y)
        across = jnp.logical_or(comb, z == root_z)
        child = (
            exists[0] & along & (z <= root_z),
            exists[1] & along & (z >= root_z),
            across & (y == root_y),
        )
        up_z = along & (z != root_z)
        up_y = across & (y != root_y)
        parent = jnp.where(up_z, jnp.where(z < root_z, 1, 0), jnp.where(up_y, 2, 3))
        depth = jnp.abs(z - root_z) + jnp.abs(y - root_y)
        return child, parent, depth

    def neighbour(d):
        return me + jnp.where(d == 0, deltas[0], jnp.where(d == 1, deltas[1], deltas[2]))

    def facing(d):
        return jnp.where(d == 2, 2, 1 - d)

    def transfer(k, d, source):
        there = facing(d)
        return remote(
            buf.at[source, k], buf.at[there, k], send.at[d, k], recv.at[there, k],
            (neighbour(d), section),
        )

    def arrived(k, d):
        remote(
            buf.at[3, k], buf.at[d, k], send.at[0, k], recv.at[d, k], (me, other_core)
        ).wait_recv()

    def put(k, source):
        kk = k - 1
        low = 0
        for target, count, high in (
            (d_ref, n_d, ends[0]), (u_ref, n_u, ends[1]), (o_ref, n_o, ends[2]),
            (q_ref, n_q, chunks - 1),
        ):

            @pl.when((kk >= low) & (kk < high))
            def _():
                at = kk - low
                pltpu.make_async_copy(
                    buf.at[source, k],
                    target.at[
                        pl.ds(pl.multiple_of(at // count[1] * BLOCK, BLOCK), BLOCK),
                        pl.ds(pl.multiple_of(at % count[1] * side, BLOCK), side),
                    ],
                    out_sem.at[k],
                ).start()

            low = high

    def product(k):
        kd = k - 1
        in_d = kd < ends[0]
        ku = kd - ends[0]
        in_u = kd < ends[1]
        ko = kd - ends[1]
        in_o = kd < ends[2]
        kq = kd - ends[2]
        a_at = jnp.where(
            in_d,
            n_q[0] + n_o[0] + n_u[0] + kd // n_d[1],
            jnp.where(
                in_u,
                n_q[0] + n_o[0] + ku // n_u[1],
                jnp.where(in_o, n_q[0] + ko // n_o[1], kq // n_q[1]),
            ),
        )
        b_at = jnp.where(
            in_d,
            n_q[1] + n_o[1] + n_u[1] + kd % n_d[1],
            jnp.where(
                in_u,
                n_q[1] + n_o[1] + ku % n_u[1],
                jnp.where(in_o, n_q[1] + ko % n_o[1], kq % n_q[1]),
            ),
        )
        left = a_ref[:, pl.ds(pl.multiple_of(a_at * BLOCK, BLOCK), BLOCK)]
        right = b_ref[:, pl.ds(pl.multiple_of(b_at * side, BLOCK), side)]
        total[...] = lax.dot_general(
            left, right, (((0,), (0,)), ((), ())), preferred_element_type=F32
        )

    def climb(k, level):
        child, parent, depth = roles(tree_of(k))

        @pl.when((k >= 0) & (k < chunks) & (depth == DEPTH - level))
        def _():
            @pl.when(k == 0)
            def _():
                total[...] = small_ref[...]

            @pl.when(k > 0)
            def _():
                product(k)

            if level > 0:
                for d in range(3):

                    @pl.when(child[d])
                    def _():
                        arrived(k, d)
                        total[...] += buf[d, k].astype(F32)

            buf[3, k] = total[...].astype(BF)
            if level < DEPTH:
                transfer(k, parent, 3).start()
            else:
                for d in range(3):

                    @pl.when(child[d])
                    def _():
                        transfer(k, d, 3).start()

                put(k, 3)

    def descend(k, level):
        child, parent, depth = roles(tree_of(k))

        @pl.when((k >= 0) & (k < chunks) & (depth == level))
        def _():
            arrived(k, parent)
            for d in range(3):

                @pl.when(child[d])
                def _():
                    transfer(k, d, parent).start()

            put(k, parent)

    def settle(k):
        child, parent, depth = roles(tree_of(k))
        for d in range(3):

            @pl.when(child[d] | (parent == d))
            def _():
                transfer(k, d, 3).wait_send()

        @pl.when(k > 0)
        def _():
            pltpu.make_async_copy(
                buf.at[3, k], d_ref.at[pl.ds(0, BLOCK), pl.ds(0, side)], out_sem.at[k]
            ).wait()

    def advance(t):
        for level in range(DEPTH + 1):
            climb(t - level * HOP, level)
        for level in range(1, DEPTH + 1):
            descend(t - (DEPTH + level) * HOP, level)

    def slots_down(c, d):
        return remote(
            rows.at[0, c], rows.at[0, c], r_send.at[d, c], r_recv.at[0, c],
            (neighbour(d), section),
        )

    def slots_across(c):
        return remote(
            rows.at[0, c], rows.at[1, c], r_send.at[3, c], r_recv.at[1, c], (me, other_layer)
        )

    def slots_beside(c, kind):
        return remote(
            rows.at[kind, c], rows.at[2 + kind, c], r_send.at[4 + kind, c],
            r_recv.at[2 + kind, c], (me, other_core),
        )

    def slots_got(c, kind):
        remote(
            rows.at[kind, c], rows.at[kind, c], r_send.at[0, c], r_recv.at[kind, c],
            (me, other_core),
        ).wait_recv()

    def share_slots(c, level):
        child, parent, depth = roles(rooted_at(c))

        @pl.when((c >= 0) & (c < GROUP) & (depth == level))
        def _():
            if level > 0:
                slots_got(c, 0)
            for d in range(3):

                @pl.when(child[d])
                def _():
                    slots_down(c, d).start()

            slots_across(c).start()
            slots_beside(c, 0).start()

    def relay_slots(c):
        @pl.when((c >= 0) & (c < GROUP))
        def _():
            slots_got(c, 1)
            slots_beside(c, 1).start()

    def table_up(c, d):
        there = facing(d)
        return remote(
            piece.at[3, c], piece.at[there, c], t_send.at[d, c], t_recv.at[there, c],
            (neighbour(d), section),
        )

    def table_out(c, step):
        to = (section + step) % n_sections
        return remote(
            piece.at[3, c, pl.ds(to * table.shape[1], table.shape[1])], table.at[section],
            f_send.at[step], f_recv.at[section], (me, to),
        )

    def table_climb(c, level):
        child, parent, depth = roles(rooted_at(c))

        @pl.when((c >= 0) & (c < GROUP) & (depth == DEPTH + 1 - level))
        def _():
            at = c * BLOCK + lax.broadcasted_iota(jnp.int32, (BLOCK, edge.shape[1]), 0)
            for part in range(2):
                spots = box_ref[part]
                ones = (at == spots[0:1]).astype(F32) + (at == spots[1:2]).astype(F32)
                term = jnp.dot(ones.astype(BF), edge[part], preferred_element_type=F32)
                if part == 0:
                    total[...] = term
                else:
                    total[...] += term
            if level > 0:
                for d in range(3):

                    @pl.when(child[d])
                    def _():
                        remote(
                            piece.at[3, c], piece.at[d, c], t_send.at[0, c], t_recv.at[d, c],
                            (me, other_core),
                        ).wait_recv()
                        total[...] += piece[d, c].astype(F32)

            piece[3, c] = total[...].astype(BF)
            if level < DEPTH + 1:
                table_up(c, parent).start()
            else:
                for step in range(1, n_sections):
                    table_out(c, step).start()
                kept = table.shape[1]
                table[section] = piece[3, c, pl.ds(pl.multiple_of(section * kept, kept), kept)]

    def extras(t):
        c = t - EXTRA
        for level in range(DEPTH + 2):
            share_slots(c - level * HOP, level)
        relay_slots(c - (DEPTH + 3) * HOP)
        for level in range(DEPTH + 2):
            table_climb(c - GROUP - level * HOP, level)

    def settle_extras(c):
        child, parent, depth = roles(rooted_at(c))
        for d in range(3):

            @pl.when(child[d])
            def _():
                slots_down(c, d).wait_send()

            @pl.when(parent == d)
            def _():
                table_up(c, d).wait_send()

        slots_across(c).wait_send()
        for kind in range(2):
            slots_beside(c, kind).wait_send()
            slots_got(c, 2 + kind)

    def handed(step):
        return remote(
            gathered.at[0], gathered.at[step], g_send.at[step], g_recv.at[step],
            (me, (section + n_sections - step) % n_sections),
        )

    loop(0, EXTRA, advance)

    @pl.when(layer == 1)
    def _():
        edge_across().wait_recv()
        edge_beside(edge.at[0]).start()

    edge_beside(edge.at[0]).wait_recv()
    wanted = listed_ref[...] == lax.broadcasted_iota(jnp.int32, (slots, edge.shape[1]), 1)
    rows[0, place] = jnp.dot(
        wanted.astype(F32).astype(BF), edge[0], preferred_element_type=F32
    ).astype(BF)

    def both(t):
        advance(t)
        extras(t)

    middle = EXTRA + 2 * GROUP + (DEPTH + 3) * HOP
    loop(EXTRA, middle, both)
    mine = roles(tree_of(0))[1]
    kept_small = gathered.shape[1]
    gathered[0] = buf[mine, 0, :kept_small]
    for step in range(1, n_sections):
        handed(step).start()
    loop(middle, chunks + 2 * DEPTH * HOP, advance)
    loop(0, GROUP, settle_extras)
    for step in range(1, n_sections):
        handed(step).wait()
        table_out(place, step).wait_send()
        source = (section + n_sections - step) % n_sections
        remote(
            piece.at[3, 0, pl.ds(0, table.shape[1])], table.at[source], f_send.at[0],
            f_recv.at[source], (me, other_core),
        ).wait_recv()
    outs = (
        pltpu.make_async_copy(gathered, gathered_ref, last_sem.at[0]),
        pltpu.make_async_copy(rows, rows_ref, last_sem.at[1]),
        pltpu.make_async_copy(table, table_ref, last_sem.at[2]),
    )
    for copy in outs:
        copy.start()

    @pl.when(layer == 0)
    def _():
        edge_across().wait_send()

    edge_beside(edge.at[0]).wait_send()
    loop(0, chunks, settle)
    for copy in outs:
        copy.wait()


def reduced(a, b, small, edge, boxes, listed, counts, side):
    chunks = 1 + sum(count[0] * count[1] for count in counts)
    n_sections = lax.axis_size("section")
    kept = 32
    slots = listed.shape[0]
    page = edge.shape[1]
    any_space = pl.BlockSpec(memory_space=pl.ANY)
    in_vmem = pl.BlockSpec(memory_space=pltpu.VMEM)
    flops = 2 * a.shape[0] * BLOCK * side * chunks
    dma = pltpu.SemaphoreType.DMA
    return pl.pallas_call(
        functools.partial(reduce_kernel, counts),
        out_shape=tuple(
            jax.ShapeDtypeStruct((count[0] * BLOCK, count[1] * side), BF) for count in counts
        )
        + (
            jax.ShapeDtypeStruct((n_sections, kept, side), BF),
            jax.ShapeDtypeStruct((4, GROUP, slots, side), BF),
            jax.ShapeDtypeStruct((n_sections, BLOCK // n_sections, side), BF),
        ),
        in_specs=[in_vmem] * 6,
        out_specs=(any_space,) * 7,
        scratch_shapes=[
            pltpu.VMEM((4, chunks, BLOCK, side), BF),
            pltpu.VMEM((BLOCK, side), F32),
            pltpu.VMEM((n_sections, kept, side), BF),
            pltpu.VMEM((2, page, side), BF),
            pltpu.VMEM((4, GROUP, slots, side), BF),
            pltpu.VMEM((n_sections, BLOCK // n_sections, side), BF),
            pltpu.VMEM((4, GROUP, BLOCK, side), BF),
            dma((3, chunks)), dma((3, chunks)), dma((chunks,)),
            dma((n_sections,)), dma((n_sections,)),
            dma((2,)), dma((2,)),
            dma((6, GROUP)), dma((4, GROUP)),
            dma((3, GROUP)), dma((3, GROUP)),
            dma((n_sections,)), dma((n_sections,)),
            dma((3,)),
        ],
        compiler_params=pltpu.CompilerParams(
            collective_id=0, has_side_effects=True, vmem_limit_bytes=60 << 20
        ),
        cost_estimate=pl.CostEstimate(
            flops=flops, bytes_accessed=400 << 20, transcendentals=0
        ),
        name="gradient_sums",
    )(a, b, small, edge, boxes, listed)


ROWS = 256


def layer_kernel(
    x_ref, given_ref, q_own, o_own, u_own, d_own, qvb_ref, upb_ref, gains_ref, shifts_ref,
    a_ref, b_ref, y_ref, dx_ref, sums_ref, qvb_sum, upb_sum,
    wq, wo, wu, wd, wide, x_land, g_land, x_low, ctx, d_ctx, h_low, act, slope, qkv, d_qkv,
    da_low, df_low, probs, n_one, n_two, r_one, r_two, z, sent_low,
    w_local, w_send, w_recv, x_send, x_recv, g_send, g_recv, p_local, p_send, p_recv, io_sem,
):
    me = lax.axis_index("dp")
    section = lax.axis_index("section")
    n_sections = lax.axis_size("section")
    layer = section // 2
    half = section % 2
    beside = (me, section + 1 - 2 * half)
    across = (me, (section + 2) % n_sections)
    mesh_id = pl.DeviceIdType.MESH
    page, width = x_low.shape
    side = ctx.shape[2]
    units = act.shape[2]
    blocks = page // ROWS
    tile = 512
    scale = HEAD_DIM ** (-0.5)

    barrier = pltpu.get_barrier_semaphore()
    for device in (beside, across):
        pl.semaphore_signal(barrier, inc=1, device_id=device, device_id_type=mesh_id)
    pl.semaphore_wait(barrier, 2)

    def remote(source, target, sent, got, device):
        return pltpu.make_async_remote_copy(
            src_ref=source, dst_ref=target, send_sem=sent, recv_sem=got, device_id=device,
            device_id_type=mesh_id,
        )

    def weight_copies(i):
        source = (q_own, o_own, u_own, d_own)[i].at[0]
        target = (wq, wo, wu, wd)[i]
        return (
            pltpu.make_async_copy(source, target.at[0], w_local.at[i]),
            remote(source, target.at[1], w_send.at[i], w_recv.at[i], beside),
        )

    def weights_here(i):
        near, far = weight_copies(i)
        near.wait()
        far.wait_recv()

    x_copy = pltpu.make_async_copy(x_ref, wide, io_sem.at[0])
    given_copy = pltpu.make_async_copy(given_ref, g_land, io_sem.at[1])

    @pl.when(layer == 0)
    def _():
        x_copy.start()

    @pl.when(layer == 1)
    def _():
        given_copy.start()

    for i in range(4):
        near, far = weight_copies(i)
        far.start()
        near.start()

    def rows_of(block):
        return pl.ds(pl.multiple_of(block * ROWS, ROWS), ROWS)

    def x_move(block):
        rows = rows_of(block)
        return remote(
            sent_low.at[rows], x_land.at[rows], x_send.at[block], x_recv.at[block], across
        )

    def g_move(block):
        rows = rows_of(block)
        return remote(
            sent_low.at[rows], g_land.at[rows], g_send.at[block], g_recv.at[block], across
        )

    spans = (
        (a_ref, 0, width), (a_ref, width, side), (a_ref, width + side, width),
        (a_ref, 2 * width + side, units),
        (b_ref, 0, 3 * side), (b_ref, 3 * side, width), (b_ref, 3 * side + width, units),
        (b_ref, 3 * side + width + units, width),
    )

    def piece_copies(i):
        target, start, size = spans[i]
        source = (x_low, ctx, h_low, act, d_qkv, da_low, slope, df_low)[i]
        double = i in (1, 3, 4, 6)
        columns = pl.ds(start, size)
        return (
            pltpu.make_async_copy(
                source.at[0] if double else source, target.at[0, :, columns], p_local.at[i]
            ),
            remote(
                source.at[1] if double else source, target.at[1, :, columns], p_send.at[i],
                p_recv.at[i], beside,
            ),
        )

    def hand_out(*pieces):
        for i in pieces:
            near, far = piece_copies(i)
            far.start()
            near.start()

    def nt(left, right):
        return lax.dot_general(
            left, right, (((1,), (1,)), ((), ())), preferred_element_type=F32
        )

    def tn(left, right):
        return lax.dot_general(
            left, right, (((0,), (0,)), ((), ())), preferred_element_type=F32
        )

    def centred(values):
        center = values - jnp.mean(values, -1, keepdims=True)
        spread = jnp.mean(center * center, -1, keepdims=True)
        inverse = lax.rsqrt(spread + EPS)
        return center * inverse, inverse

    def pulled(grad, normed, inverse, gain):
        scaled = grad * gain
        return inverse * (
            scaled
            - jnp.mean(scaled, -1, keepdims=True)
            - normed * jnp.mean(scaled * normed, -1, keepdims=True)
        )

    def add_sum(row, values):
        sums_ref[row : row + 1] += jnp.sum(values, 0, keepdims=True)

    sums_ref[...] = jnp.zeros_like(sums_ref)
    upb_sum[...] = jnp.zeros_like(upb_sum)

    weights_here(0)

    @pl.when(layer == 0)
    def _():
        x_copy.wait()

    def project(block):
        rows = rows_of(block)

        @pl.when(layer == 1)
        def _():
            x_move(block).wait_recv()
            wide[rows] = x_land[rows].astype(F32)

        low = wide[rows].astype(BF)
        x_low[rows] = low
        for slot in range(2):
            for c in range(3):
                part = pl.ds(c * side, side)
                value = jnp.dot(low, wq[slot, :, part], preferred_element_type=F32)
                if c != 1:
                    value = value + qvb_ref[slot, c // 2 : c // 2 + 1]
                qkv[slot, rows, part] = value.astype(BF)

    loop(0, blocks, project)
    hand_out(0)

    lane = lax.broadcasted_iota(jnp.int32, (1, 2 * HEAD_DIM), 1)
    masks = ((lane < HEAD_DIM).astype(F32).astype(BF), (lane >= HEAD_DIM).astype(F32).astype(BF))
    first_lane = lax.broadcasted_iota(jnp.int32, (page, 2 * HEAD_DIM), 1) < HEAD_DIM
    first_row = lax.broadcasted_iota(jnp.int32, (2 * HEAD_DIM, page), 0) < HEAD_DIM
    pairs = side // (2 * HEAD_DIM)

    def lanes(i, third):
        at = third * side + (i % pairs) * 2 * HEAD_DIM
        return pl.ds(pl.multiple_of(at, 2 * HEAD_DIM), 2 * HEAD_DIM)

    def attend(i):
        slot = i // pairs
        queries = qkv[slot, :, lanes(i, 0)] * jnp.asarray(scale, BF)
        keys = qkv[slot, :, lanes(i, 1)]
        values = qkv[slot, :, lanes(i, 2)]
        found = []
        for e in range(2):
            scores = nt(keys * masks[e], queries)
            expo = jnp.exp(scores - jnp.max(scores, 0, keepdims=True))
            share = 1.0 / jnp.sum(expo, 0, keepdims=True)
            low = (expo * share).astype(BF)
            probs[2 * i + e] = low
            found.append(tn(values, low))
        ctx[slot, :, lanes(i, 0)] = jnp.where(first_row, found[0], found[1]).T.astype(BF)

    loop(0, 2 * pairs, attend)
    hand_out(1)
    for i in range(1, 4):
        weights_here(i)

    def feed(block):
        rows = rows_of(block)
        attended = (
            jnp.dot(ctx[0, rows], wo[0], preferred_element_type=F32)
            + jnp.dot(ctx[1, rows], wo[1], preferred_element_type=F32)
            + shifts_ref[0:1]
        )
        normed, inverse = centred(wide[rows] + attended)
        n_one[rows] = normed
        r_one[rows] = inverse
        hidden = normed * gains_ref[0:1] + shifts_ref[1:2]
        z[rows] = hidden
        h_low[rows] = hidden.astype(BF)
        for slot in range(2):
            for c in range(units // tile):
                part = pl.ds(c * tile, tile)
                upper = (
                    jnp.dot(h_low[rows], wu[slot, :, part], preferred_element_type=F32)
                    + upb_ref[slot : slot + 1, part]
                )
                below = 0.5 * (1.0 + lax.erf(upper * ROOT_HALF))
                act[slot, rows, part] = (upper * below).astype(BF)
                slope[slot, rows, part] = (
                    below + upper * jnp.exp(-0.5 * upper * upper) * INV_ROOT_TWO_PI
                ).astype(BF)
        mixed = (
            jnp.dot(act[0, rows], wd[0], preferred_element_type=F32)
            + jnp.dot(act[1, rows], wd[1], preferred_element_type=F32)
            + shifts_ref[2:3]
        )
        normed, inverse = centred(z[rows] + mixed)
        n_two[rows] = normed
        r_two[rows] = inverse
        output = normed * gains_ref[1:2] + shifts_ref[3:4]
        wide[rows] = output

        @pl.when(layer == 0)
        def _():
            sent_low[rows] = output.astype(BF)
            x_move(block).start()

    loop(0, blocks, feed)
    y_copy = pltpu.make_async_copy(wide, y_ref, io_sem.at[2])
    y_copy.start()
    hand_out(2, 3)

    @pl.when(layer == 1)
    def _():
        given_copy.wait()

    def feed_back(block):
        rows = rows_of(block)

        @pl.when(layer == 0)
        def _():
            g_move(block).wait_recv()

        grad = g_land[rows].astype(F32)
        normed = n_two[rows]
        add_sum(1, grad * normed)
        add_sum(5, grad)
        grad = pulled(grad, normed, r_two[rows], gains_ref[1:2])
        z[rows] = grad
        low = grad.astype(BF)
        df_low[rows] = low
        add_sum(4, low.astype(F32))
        for slot in range(2):
            for c in range(units // tile):
                part = pl.ds(c * tile, tile)
                term = nt(df_low[rows], wd[slot, part])
                term = (term * slope[slot, rows, part].astype(F32)).astype(BF)
                slope[slot, rows, part] = term
                upb_sum[slot : slot + 1, part] += jnp.sum(term.astype(F32), 0, keepdims=True)
        grad = z[rows] + nt(slope[0, rows], wu[0]) + nt(slope[1, rows], wu[1])
        normed = n_one[rows]
        add_sum(0, grad * normed)
        add_sum(3, grad)
        grad = pulled(grad, normed, r_one[rows], gains_ref[0:1])
        z[rows] = grad
        low = grad.astype(BF)
        da_low[rows] = low
        add_sum(2, low.astype(F32))
        for slot in range(2):
            d_ctx[slot, rows] = nt(da_low[rows], wo[slot]).astype(BF)

    loop(0, blocks, feed_back)
    hand_out(5, 6, 7)

    def attend_back(i):
        slot = i // pairs
        queries = qkv[slot, :, lanes(i, 0)]
        keys = qkv[slot, :, lanes(i, 1)]
        values = qkv[slot, :, lanes(i, 2)]
        grads = d_ctx[slot, :, lanes(i, 0)]
        d_q, d_k, d_v = [], [], []
        for e in range(2):
            low = probs[2 * i + e]
            share = low.astype(F32)
            term = share * nt(values * masks[e], grads)
            term = (term - share * jnp.sum(term, 0, keepdims=True)).astype(BF)
            d_k.append(jnp.dot(term, queries, preferred_element_type=F32))
            d_v.append(jnp.dot(low, grads, preferred_element_type=F32))
            d_q.append(tn(keys, term))
        d_qkv[slot, :, lanes(i, 0)] = (
            jnp.where(first_row, d_q[0], d_q[1]).T * scale
        ).astype(BF)
        d_qkv[slot, :, lanes(i, 1)] = (jnp.where(first_lane, d_k[0], d_k[1]) * scale).astype(BF)
        d_qkv[slot, :, lanes(i, 2)] = jnp.where(first_lane, d_v[0], d_v[1]).astype(BF)

    loop(0, 2 * pairs, attend_back)
    hand_out(4)

    def leave(block):
        rows = rows_of(block)
        grad = z[rows] + nt(d_qkv[0, rows], wq[0]) + nt(d_qkv[1, rows], wq[1])
        z[rows] = grad

        @pl.when(layer == 1)
        def _():
            sent_low[rows] = grad.astype(BF)
            g_move(block).start()

    loop(0, blocks, leave)
    dx_copy = pltpu.make_async_copy(z, dx_ref, io_sem.at[3])
    dx_copy.start()
    for slot in range(2):
        for i in range(2):
            columns = pl.ds(2 * i * side, side)
            qvb_sum[slot, i : i + 1] = jnp.sum(
                d_qkv[slot, :, columns].astype(F32), 0, keepdims=True
            )
    for block in range(blocks):

        @pl.when(layer == 0)
        def _():
            x_move(block).wait_send()

        @pl.when(layer == 1)
        def _():
            g_move(block).wait_send()

    for i in range(4):
        weight_copies(i)[1].wait_send()
    for i in range(8):
        near, far = piece_copies(i)
        near.wait()
        far.wait()
    y_copy.wait()
    dx_copy.wait()


def layered(x, given, weights, qvb, upb, gains, shifts):
    page, width = x.shape
    qkv_weight, out_weight, up_weight, down_weight = weights
    side = out_weight.shape[1]
    units = down_weight.shape[1]
    blocks = page // ROWS
    heads = 2 * side // HEAD_DIM
    any_space = pl.BlockSpec(memory_space=pl.ANY)
    in_vmem = pl.BlockSpec(memory_space=pltpu.VMEM)
    dma = pltpu.SemaphoreType.DMA
    vmem = pltpu.VMEM
    flops = 8 * page * width * (4 * width + 4 * units) * 2
    return pl.pallas_call(
        layer_kernel,
        out_shape=(
            jax.ShapeDtypeStruct((2, page, 2 * width + side + units), BF),
            jax.ShapeDtypeStruct((2, page, 3 * side + 2 * width + units), BF),
            jax.ShapeDtypeStruct((page, width), F32),
            jax.ShapeDtypeStruct((page, width), F32),
            jax.ShapeDtypeStruct((6, width), F32),
            jax.ShapeDtypeStruct((2, 2, side), F32),
            jax.ShapeDtypeStruct((2, units), F32),
        ),
        in_specs=[any_space] * 6 + [in_vmem] * 4,
        out_specs=(any_space,) * 4 + (in_vmem,) * 3,
        scratch_shapes=[
            vmem((2, width, 3 * side), BF), vmem((2, side, width), BF),
            vmem((2, width, units), BF), vmem((2, units, width), BF),
            vmem((page, width), F32), vmem((page, width), BF), vmem((page, width), BF),
            vmem((page, width), BF), vmem((2, page, side), BF), vmem((2, page, side), BF),
            vmem((page, width), BF), vmem((2, page, units), BF), vmem((2, page, units), BF),
            vmem((2, page, 3 * side), BF), vmem((2, page, 3 * side), BF),
            vmem((page, width), BF), vmem((page, width), BF), vmem((heads, page, page), BF),
            vmem((page, width), F32), vmem((page, width), F32),
            vmem((page, 1), F32), vmem((page, 1), F32),
            vmem((page, width), F32), vmem((page, width), BF),
            dma((4,)), dma((4,)), dma((4,)),
            dma((blocks,)), dma((blocks,)), dma((blocks,)), dma((blocks,)),
            dma((8,)), dma((8,)), dma((8,)), dma((4,)),
        ],
        compiler_params=pltpu.CompilerParams(
            collective_id=1, has_side_effects=True, vmem_limit_bytes=62 << 20
        ),
        cost_estimate=pl.CostEstimate(
            flops=flops, bytes_accessed=200 << 20, transcendentals=0
        ),
        name="layer_both_ways",
    )(x, given, *weights, qvb, upb, gains, shifts)


def on_device(
    word_embed, boxes, mask_pos, replace_ids, cotangent, layout_table, vocab_table, embed_gain,
    embed_shift, qkv_weight, qv_bias, out_weight, up_weight, up_bias, down_weight, layer_gains,
    layer_biases,
):
    section = lax.axis_index("section")
    layer = section // 2
    half = section % 2
    is_first = layer == 0
    quarter, width = word_embed.shape
    page = 2 * quarter
    side = qkv_weight.shape[2] // 3

    words_a = routed(word_embed, [(1, 0), (2, 1)])
    words_b = routed(word_embed, [(3, 1)])
    given_a = routed(cotangent, [(0, 2), (2, 3)])
    given_b = routed(cotangent, [(1, 2)])
    words = jnp.concatenate(
        [jnp.where(half == 0, word_embed, words_a), jnp.where(half == 0, words_a, words_b)], 0
    )
    given = jnp.concatenate(
        [given_a, jnp.where(half == 0, given_b, cotangent)], 0
    )

    qvb = jnp.stack([qv_bias[0], swapped(qv_bias[0])])
    upb = jnp.concatenate([up_bias, swapped(up_bias)])
    gains = lax.dynamic_index_in_dim(layer_gains, layer, 0, keepdims=False)
    shifts = lax.dynamic_index_in_dim(layer_biases, layer, 0, keepdims=False)

    listed = lax.dynamic_index_in_dim(mask_pos, half, 0, keepdims=False)
    ids = lax.dynamic_index_in_dim(replace_ids, half, 0, keepdims=False)
    slots = ids.shape[0]
    rows_held = vocab_table.shape[0]
    asked = lax.all_gather(ids, "dp", axis=0, tiled=True)
    held = jnp.arange(rows_held, dtype=jnp.int32) + lax.axis_index("dp") * rows_held
    picked = (asked[:, None] == held[None, :]).astype(BF)
    slot_rows = lax.psum_scatter(
        matmul(picked, vocab_table).astype(BF), "dp", scatter_dimension=0, tiled=True
    )

    places = jnp.arange(page, dtype=jnp.int32)
    chosen = (listed[:, None] == places[None, :]).astype(BF)
    marked = jnp.any(listed[:, None] == places[None, :], axis=0)
    replaced = matmul_left_t(chosen, slot_rows)
    box_rows = lax.dynamic_slice_in_dim(boxes, half * page, page, 1)
    coords = jnp.arange(layout_table.shape[1], dtype=jnp.int32)
    one_x, one_y = (
        (box_rows[a][:, None] == coords[None, :]).astype(BF)
        + (box_rows[a + 2][:, None] == coords[None, :]).astype(BF)
        for a in (0, 1)
    )
    summed = (
        jnp.where(marked[:, None], replaced, words.astype(F32))
        + matmul(one_x, layout_table[0])
        + matmul(one_y, layout_table[1])
    )
    hidden_in, normed_in, inverse_in = normalize(summed, embed_gain, embed_shift)

    left, right, output, grad_rows, sums_grad, qvb_grad, upb_grad = layered(
        hidden_in, given, (qkv_weight, out_weight, up_weight, down_weight), qvb, upb, gains, shifts
    )

    grad_summed, eg_grad, es_grad = normalize_back(grad_rows, normed_in, inverse_in, embed_gain)
    grad_low = jnp.where(is_first, grad_summed, 0.0).astype(BF)
    word_grad = jnp.where(marked[:, None], 0.0, grad_low.astype(F32))
    left, right = (array.reshape(2 * page, -1) for array in (left, right))
    hidden_units = up_bias.shape[1]
    counts = (
        (width // BLOCK, 3),
        (side // BLOCK, width // side),
        (width // BLOCK, hidden_units // side),
        (hidden_units // BLOCK, width // side),
    )
    flat = jnp.concatenate(
        [
            qvb_grad[0].reshape(-1), upb_grad[0], qvb_grad[1].reshape(-1), upb_grad[1],
            sums_grad.reshape(-1), eg_grad, es_grad,
        ]
    ).reshape(-1, side)
    small_in = jnp.pad(flat, ((0, BLOCK - flat.shape[0]), (0, 0)))
    edge = jnp.stack([grad_low[:, :side], grad_low[:, side:]])
    first, second = boxes[:, :page], boxes[:, page:]
    pair = jnp.stack([jnp.where(half == 0, first, second), jnp.where(half == 0, second, first)])
    pair = jnp.where(half == 0, pair[:, 0::2], pair[:, 1::2])
    *sums, gathered, slot_rows_all, table_rows = reduced(
        left, right, small_in, edge, pair, listed[:, None], counts, side
    )
    outer = lax.axis_size("dp") // GROUP
    if outer > 1:
        groups = [[i + GROUP * g for g in range(outer)] for i in range(GROUP)]
        *sums, gathered = lax.psum((*sums, gathered), "dp", axis_index_groups=groups)
        slot_rows_all = lax.all_gather(
            slot_rows_all, "dp", axis_index_groups=groups, axis=1, tiled=True
        )
        table_grad = jnp.stack([matmul_left_t(one_x, grad_low), matmul_left_t(one_y, grad_low)])
        table_part = lax.psum_scatter(
            table_grad.astype(BF), ("dp", "section"), scatter_dimension=1, tiled=True
        ).astype(F32)
    else:
        table_part = (
            table_rows.reshape(2, 2, -1, side).transpose(1, 2, 0, 3).reshape(2, -1, width)
        ).astype(F32)
    sums = [total.astype(F32)[None] for total in sums]

    other_asked = swapped(asked)
    count = rows_held // lax.axis_size("section")
    base = (lax.axis_index("dp") * lax.axis_size("section") + section) * count
    rows_here = jnp.arange(count, dtype=jnp.int32) + base
    all_ids = jnp.concatenate([asked, other_asked])
    ordered = slot_rows_all.reshape(2, 2, -1, side).transpose(0, 2, 1, 3)
    ordered = ordered.reshape(-1, width)
    found = matmul((rows_here[:, None] == all_ids[None, :]).astype(BF), ordered)
    vocab_part = jnp.where(
        is_first, found, jnp.concatenate([found[:, side:], found[:, :side]], 1)
    )

    parts = gathered.astype(F32)[:, : flat.shape[0]].reshape(4, -1)
    partner = parts[jnp.where(half == 0, 1, 3)]
    far_partner = parts[jnp.where(half == 0, 3, 1)]
    edge_at = 2 * side + hidden_units
    own = parts[0, :edge_at] + partner[edge_at : 2 * edge_at]
    in_order = jnp.stack([parts[0] + partner, parts[2] + far_partner])[:, 2 * edge_at :]
    by_layer = jnp.where(layer == 0, in_order, in_order[::-1])
    small = (
        by_layer[:, : 2 * width].reshape(2, 2, width),
        by_layer[:, 2 * width : 6 * width].reshape(2, 4, width),
        by_layer[0, 6 * width : 7 * width],
        by_layer[0, 7 * width :],
        own[: 2 * side].reshape(1, 2, side),
        own[2 * side :].reshape(1, hidden_units),
    )

    out_first = output[:quarter].astype(BF)
    out_second = output[quarter:].astype(BF)
    act_a = routed(out_first, [(2, 0), (3, 2)])
    act_b = routed(out_second, [(2, 1)])
    grad_first = word_grad[:quarter].astype(BF)
    grad_second = word_grad[quarter:].astype(BF)
    ing_a = routed(grad_second, [(0, 1), (1, 3)])
    ing_b = routed(grad_first, [(1, 2)])
    activations = jnp.where(
        section == 3,
        output[quarter:],
        jnp.where(section == 1, act_b, act_a).astype(F32),
    )
    input_grad = jnp.where(
        section == 0,
        word_grad[:quarter],
        jnp.where(section == 2, ing_b, ing_a).astype(F32),
    )
    return (
        activations, input_grad, table_part, vocab_part, small[2], small[3],
        sums[0],
        small[4],
        sums[1], sums[2],
        small[5],
        sums[3], small[0], small[1],
    )


def solution(mesh):
    both = ("dp", "section")
    by_section = P("section", None, None)
    return jax.shard_map(
        on_device,
        mesh=mesh,
        in_specs=(
            P(both, None), P(None, "dp"), P("dp", None), P("dp", None), P(both, None), P(),
            P("dp", None), P(), P(), by_section, by_section, by_section, by_section,
            P("section", None), by_section, P(), P(),
        ),
        out_specs=(
            P(both, None), P(both, None), P(None, both, None), P(both, None), P(), P(),
            by_section, by_section, by_section, by_section, P("section", None), by_section,
            P(), P(),
        ),
        check_vma=False,
    )
```

time: 733 us -> 448 us (0.61)
  matrix products: 167 us -> 16 us
  Pallas kernels: 151 us -> 282 us
  local copies, waits for them, and re-layouts: 127 us -> 17.8 us
  other arithmetic: 93.2 us -> 27.1 us
  blocking collectives: 52.1 us -> 12.2 us
  waiting for transfers between devices: 85.2 us -> 50.2 us
  starting transfers between devices: 30.3 us -> 20.2 us
    pallas_call x1 -> x2, Pallas kernels: 151 us -> 282 us  [the longest x1 164 us: reduced(): pl.pallas_call(functools.partial(reduce_kernel, counts), out_shape=tuple(...]
    dot_general x21 -> x0, matrix products: 92.8 us -> none  [the longest x11 42.4 us: matmul_right_t(): return jnp.einsum('pa,ba->pb', left, right, preferred_element_type=F32)]
    unnamed x2 -> x0, blocking collectives: 52.1 us -> none
    ppermute x27 -> x11, waiting for transfers between devices: 41.5 us -> 1.07 us  [routed(): return lax.ppermute(block, 'section', route)]
    dot_general x16 -> x4, matrix products: 53.7 us -> 13.4 us  [matmul(): return jnp.dot(left, right, preferred_element_type=F32)]
    concatenate x4 -> x3, other arithmetic: 41.9 us -> 1.55 us  [the longest x1 0.93 us: on_device(): jnp.concatenate([given_a, jnp.where(half == 0, given_b, cotangent)], 0)]
    reshape x11 -> x3, local copies, waits for them, and re-layouts: 37.4 us -> 2.44 us  [the longest x1 2.43 us: on_device(): ordered = slot_rows_all.reshape(2, 2, -1, side).transpose(0, 2, 1, 3)]
    unnamed x348 -> x63, local copies, waits for them, and re-layouts: 39.9 us -> 5.44 us
  transfers between devices with their start and end apart: 30 -> 12, of which waited for: 6 -> 3; matrix products, arithmetic and copies ran while one was open for 32% -> 9% of each run, Pallas kernels for 21% -> 0%
where the time goes in v2:
time: 448 us; the launch traced here: 442 us
  Pallas kernels  282 us (63%)
  waiting for transfers between devices  50.2 us (11%)
  other arithmetic  27.1 us (6%)
  starting transfers between devices  20.2 us (5%)
  local copies, waits for them, and re-layouts  17.8 us (4%)
  matrix products  16 us (4%)
  between operations  15.8 us (4%)
  blocking collectives  12.2 us (3%)
    pallas_call x1, Pallas kernels, reduced(): pl.pallas_call(functools.partial(reduce_kernel, counts), out_shape=tuple(...  164 us
    pallas_call x1, Pallas kernels, layered(): pl.pallas_call(layer_kernel, out_shape=(jax.ShapeDtypeStruct((2, page, 2...  118 us
    reduce_scatter x1, waiting for transfers between devices, on_device(): lax.psum_scatter(matmul(picked, vocab_table).astype(BF), 'dp', scatter_di...  49.1 us
    ppermute x11, starting transfers between devices, routed(): return lax.ppermute(block, 'section', route)  20.1 us
    dot_general x4, matrix products, matmul(): return jnp.dot(left, right, preferred_element_type=F32)  13.4 us
    all_gather x1, blocking collectives, on_device(): asked = lax.all_gather(ids, 'dp', axis=0, tiled=True)  12.2 us
    broadcast_in_dim x4, other arithmetic, on_device(): sums = [total.astype(F32)[None] for total in sums]  9.54 us
  transfers between devices with their start and end apart: 12, of which 3 were waited for; matrix products, arithmetic and copies ran while one was open for 9% of the time, Pallas kernels for 0%

profile of v2, /device:TPU:0, one launch (start us, length us, event | category | flops | bytes accessed | tf_op | source)
XLA Modules:
  0.0 441.7 jit_solution(2755434785205344101)
XLA Ops:
  7.2 1.3 collective-permute-start
  8.5 0.7 collective-permute-start.1
  9.2 0.7 collective-permute-start.3
  9.9 5.5 %collective-permute-start.2 = (bf16[256,768]{1,0:T(8,128)(2,1)}, bf16[256,768]{1,0:T(8,128)(2,1)S(1)}, u32[]{:S(2)}, u32[]{:S(2)}) collective-permute-start(bf16[256,768]{1,0:T(8,128)(2,1)} %param.21), channel_id=1, source_target_pairs={{0,2},{2,3},{4,6},{6,7},{8,10},{10,11},{12,14},{14,15},{16,18},{18... | collective-permute-start | bytes 1179656 | tf_op jit(solution)/shard_map/ppermute | solution.py:19
  15.5 1.2 dynamic-slice
  17.4 0.8 fusion.35
  18.2 12.2 %all-reduce.1 = s32[768]{0:T(1024)S(1)} all-reduce(s32[768]{0:T(1024)S(1)} %fusion.35), channel_id=2, replica_groups=mesh['dp'=8,'section'=4] {'dp'}, use_global_device_ids=true, to_apply=%add.1 | all-reduce | flops 768 | bytes 6144 | tf_op jit(solution)/shard_map/all_gather | solution.py:952
  30.4 5.6 %fusion.18 = bf16[768,768]{1,0:T(8,128)(2,1)} fusion(bf16[2048,768]{1,0:T(8,128)(2,1)} %param.23, s32[2048]{0:T(1024)S(1)} %iota_add_fusion, s32[768]{0:T(1024)S(1)} %all-reduce.1), kind=kOutput, calls=%fused_computation.33 | convolution fusion | flops 2418081792 | bytes 4336640 | tf_op jit(solution)/shard_map/dot_general | solution.py:48
  36.2 0.6 dynamic-slice_bitcast_fusion.1.gains_ref
  36.8 0.1 constant_dynamic-slice_fusion
  36.9 0.6 dynamic-slice_bitcast_fusion.shifts_ref
  37.5 0.1 fusion.32
  37.6 0.6 broadcast_select_fusion.4.box_ref
  38.2 3.9 fusion.10
  42.2 2.4 fusion.12
  44.6 0.7 copy.36.listed_ref
  45.3 0.5 collective-permute-start.4
  45.8 0.8 collective-permute-done.4
  46.6 0.3 collective-permute-start.5
  47.0 0.6 pad_maximum_fusion.4.qvb_ref
  47.5 0.2 collective-permute-done.5
  47.8 0.6 pad_maximum_fusion.3.upb_ref
  48.5 0.9 pad_maximum_fusion.given_ref
  49.5 49.1 %reduce-scatter.2.cloned.1.call-done = bf16[96,768]{1,0:T(8,128)(2,1)} async-done(((bf16[768,768]{1,0:T(8,128)(2,1)}), bf16[96,768]{1,0:T(8,128)(2,1)}) %reduce-scatter.2.cloned.1.call-update) | async-done | bytes 147472 | tf_op jit(solution)/shard_map/reduce_scatter | solution.py:955
  98.6 2.6 fusion.42
  101.2 0.3 multiply_reduce_fusion.2
  101.5 0.3 copy-done.14
  101.9 1.4 multiply_add_fusion.x_ref
  103.3 118.3 %layer_both_ways.1 = (bf16[2,512,3456]{2,1,0:T(8,128)(2,1)}, bf16[2,512,4224]{2,1,0:T(8,128)(2,1)}, f32[512,768]{1,0:T(8,128)}, f32[512,768]{1,0:T(8,128)}, f32[...) custom-call(f32[512,768]{1,0:T(8,128)} %multiply_add_fusion.x_ref, ...), custom_call_target="tpu_custom_call" | custom-call | flops 57982058496 | bytes 209715200 | tf_op jit(solution)/shard_map/layer_both_ways/pallas_call | solution.py:881
  221.7 2.2 multiply_reduce_fusion
  224.1 3.1 convert_select_fusion
  227.3 0.7 pad.4.small_ref
  228.0 1.0 pad_maximum_fusion.1.edge_ref
  229.0 164.2 %gradient_sums.1 = (bf16[768,1152]{1,0:T(8,128)(2,1)}, bf16[384,768]{1,0:T(8,128)(2,1)}, bf16[768,1536]{1,0:T(8,128)(2,1)}, bf16[1536,768]{1,0:T(8,128)(2,1)}, b...) custom-call(bf16[1024,3456]{1,0:T(8,128)(2,1)} %bitcast.86, ...), custom_call_target="tpu_custom_call" | custom-call | flops 7348420608 | bytes 419430400 | tf_op jit(solution)/shard_map/gradient_sums/pallas_call | solution.py:485
  393.1 0.9 convert_element_type.78
  394.1 0.1 copy.42
  394.2 0.1 dynamic-slice_add_fusion.2
  394.3 0.6 slice.165
  395.0 0.1 dynamic-slice_add_fusion.1
  395.2 1.2 rev.3
  396.5 1.0 fusion.40
  397.5 1.6 collective-permute-start.6
  399.0 1.3 collective-permute-start.7
  400.3 1.0 fusion.39
  401.4 1.4 collective-permute-start.8
  402.8 6.9 %collective-permute-start.9 = (bf16[256,768]{1,0:T(8,128)(2,1)}, bf16[256,768]{1,0:T(8,128)(2,1)}, u32[]{:S(2)}, u32[]{:S(2)}) collective-permute-start(bf16[256,768]{1,0:T(8,128)(2,1)} %get-tuple-element.54), channel_id=1, source_target_pairs={{0,1},{1,3},{4,5},{5,7},{8,9},{9,11},{12,13},{13,15},{16,17},{17,1... | collective-permute-start | bytes 1179656 | tf_op jit(solution)/shard_map/ppermute | solution.py:19
  409.7 2.4 copy.38
  412.1 0.5 copy.40
  412.6 1.4 fusion.4
  414.1 0.1 fusion.38
  414.2 1.4 copy-done.6
  415.5 2.0 bitcast_convert_fusion.2
  417.6 0.8 copy-done.4
  418.4 2.8 bitcast_convert_fusion.1
  421.2 2.5 bitcast_convert_fusion
  423.7 1.3 maximum_select_fusion
  425.1 0.7 copy.39
  425.8 0.6 slice.147
  426.3 0.6 reshape.124
  427.0 0.6 reshape.125
  427.6 2.2 bitcast_convert_fusion.3
  429.8 0.6 slice_reduce_fusion.3
  430.4 2.0 convert_select_fusion.2
  432.4 2.0 convert_select_fusion.1
  (98 shorter events, 0.9 us)
Async XLA Ops:
  7.2 29.7 %copy-start = (f32[2,4,768]{2,1,0:T(4,128)S(1)}, f32[2,4,768]{2,1,0:T(4,128)}, u32[]{:S(2)}) copy-start(f32[2,4,768]{2,1,0:T(4,128)} %param.33) | copy-start | bytes 73732
  7.2 91.4 %reduce-scatter.2.cloned.1.call-start = ((), (), s32[]{:S(2)}) async-start(), calls=%async_computation.1 | async-start | bytes 1327104 | tf_op jit(solution)/shard_map/reduce_scatter | solution.py:955
  7.2 42.2 %collective-permute-start = (bf16[256,768]{1,0:T(8,128)(2,1)}, bf16[256,768]{1,0:T(8,128)(2,1)S(1)}, u32[]{:S(2)}, u32[]{:S(2)}) collective-permute-start(bf16[256,768]{1,0:T(8,128)(2,1)} %param.17), channel_id=1, source_target_pairs={{1,0},{2,1},{5,4},{6,5},{9,8},{10,9},{13,12},{14,13},{17,16},{18,1... | collective-permute-start | bytes 1179656 | tf_op jit(solution)/shard_map/ppermute | solution.py:19
  8.5 40.9 %collective-permute-start.1 = (bf16[256,768]{1,0:T(8,128)(2,1)}, bf16[256,768]{1,0:T(8,128)(2,1)S(1)}, u32[]{:S(2)}, u32[]{:S(2)}) collective-permute-start(bf16[256,768]{1,0:T(8,128)(2,1)} %param.17), channel_id=1, source_target_pairs={{3,1},{7,5},{11,9},{15,13},{19,17},{23,21},{27,25},{31,29}} | collective-permute-start | bytes 1179656 | tf_op jit(solution)/shard_map/ppermute | solution.py:19
  9.2 39.2 %collective-permute-start.3 = (bf16[256,768]{1,0:T(8,128)(2,1)}, bf16[256,768]{1,0:T(8,128)(2,1)S(1)}, u32[]{:S(2)}, u32[]{:S(2)}) collective-permute-start(bf16[256,768]{1,0:T(8,128)(2,1)} %param.21), channel_id=1, source_target_pairs={{1,2},{5,6},{9,10},{13,14},{17,18},{21,22},{25,26},{29,30}} | collective-permute-start | bytes 1179656 | tf_op jit(solution)/shard_map/ppermute | solution.py:19
  9.9 38.5 %collective-permute-start.2 = (bf16[256,768]{1,0:T(8,128)(2,1)}, bf16[256,768]{1,0:T(8,128)(2,1)S(1)}, u32[]{:S(2)}, u32[]{:S(2)}) collective-permute-start(bf16[256,768]{1,0:T(8,128)(2,1)} %param.21), channel_id=1, source_target_pairs={{0,2},{2,3},{4,6},{6,7},{8,10},{10,11},{12,14},{14,15},{16,18},{18... | collective-permute-start | bytes 1179656 | tf_op jit(solution)/shard_map/ppermute | solution.py:19
  30.4 14.9 %collective-permute-start.10 = (s32[768]{0:T(1024)S(1)}, s32[768]{0:T(1024)S(1)}, u32[]{:S(2)}, u32[]{:S(2)}) collective-permute-start(s32[768]{0:T(1024)S(1)} %all-reduce.1), channel_id=1, source_target_pairs={{0,1},{1,0},{2,3},{3,2},{4,5},{5,4},{6,7},{7,6},{8,9},{9,8},{10,11... | collective-permute-start | bytes 9224 | tf_op jit(solution)/shard_map/ppermute | solution.py:19
  30.4 5.7 %copy-start.13 = (s32[4,1024]{1,0:T(4,128)S(1)}, s32[4,1024]{1,0:T(4,128)}, u32[]{:S(2)}) copy-start(s32[4,1024]{1,0:T(4,128)} %param.18) | copy-start | bytes 49156
  30.4 5.8 %copy-start.20 = (f32[2,2,768]{2,1,0:T(2,128)S(1)}, f32[2,2,768]{2,1,0:T(2,128)}, u32[]{:S(2)}) copy-start(f32[2,2,768]{2,1,0:T(2,128)} %param.32) | copy-start | bytes 36868
  30.4 6.5 %copy-start.22 = (s32[2,96]{1,0:T(2,128)S(1)}, s32[2,96]{1,0:T(2,128)}, u32[]{:S(2)}) copy-start(s32[2,96]{1,0:T(2,128)} %param.19) | copy-start | bytes 2308
  38.2 3.9 copy-start.23
  42.1 3.1 copy-start.21
  42.1 4.5 %copy-start.18 = (f32[1,1536]{1,0:T(1,128)S(1)}, f32[1,1536]{1,0:T(1,128)}, u32[]{:S(2)}) copy-start(f32[1,1536]{1,0:T(1,128)} %param.30) | copy-start | bytes 18436
  42.1 6.3 %copy-start.8 = (bf16[256,768]{1,0:T(8,128)(2,1)S(1)}, bf16[256,768]{1,0:T(8,128)(2,1)}, u32[]{:S(2)}) copy-start(bf16[256,768]{1,0:T(8,128)(2,1)} %param.21) | copy-start | bytes 1179652
  44.5 4.9 %copy-start.9 = (bf16[256,768]{1,0:T(8,128)(2,1)S(1)}, bf16[256,768]{1,0:T(8,128)(2,1)}, u32[]{:S(2)}) copy-start(bf16[256,768]{1,0:T(8,128)(2,1)} %param.17) | copy-start | bytes 1179652
  45.3 1.3 collective-permute-start.4
  46.6 1.2 collective-permute-start.5
  101.2 0.7 copy-start.14
  101.2 0.7 copy-start.19
  221.6 2.2 copy-start.17
  221.6 2.2 copy-start.16
  221.6 2.3 copy-start.15
  229.0 167.5 %copy-start.7 = (f32[512,768]{1,0:T(8,128)S(1)}, f32[512,768]{1,0:T(8,128)}, u32[]{:S(2)}) copy-start(f32[512,768]{1,0:T(8,128)} %get-tuple-element.28) | copy-start | bytes 4718596
  394.1 6.3 %copy-start.2 = (f32[512,768]{1,0:T(8,128)S(1)}, f32[512,768]{1,0:T(8,128)}, u32[]{:S(2)}) copy-start(f32[512,768]{1,0:T(8,128)} %get-tuple-element.50) | copy-start | bytes 4718596
  396.5 4.9 %copy-start.10 = (f32[2,6144]{1,0:T(2,128)}, f32[2,6144]{1,0:T(2,128)S(1)}, u32[]{:S(2)}) copy-start(f32[2,6144]{1,0:T(2,128)S(1)} %broadcast_select_fusion.3) | copy-start | bytes 147460
  396.5 13.2 %copy-start.5 = (bf16[4,8,96,384]{3,2,1,0:T(8,128)(2,1)S(1)}, bf16[4,8,96,384]{3,2,1,0:T(8,128)(2,1)}, u32[]{:S(2)}) copy-start(bf16[4,8,96,384]{3,2,1,0:T(8,128)(2,1)} %get-tuple-element.36) | copy-start | bytes 7077892
  397.5 32.9 %collective-permute-start.6 = (bf16[256,768]{1,0:T(8,128)(2,1)}, bf16[256,768]{1,0:T(8,128)(2,1)}, u32[]{:S(2)}, u32[]{:S(2)}) collective-permute-start(bf16[256,768]{1,0:T(8,128)(2,1)} %get-tuple-element.57), channel_id=1, source_target_pairs={{2,1},{6,5},{10,9},{14,13},{18,17},{22,21},{26,25},{30,29}} | collective-permute-start | bytes 1179656 | tf_op jit(solution)/shard_map/ppermute | solution.py:19
  399.0 31.4 %collective-permute-start.7 = (bf16[256,768]{1,0:T(8,128)(2,1)}, bf16[256,768]{1,0:T(8,128)(2,1)}, u32[]{:S(2)}, u32[]{:S(2)}) collective-permute-start(bf16[256,768]{1,0:T(8,128)(2,1)} %get-tuple-element.56), channel_id=1, source_target_pairs={{2,0},{3,2},{6,4},{7,6},{10,8},{11,10},{14,12},{15,14},{18,16},{19... | collective-permute-start | bytes 1179656 | tf_op jit(solution)/shard_map/ppermute | solution.py:19
  401.4 31.0 %collective-permute-start.8 = (bf16[256,768]{1,0:T(8,128)(2,1)}, bf16[256,768]{1,0:T(8,128)(2,1)}, u32[]{:S(2)}, u32[]{:S(2)}) collective-permute-start(bf16[256,768]{1,0:T(8,128)(2,1)} %get-tuple-element.55), channel_id=1, source_target_pairs={{1,2},{5,6},{9,10},{13,14},{17,18},{21,22},{25,26},{29,30}} | collective-permute-start | bytes 1179656 | tf_op jit(solution)/shard_map/ppermute | solution.py:19
  402.8 29.6 %collective-permute-start.9 = (bf16[256,768]{1,0:T(8,128)(2,1)}, bf16[256,768]{1,0:T(8,128)(2,1)}, u32[]{:S(2)}, u32[]{:S(2)}) collective-permute-start(bf16[256,768]{1,0:T(8,128)(2,1)} %get-tuple-element.54), channel_id=1, source_target_pairs={{0,1},{1,3},{4,5},{5,7},{8,9},{9,11},{12,13},{13,15},{16,17},{17,1... | collective-permute-start | bytes 1179656 | tf_op jit(solution)/shard_map/ppermute | solution.py:19
  414.1 1.5 copy-start.6
  415.5 2.8 copy-start.4
  418.4 2.8 copy-start.3
  423.7 1.3 copy-start.12
  423.7 2.6 slice-start
  423.7 3.2 slice-start.1
  425.0 4.7 %copy-start.11 = (f32[2,6144]{1,0:T(2,128)S(1)}, f32[2,6144]{1,0:T(2,128)}, u32[]{:S(2)}) copy-start(f32[2,6144]{1,0:T(2,128)} %copy-done.10) | copy-start | bytes 147460
  430.4 4.0 copy-start.1
Sparse Core Ops, SparseCore 0:
  36.1 62.3 reduce-scatter.1

commit v3 on v2

--- a/solution.py
+++ b/solution.py
@@ -26,28 +26,6 @@
     return routed(block, SWAP)
 
 
-def normalize(values, gain, shift):
-    center = values - jnp.mean(values, -1, keepdims=True)
-    spread = jnp.mean(center * center, -1, keepdims=True)
-    inverse = lax.rsqrt(spread + EPS)
-    normed = center * inverse
-    return (normed * gain + shift, normed, inverse)
-
-
-def normalize_back(grad, normed, inverse, gain):
-    scaled = grad * gain
-    centered = (
-        scaled
-        - jnp.mean(scaled, -1, keepdims=True)
-        - normed * jnp.mean(scaled * normed, -1, keepdims=True)
-    )
-    return (inverse * centered, jnp.sum(grad * normed, 0), jnp.sum(grad, 0))
-
-
-def matmul(left, right):
-    return jnp.dot(left, right, preferred_element_type=F32)
-
-
 def matmul_left_t(left, right):
     return jnp.einsum("pa,pb->ab", left, right, preferred_element_type=F32)
 
@@ -77,12 +55,18 @@
 
 
 def reduce_kernel(
-    counts, a_ref, b_ref, small_ref, edge_ref, box_ref, listed_ref,
-    q_ref, o_ref, u_ref, d_ref, gathered_ref, rows_ref, table_ref,
-    buf, total, gathered, edge, rows, table, piece,
+    counts, a_in, b_in, small_ref, edge_ref, mine_ref, box_ref, listed_ref,
+    q_ref, o_ref, u_ref, d_ref, gathered_ref, rows_ref, table_ref, act_ref, ing_ref,
+    a_ref, b_ref, buf, total, gathered, edge, rows, table, piece,
     send, recv, out_sem, g_send, g_recv, e_send, e_recv, r_send, r_recv, t_send, t_recv,
-    f_send, f_recv, last_sem,
+    f_send, f_recv, m_send, m_recv, last_sem, in_sem,
 ):
+    loads = (
+        pltpu.make_async_copy(a_in, a_ref, in_sem.at[0]),
+        pltpu.make_async_copy(b_in, b_ref, in_sem.at[1]),
+    )
+    for copy in loads:
+        copy.start()
     me = lax.axis_index("dp")
     section = lax.axis_index("section")
     n_sections = lax.axis_size("section")
@@ -128,6 +112,30 @@
             device_id_type=mesh_id,
         )
 
+    quarter = mine_ref.shape[0] // 2
+
+    def spread(r, target, kind):
+        return remote(
+            mine_ref.at[pl.ds(r * quarter, quarter)], target, m_send.at[r], m_recv.at[kind],
+            (me, 2 * half + r),
+        )
+
+    def keep(r, target):
+        return pltpu.make_async_copy(
+            mine_ref.at[pl.ds(r * quarter, quarter)], target, m_send.at[r]
+        )
+
+    for r in range(2):
+        for kind, target in ((0, ing_ref), (1, act_ref)):
+
+            @pl.when((layer == kind) & (section != 2 * half + r))
+            def _():
+                spread(r, target, kind).start()
+
+            @pl.when((layer == kind) & (section == 2 * half + r))
+            def _():
+                keep(r, target).start()
+
     def edge_across():
         return remote(
             edge_ref.at[1], edge.at[0], e_send.at[0], e_recv.at[0], (me, other_layer)
@@ -420,6 +428,8 @@
             (me, (section + n_sections - step) % n_sections),
         )
 
+    for copy in loads:
+        copy.wait()
     loop(0, EXTRA, advance)
 
     @pl.when(layer == 1)
@@ -462,6 +472,23 @@
     for copy in outs:
         copy.start()
 
+    for r in range(2):
+        for kind, target in ((0, ing_ref), (1, act_ref)):
+
+            @pl.when((layer == kind) & (section != 2 * half + r))
+            def _():
+                spread(r, target, kind).wait_send()
+
+            @pl.when((layer == kind) & (section == 2 * half + r))
+            def _():
+                keep(r, target).wait()
+
+    for kind, target in ((0, ing_ref), (1, act_ref)):
+
+        @pl.when(section != 2 * kind + layer)
+        def _():
+            spread(0, target, kind).wait_recv()
+
     @pl.when(layer == 0)
     def _():
         edge_across().wait_send()
@@ -472,7 +499,7 @@
         copy.wait()
 
 
-def reduced(a, b, small, edge, boxes, listed, counts, side):
+def reduced(a, b, small, edge, mine, boxes, listed, counts, side):
     chunks = 1 + sum(count[0] * count[1] for count in counts)
     n_sections = lax.axis_size("section")
     kept = 32
@@ -491,10 +518,14 @@
             jax.ShapeDtypeStruct((n_sections, kept, side), BF),
             jax.ShapeDtypeStruct((4, GROUP, slots, side), BF),
             jax.ShapeDtypeStruct((n_sections, BLOCK // n_sections, side), BF),
+            jax.ShapeDtypeStruct((mine.shape[0] // 2, mine.shape[1]), BF),
+            jax.ShapeDtypeStruct((mine.shape[0] // 2, mine.shape[1]), BF),
         ),
-        in_specs=[in_vmem] * 6,
-        out_specs=(any_space,) * 7,
+        in_specs=[any_space] * 2 + [in_vmem] * 2 + [any_space] + [in_vmem] * 2,
+        out_specs=(any_space,) * 9,
         scratch_shapes=[
+            pltpu.VMEM(a.shape, BF),
+            pltpu.VMEM(b.shape, BF),
             pltpu.VMEM((4, chunks, BLOCK, side), BF),
             pltpu.VMEM((BLOCK, side), F32),
             pltpu.VMEM((n_sections, kept, side), BF),
@@ -508,7 +539,8 @@
             dma((6, GROUP)), dma((4, GROUP)),
             dma((3, GROUP)), dma((3, GROUP)),
             dma((n_sections,)), dma((n_sections,)),
-            dma((3,)),
+            dma((2,)), dma((2,)),
+            dma((3,)), dma((2,)),
         ],
         compiler_params=pltpu.CompilerParams(
             collective_id=0, has_side_effects=True, vmem_limit_bytes=60 << 20
@@ -517,17 +549,18 @@
             flops=flops, bytes_accessed=400 << 20, transcendentals=0
         ),
         name="gradient_sums",
-    )(a, b, small, edge, boxes, listed)
+    )(a, b, small, edge, mine, boxes, listed)
 
 
 ROWS = 256
 
 
 def layer_kernel(
-    x_ref, given_ref, q_own, o_own, u_own, d_own, qvb_ref, upb_ref, gains_ref, shifts_ref,
-    a_ref, b_ref, y_ref, dx_ref, sums_ref, qvb_sum, upb_sum,
+    x_ref, given_ref, norm_ref, column_ref, q_own, o_own, u_own, d_own, qvb_ref, upb_ref,
+    gains_ref, shifts_ref, first_gain_ref,
+    a_ref, b_ref, edge_ref, mine_ref, small_ref, sums_ref, upb_sum,
     wq, wo, wu, wd, wide, x_land, g_land, x_low, ctx, d_ctx, h_low, act, slope, qkv, d_qkv,
-    da_low, df_low, probs, n_one, n_two, r_one, r_two, z, sent_low,
+    da_low, df_low, probs, n_one, n_two, r_one, r_two, z, sent_low, columns,
     w_local, w_send, w_recv, x_send, x_recv, g_send, g_recv, p_local, p_send, p_recv, io_sem,
 ):
     me = lax.axis_index("dp")
@@ -749,16 +782,17 @@
         n_two[rows] = normed
         r_two[rows] = inverse
         output = normed * gains_ref[1:2] + shifts_ref[3:4]
-        wide[rows] = output
+        sent_low[rows] = output.astype(BF)
 
         @pl.when(layer == 0)
         def _():
-            sent_low[rows] = output.astype(BF)
             x_move(block).start()
 
+        @pl.when(layer == 1)
+        def _():
+            mine_ref[rows] = sent_low[rows]
+
     loop(0, blocks, feed)
-    y_copy = pltpu.make_async_copy(wide, y_ref, io_sem.at[2])
-    y_copy.start()
     hand_out(2, 3)
 
     @pl.when(layer == 1)
@@ -802,6 +836,13 @@
 
     loop(0, blocks, feed_back)
     hand_out(5, 6, 7)
+    norm_copy = pltpu.make_async_copy(norm_ref, n_two, io_sem.at[2])
+    column_copy = pltpu.make_async_copy(column_ref, columns, io_sem.at[3])
+
+    @pl.when(layer == 0)
+    def _():
+        norm_copy.start()
+        column_copy.start()
 
     def attend_back(i):
         slot = i // pairs
@@ -827,6 +868,11 @@
     loop(0, 2 * pairs, attend_back)
     hand_out(4)
 
+    @pl.when(layer == 0)
+    def _():
+        norm_copy.wait()
+        column_copy.wait()
+
     def leave(block):
         rows = rows_of(block)
         grad = z[rows] + nt(d_qkv[0, rows], wq[0]) + nt(d_qkv[1, rows], wq[1])
@@ -834,18 +880,37 @@
 
         @pl.when(layer == 1)
         def _():
-            sent_low[rows] = grad.astype(BF)
+            sent_low[rows] = z[rows].astype(BF)
             g_move(block).start()
 
+        @pl.when(layer == 0)
+        def _():
+            grad = z[rows]
+            normed = n_two[rows]
+            add_sum(6, grad * normed)
+            add_sum(7, grad)
+            low = pulled(grad, normed, columns[0, rows], first_gain_ref[...]).astype(BF)
+            edge_ref[0, rows] = low[:, :side]
+            edge_ref[1, rows] = low[:, side:]
+            mine_ref[rows] = (low.astype(F32) * columns[1, rows]).astype(BF)
+
     loop(0, blocks, leave)
-    dx_copy = pltpu.make_async_copy(z, dx_ref, io_sem.at[3])
-    dx_copy.start()
+    small_ref[...] = jnp.zeros_like(small_ref)
+    pieces = units // side
     for slot in range(2):
         for i in range(2):
-            columns = pl.ds(2 * i * side, side)
-            qvb_sum[slot, i : i + 1] = jnp.sum(
-                d_qkv[slot, :, columns].astype(F32), 0, keepdims=True
+            part = pl.ds(2 * i * side, side)
+            at = slot * (2 + pieces) + i
+            small_ref[at : at + 1] = jnp.sum(
+                d_qkv[slot, :, part].astype(F32), 0, keepdims=True
             )
+        for i in range(pieces):
+            at = slot * (2 + pieces) + 2 + i
+            small_ref[at : at + 1] = upb_sum[slot : slot + 1, pl.ds(i * side, side)]
+    for i in range(8):
+        for j in range(2):
+            at = 2 * (2 + pieces) + 2 * i + j
+            small_ref[at : at + 1] = sums_ref[i : i + 1, pl.ds(j * side, side)]
     for block in range(blocks):
 
         @pl.when(layer == 0)
@@ -862,11 +927,9 @@
         near, far = piece_copies(i)
         near.wait()
         far.wait()
-    y_copy.wait()
-    dx_copy.wait()
-
-
-def layered(x, given, weights, qvb, upb, gains, shifts):
+
+
+def layered(x, given, norm, columns, weights, qvb, upb, gains, shifts, first_gain):
     page, width = x.shape
     qkv_weight, out_weight, up_weight, down_weight = weights
     side = out_weight.shape[1]
@@ -883,15 +946,14 @@
         out_shape=(
             jax.ShapeDtypeStruct((2, page, 2 * width + side + units), BF),
             jax.ShapeDtypeStruct((2, page, 3 * side + 2 * width + units), BF),
-            jax.ShapeDtypeStruct((page, width), F32),
-            jax.ShapeDtypeStruct((page, width), F32),
-            jax.ShapeDtypeStruct((6, width), F32),
-            jax.ShapeDtypeStruct((2, 2, side), F32),
-            jax.ShapeDtypeStruct((2, units), F32),
+            jax.ShapeDtypeStruct((2, page, side), BF),
+            jax.ShapeDtypeStruct((page, width), BF),
+            jax.ShapeDtypeStruct((BLOCK, side), F32),
         ),
-        in_specs=[any_space] * 6 + [in_vmem] * 4,
-        out_specs=(any_space,) * 4 + (in_vmem,) * 3,
+        in_specs=[any_space] * 8 + [in_vmem] * 5,
+        out_specs=(any_space,) * 2 + (in_vmem,) * 3,
         scratch_shapes=[
+            vmem((8, width), F32), vmem((2, units), F32),
             vmem((2, width, 3 * side), BF), vmem((2, side, width), BF),
             vmem((2, width, units), BF), vmem((2, units, width), BF),
             vmem((page, width), F32), vmem((page, width), BF), vmem((page, width), BF),
@@ -901,7 +963,7 @@
             vmem((page, width), BF), vmem((page, width), BF), vmem((heads, page, page), BF),
             vmem((page, width), F32), vmem((page, width), F32),
             vmem((page, 1), F32), vmem((page, 1), F32),
-            vmem((page, width), F32), vmem((page, width), BF),
+            vmem((page, width), F32), vmem((page, width), BF), vmem((2, page, 1), F32),
             dma((4,)), dma((4,)), dma((4,)),
             dma((blocks,)), dma((blocks,)), dma((blocks,)), dma((blocks,)),
             dma((8,)), dma((8,)), dma((8,)), dma((4,)),
@@ -913,7 +975,378 @@
             flops=flops, bytes_accessed=200 << 20, transcendentals=0
         ),
         name="layer_both_ways",
-    )(x, given, *weights, qvb, upb, gains, shifts)
+    )(x, given, norm, columns, *weights, qvb, upb, gains, shifts, first_gain)
+
+
+def front_kernel(
+    words_ref, cot_ref, ids_ref, listed_ref, box_ref, vocab_ref, table_ref, gain_ref, shift_ref,
+    x_ref, given_ref, norm_ref, column_ref, ids_out,
+    words, ids_all, vocab, spots, picks, land, other, sum_scratch, x_s, norm_s, column_s,
+    w_send, w_recv, c_send, c_recv, i_send, i_recv, s_send, s_recv, o_send, o_recv, local,
+):
+    me = lax.axis_index("dp")
+    section = lax.axis_index("section")
+    n_sections = lax.axis_size("section")
+    n_dp = ids_all.shape[0]
+    layer = section // 2
+    half = section % 2
+    mesh_id = pl.DeviceIdType.MESH
+    quarter = words_ref.shape[0]
+    page, width = x_s.shape
+    slots = picks.shape[1]
+    side = picks.shape[2]
+    held = vocab.shape[0]
+
+    vocab_copy = pltpu.make_async_copy(
+        vocab_ref.at[:, pl.ds(pl.multiple_of(layer * side, side), side)], vocab, local.at[0]
+    )
+    vocab_copy.start()
+
+    barrier = pltpu.get_barrier_semaphore()
+
+    def greet(step, carry):
+        pl.semaphore_signal(
+            barrier, inc=1, device_id=((me + step) % n_dp, section), device_id_type=mesh_id
+        )
+        return carry
+
+    lax.fori_loop(1, n_dp, greet, 0)
+    for step in range(1, n_sections):
+        pl.semaphore_signal(
+            barrier, inc=1, device_id=(me, (section + step) % n_sections), device_id_type=mesh_id
+        )
+    pl.semaphore_wait(barrier, n_dp - 1 + n_sections - 1)
+
+    def remote(source, target, sent, got, device):
+        return pltpu.make_async_remote_copy(
+            src_ref=source, dst_ref=target, send_sem=sent, recv_sem=got, device_id=device,
+            device_id_type=mesh_id,
+        )
+
+    def ids_move(step):
+        return remote(
+            ids_ref, ids_all.at[me], i_send.at[step], i_recv.at[me], ((me + step) % n_dp, section)
+        )
+
+    def ids_got(step):
+        source = (me + step) % n_dp
+        return remote(
+            ids_ref, ids_all.at[source], i_send.at[0], i_recv.at[source],
+            (me, (section + 1) % n_sections),
+        )
+
+    loop(1, n_dp, lambda step: ids_move(step).start())
+    ids_all[me] = ids_ref[...]
+
+    words_move = remote(
+        words_ref, words.at[half], w_send, w_recv.at[half], (me, layer)
+    )
+    given_part = given_ref.at[pl.ds(pl.multiple_of(half * quarter, quarter), quarter)]
+    given_move = remote(cot_ref, given_part, c_send, c_recv.at[half], (me, 2 + layer))
+    given_keep = pltpu.make_async_copy(cot_ref, given_part, c_send)
+
+    @pl.when(section != 0)
+    def _():
+        words_move.start()
+
+    @pl.when(section == 0)
+    def _():
+        words[0] = words_ref[...]
+
+    @pl.when(section != 3)
+    def _():
+        given_move.start()
+
+    @pl.when(section == 3)
+    def _():
+        given_keep.start()
+
+    loop(1, n_dp, lambda step: ids_got(step).wait_recv())
+    lists = ids_all[...].astype(F32)
+    lists = jnp.where(half == 0, lists[:, 0], lists[:, 1])
+    sum_scratch[...] = jnp.zeros_like(sum_scratch)
+    sum_scratch[0:n_dp] = lists
+    across = sum_scratch[...].T
+    at = (me * held + lax.broadcasted_iota(jnp.int32, (slots, held), 1)).astype(F32)
+    for origin in range(n_dp):
+        spots[origin * slots : (origin + 1) * slots] = (
+            at == across[:slots, origin : origin + 1]
+        ).astype(F32).astype(BF)
+    vocab_copy.wait()
+    found = jnp.dot(spots[...], vocab[...], preferred_element_type=F32).astype(BF)
+    for origin in range(n_dp):
+        picks[origin] = found[origin * slots : (origin + 1) * slots]
+
+    def slots_move(step):
+        to = (me + step) % n_dp
+        return remote(
+            picks.at[to], land.at[me], s_send.at[step], s_recv.at[me], (to, section)
+        )
+
+    def slots_got(step):
+        source = (me + step) % n_dp
+        return remote(
+            picks.at[0], land.at[source], s_send.at[0], s_recv.at[source],
+            (me, (section + 1) % n_sections),
+        )
+
+    loop(1, n_dp, lambda step: slots_move(step).start())
+    land[me] = picks[me]
+
+    @pl.when(layer == 0)
+    def _():
+        coords = lax.broadcasted_iota(jnp.int32, (table_ref.shape[1], page), 0)
+        for kind in range(2):
+            ones = (coords == box_ref[kind : kind + 1]).astype(F32) + (
+                coords == box_ref[kind + 2 : kind + 3]
+            ).astype(F32)
+            term = lax.dot_general(
+                ones.astype(BF), table_ref[kind], (((0,), (0,)), ((), ())),
+                preferred_element_type=F32,
+            )
+            if kind == 0:
+                x_s[...] = term
+            else:
+                x_s[...] += term
+
+    loop(1, n_dp, lambda step: slots_got(step).wait_recv())
+    mine = land[0]
+    for origin in range(1, n_dp):
+        mine = mine + land[origin]
+    other[1] = mine
+    other_move = remote(other.at[1], other.at[0], o_send, o_recv, (me, half))
+
+    @pl.when(layer == 1)
+    def _():
+        other_move.start()
+
+    @pl.when(layer == 0)
+    def _():
+        for r in range(2):
+
+            @pl.when(section + r > 0)
+            def _():
+                remote(
+                    words_ref, words.at[r], w_send, w_recv.at[r], (me, section + 1)
+                ).wait_recv()
+
+        chosen = (listed_ref[...] == lax.broadcasted_iota(jnp.int32, (slots, page), 1))
+        chosen = chosen.astype(F32).astype(BF)
+
+        def tn(right):
+            return lax.dot_general(
+                chosen, right, (((0,), (0,)), ((), ())), preferred_element_type=F32
+            )
+
+        marked = tn(jnp.ones((slots, BLOCK), BF))[:, 0:1]
+        column_s[1] = 1.0 - marked
+        other_move.wait_recv()
+        for part, values in ((0, other[1]), (1, other[0])):
+            columns = pl.ds(part * side, side)
+            x_s[:, columns] += tn(values)
+        for r in range(2):
+            rows = pl.ds(r * quarter, quarter)
+            kept = column_s[1, rows]
+            summed = x_s[rows] + words[r].astype(F32) * kept
+            center = summed - jnp.mean(summed, -1, keepdims=True)
+            spread = jnp.mean(center * center, -1, keepdims=True)
+            inverse = lax.rsqrt(spread + EPS)
+            normed = center * inverse
+            norm_s[rows] = normed
+            column_s[0, rows] = inverse
+            x_s[rows] = normed * gain_ref[...] + shift_ref[...]
+
+    outs = (
+        pltpu.make_async_copy(x_s, x_ref, local.at[1]),
+        pltpu.make_async_copy(norm_s, norm_ref, local.at[2]),
+        pltpu.make_async_copy(column_s, column_ref, local.at[3]),
+    )
+    ids_copy = pltpu.make_async_copy(ids_all, ids_out, local.at[4])
+    ids_copy.start()
+
+    @pl.when(layer == 0)
+    def _():
+        for copy in outs:
+            copy.start()
+
+    @pl.when(layer == 1)
+    def _():
+        other_move.wait_send()
+        for r in range(2):
+
+            @pl.when(section + r < 4)
+            def _():
+                remote(
+                    cot_ref, given_ref.at[pl.ds(r * quarter, quarter)], c_send, c_recv.at[r],
+                    (me, section - 1),
+                ).wait_recv()
+
+    @pl.when(section != 0)
+    def _():
+        words_move.wait_send()
+
+    @pl.when(section != 3)
+    def _():
+        given_move.wait_send()
+
+    @pl.when(section == 3)
+    def _():
+        given_keep.wait()
+
+    loop(1, n_dp, lambda step: ids_move(step).wait_send())
+    loop(1, n_dp, lambda step: slots_move(step).wait_send())
+    ids_copy.wait()
+
+    @pl.when(layer == 0)
+    def _():
+        for copy in outs:
+            copy.wait()
+
+
+def front(words, cot, ids, listed, boxes, vocab, table, gain, shift):
+    quarter, width = words.shape
+    page = 2 * quarter
+    n_dp = lax.axis_size("dp")
+    slots = listed.shape[0]
+    held = vocab.shape[0]
+    side = width // 2
+    any_space = pl.BlockSpec(memory_space=pl.ANY)
+    in_vmem = pl.BlockSpec(memory_space=pltpu.VMEM)
+    dma = pltpu.SemaphoreType.DMA
+    vmem = pltpu.VMEM
+    return pl.pallas_call(
+        front_kernel,
+        out_shape=(
+            jax.ShapeDtypeStruct((page, width), F32),
+            jax.ShapeDtypeStruct((page, width), BF),
+            jax.ShapeDtypeStruct((page, width), F32),
+            jax.ShapeDtypeStruct((2, page, 1), F32),
+            jax.ShapeDtypeStruct((n_dp, 2, BLOCK), jnp.int32),
+        ),
+        in_specs=[in_vmem, any_space, in_vmem, in_vmem, in_vmem, any_space] + [in_vmem] * 3,
+        out_specs=(any_space,) * 5,
+        scratch_shapes=[
+            vmem((2, quarter, width), BF), vmem((n_dp, 2, BLOCK), jnp.int32),
+            vmem((held, side), BF), vmem((n_dp * slots, held), BF),
+            vmem((n_dp, slots, side), BF), vmem((n_dp, slots, side), BF),
+            vmem((2, slots, side), BF), vmem((BLOCK, BLOCK), F32),
+            vmem((page, width), F32), vmem((page, width), F32), vmem((2, page, 1), F32),
+            dma, dma((2,)), dma, dma((2,)), dma((n_dp,)), dma((n_dp,)),
+            dma((n_dp,)), dma((n_dp,)), dma, dma, dma((5,)),
+        ],
+        compiler_params=pltpu.CompilerParams(
+            collective_id=2, has_side_effects=True, vmem_limit_bytes=60 << 20
+        ),
+        name="embedded_rows",
+    )(words, cot, ids, listed, boxes, vocab, table, gain, shift)
+
+
+def finish_kernel(
+    pieces, q_in, o_in, u_in, d_in, rows_in, ids_ref, small_ref, table_ref, act_in, ing_in,
+    act_ref, ing_ref, tab_ref, voc_ref, q_ref, qvb_ref, o_ref, u_ref, upb_ref, d_ref, own_ref,
+    q_s, o_s, u_s, d_s, q_f, o_f, u_f, d_f, rows_s, in_sem, out_sem, rows_sem,
+):
+    section = lax.axis_index("section")
+    layer = section // 2
+    half = section % 2
+    side = rows_s.shape[3]
+    n_dp = rows_s.shape[1]
+    rows_copy = pltpu.make_async_copy(rows_in, rows_s, rows_sem)
+    rows_copy.start()
+    moves = []
+    for source, low, wide, target in (
+        (d_in, d_s, d_f, d_ref), (u_in, u_s, u_f, u_ref), (q_in, q_s, q_f, q_ref),
+        (o_in, o_s, o_f, o_ref),
+    ):
+        count = low.shape[0] // pieces
+        for i in range(pieces):
+            rows = pl.ds(i * count, count)
+            moves.append((source.at[rows], low.at[rows], wide.at[rows], target.at[0, rows]))
+    for i, (source, low, wide, target) in enumerate(moves):
+        pltpu.make_async_copy(source, low, in_sem.at[i]).start()
+
+    act_ref[...] = act_in[...].astype(F32)
+    ing_ref[...] = ing_in[...].astype(F32)
+
+    parts = small_ref[...].astype(F32)
+    partner = jnp.where(half == 0, parts[1], parts[3])
+    far_partner = jnp.where(half == 0, parts[3], parts[1])
+    splits = d_in.shape[0] // side
+    kept = 2 + splits
+    own = parts[0, :kept] + partner[kept : 2 * kept]
+    qvb_ref[0] = own[:2]
+    for i in range(splits):
+        upb_ref[0:1, pl.ds(i * side, side)] = own[2 + i : 3 + i]
+    here = (parts[0] + partner)[2 * kept : 2 * kept + 16]
+    there = (parts[2] + far_partner)[2 * kept : 2 * kept + 16]
+    own_ref[0] = jnp.where(layer == 0, here, there)
+    own_ref[1] = jnp.where(layer == 0, there, here)
+    for l in range(2):
+        for h in range(2):
+            tab_ref[h, :, pl.ds(l * side, side)] = table_ref[2 * l + h].astype(F32)
+
+    for i, (source, low, wide, target) in enumerate(moves):
+        pltpu.make_async_copy(source, low, in_sem.at[i]).wait()
+        wide[...] = low[...].astype(F32)
+        pltpu.make_async_copy(wide, target, out_sem.at[i]).start()
+
+    count = voc_ref.shape[0]
+    base = (lax.axis_index("dp") * lax.axis_size("section") + section) * count
+    rows_copy.wait()
+    at = base + lax.broadcasted_iota(jnp.int32, (count, BLOCK), 0)
+    for h in range(2):
+        list_at = jnp.where(half == 0, h, 1 - h)
+        for group in range(n_dp // 4):
+            spots = []
+            for origin in range(group * 4, group * 4 + 4):
+                row = ids_ref[origin]
+                row = jnp.where(list_at == 0, row[0:1], row[1:2])
+                spots.append((at == row).astype(F32).astype(BF))
+            spots = jnp.concatenate(spots, 1)
+            for l in range(2):
+                rows = rows_s[2 * h + l, group * 4 : group * 4 + 4].reshape(4 * BLOCK, side)
+                term = jnp.dot(spots, rows, preferred_element_type=F32)
+                columns = pl.ds(
+                    pl.multiple_of(jnp.where(layer == 0, l, 1 - l) * side, side), side
+                )
+                if h == 0 and group == 0:
+                    voc_ref[:, columns] = term
+                else:
+                    voc_ref[:, columns] += term
+
+    for i, (source, low, wide, target) in enumerate(moves):
+        pltpu.make_async_copy(wide, target, out_sem.at[i]).wait()
+
+
+def finished(sums, rows, ids, small, tables, act, ing, count, side):
+    any_space = pl.BlockSpec(memory_space=pl.ANY)
+    in_vmem = pl.BlockSpec(memory_space=pltpu.VMEM)
+    dma = pltpu.SemaphoreType.DMA
+    vmem = pltpu.VMEM
+    pieces = 6
+    width = act.shape[1]
+    units = sums[3].shape[0]
+    shapes = [array.shape for array in sums]
+    outs = [
+        jax.ShapeDtypeStruct(shape, F32)
+        for shape in (
+            act.shape, ing.shape, (2, tables.shape[1], width), (count, width), (1, *shapes[0]),
+            (1, 2, side), (1, *shapes[1]), (1, *shapes[2]), (1, units), (1, *shapes[3]),
+            (2, 16, side),
+        )
+    ]
+    specs = [in_vmem] * 4 + [any_space, in_vmem, any_space, any_space, in_vmem, any_space, in_vmem]
+    return pl.pallas_call(
+        functools.partial(finish_kernel, pieces),
+        out_shape=outs,
+        in_specs=[any_space] * 5 + [in_vmem] * 5,
+        out_specs=specs,
+        scratch_shapes=[vmem(shape, BF) for shape in shapes]
+        + [vmem(shape, F32) for shape in shapes]
+        + [vmem(rows.shape, BF), dma((4 * pieces,)), dma((4 * pieces,)), dma],
+        compiler_params=pltpu.CompilerParams(vmem_limit_bytes=60 << 20),
+        name="finished_outputs",
+    )(*sums, rows, ids, small, tables, act, ing)
 
 
 def on_device(
@@ -924,155 +1357,76 @@
     section = lax.axis_index("section")
     layer = section // 2
     half = section % 2
-    is_first = layer == 0
     quarter, width = word_embed.shape
     page = 2 * quarter
     side = qkv_weight.shape[2] // 3
-
-    words_a = routed(word_embed, [(1, 0), (2, 1)])
-    words_b = routed(word_embed, [(3, 1)])
-    given_a = routed(cotangent, [(0, 2), (2, 3)])
-    given_b = routed(cotangent, [(1, 2)])
-    words = jnp.concatenate(
-        [jnp.where(half == 0, word_embed, words_a), jnp.where(half == 0, words_a, words_b)], 0
-    )
-    given = jnp.concatenate(
-        [given_a, jnp.where(half == 0, given_b, cotangent)], 0
-    )
+    units = up_bias.shape[1]
 
     qvb = jnp.stack([qv_bias[0], swapped(qv_bias[0])])
     upb = jnp.concatenate([up_bias, swapped(up_bias)])
     gains = lax.dynamic_index_in_dim(layer_gains, layer, 0, keepdims=False)
     shifts = lax.dynamic_index_in_dim(layer_biases, layer, 0, keepdims=False)
-
-    listed = lax.dynamic_index_in_dim(mask_pos, half, 0, keepdims=False)
-    ids = lax.dynamic_index_in_dim(replace_ids, half, 0, keepdims=False)
-    slots = ids.shape[0]
-    rows_held = vocab_table.shape[0]
-    asked = lax.all_gather(ids, "dp", axis=0, tiled=True)
-    held = jnp.arange(rows_held, dtype=jnp.int32) + lax.axis_index("dp") * rows_held
-    picked = (asked[:, None] == held[None, :]).astype(BF)
-    slot_rows = lax.psum_scatter(
-        matmul(picked, vocab_table).astype(BF), "dp", scatter_dimension=0, tiled=True
+    slots = mask_pos.shape[1]
+    listed = lax.dynamic_index_in_dim(mask_pos, half, 0, keepdims=False)[:, None]
+    listed_wide = jnp.pad(listed, ((0, BLOCK - slots), (0, 0)), constant_values=-1)
+    ids = jnp.pad(replace_ids, ((0, 0), (0, BLOCK - slots)), constant_values=-1)
+    page_boxes = lax.dynamic_slice_in_dim(boxes, half * page, page, 1)
+
+    hidden_in, given, norm_in, columns, all_ids = front(
+        word_embed, cotangent, ids, listed, page_boxes, vocab_table, layout_table,
+        embed_gain[None], embed_shift[None],
     )
-
-    places = jnp.arange(page, dtype=jnp.int32)
-    chosen = (listed[:, None] == places[None, :]).astype(BF)
-    marked = jnp.any(listed[:, None] == places[None, :], axis=0)
-    replaced = matmul_left_t(chosen, slot_rows)
-    box_rows = lax.dynamic_slice_in_dim(boxes, half * page, page, 1)
-    coords = jnp.arange(layout_table.shape[1], dtype=jnp.int32)
-    one_x, one_y = (
-        (box_rows[a][:, None] == coords[None, :]).astype(BF)
-        + (box_rows[a + 2][:, None] == coords[None, :]).astype(BF)
-        for a in (0, 1)
+    left, right, edge, mine, small = layered(
+        hidden_in, given, norm_in, columns, (qkv_weight, out_weight, up_weight, down_weight),
+        qvb, upb, gains, shifts, embed_gain[None],
     )
-    summed = (
-        jnp.where(marked[:, None], replaced, words.astype(F32))
-        + matmul(one_x, layout_table[0])
-        + matmul(one_y, layout_table[1])
-    )
-    hidden_in, normed_in, inverse_in = normalize(summed, embed_gain, embed_shift)
-
-    left, right, output, grad_rows, sums_grad, qvb_grad, upb_grad = layered(
-        hidden_in, given, (qkv_weight, out_weight, up_weight, down_weight), qvb, upb, gains, shifts
-    )
-
-    grad_summed, eg_grad, es_grad = normalize_back(grad_rows, normed_in, inverse_in, embed_gain)
-    grad_low = jnp.where(is_first, grad_summed, 0.0).astype(BF)
-    word_grad = jnp.where(marked[:, None], 0.0, grad_low.astype(F32))
     left, right = (array.reshape(2 * page, -1) for array in (left, right))
-    hidden_units = up_bias.shape[1]
     counts = (
         (width // BLOCK, 3),
         (side // BLOCK, width // side),
-        (width // BLOCK, hidden_units // side),
-        (hidden_units // BLOCK, width // side),
+        (width // BLOCK, units // side),
+        (units // BLOCK, width // side),
     )
-    flat = jnp.concatenate(
-        [
-            qvb_grad[0].reshape(-1), upb_grad[0], qvb_grad[1].reshape(-1), upb_grad[1],
-            sums_grad.reshape(-1), eg_grad, es_grad,
-        ]
-    ).reshape(-1, side)
-    small_in = jnp.pad(flat, ((0, BLOCK - flat.shape[0]), (0, 0)))
-    edge = jnp.stack([grad_low[:, :side], grad_low[:, side:]])
     first, second = boxes[:, :page], boxes[:, page:]
     pair = jnp.stack([jnp.where(half == 0, first, second), jnp.where(half == 0, second, first)])
     pair = jnp.where(half == 0, pair[:, 0::2], pair[:, 1::2])
-    *sums, gathered, slot_rows_all, table_rows = reduced(
-        left, right, small_in, edge, pair, listed[:, None], counts, side
+    *sums, gathered, slot_rows, table_rows, act, ing = reduced(
+        left, right, small, edge, mine, pair, listed_wide, counts, side
     )
     outer = lax.axis_size("dp") // GROUP
+    table_part = None
     if outer > 1:
         groups = [[i + GROUP * g for g in range(outer)] for i in range(GROUP)]
         *sums, gathered = lax.psum((*sums, gathered), "dp", axis_index_groups=groups)
-        slot_rows_all = lax.all_gather(
-            slot_rows_all, "dp", axis_index_groups=groups, axis=1, tiled=True
-        )
-        table_grad = jnp.stack([matmul_left_t(one_x, grad_low), matmul_left_t(one_y, grad_low)])
+        slot_rows = lax.all_gather(slot_rows, "dp", axis_index_groups=groups, axis=1, tiled=True)
+        coords = jnp.arange(layout_table.shape[1], dtype=jnp.int32)
+        grad_low = jnp.concatenate([edge[0], edge[1]], 1)
+        grad_low = jnp.where(layer == 0, grad_low, jnp.zeros_like(grad_low))
+        table_grad = jnp.stack(
+            [
+                matmul_left_t(
+                    (page_boxes[a][:, None] == coords[None, :]).astype(BF)
+                    + (page_boxes[a + 2][:, None] == coords[None, :]).astype(BF),
+                    grad_low,
+                )
+                for a in (0, 1)
+            ]
+        )
         table_part = lax.psum_scatter(
             table_grad.astype(BF), ("dp", "section"), scatter_dimension=1, tiled=True
         ).astype(F32)
-    else:
-        table_part = (
-            table_rows.reshape(2, 2, -1, side).transpose(1, 2, 0, 3).reshape(2, -1, width)
-        ).astype(F32)
-    sums = [total.astype(F32)[None] for total in sums]
-
-    other_asked = swapped(asked)
-    count = rows_held // lax.axis_size("section")
-    base = (lax.axis_index("dp") * lax.axis_size("section") + section) * count
-    rows_here = jnp.arange(count, dtype=jnp.int32) + base
-    all_ids = jnp.concatenate([asked, other_asked])
-    ordered = slot_rows_all.reshape(2, 2, -1, side).transpose(0, 2, 1, 3)
-    ordered = ordered.reshape(-1, width)
-    found = matmul((rows_here[:, None] == all_ids[None, :]).astype(BF), ordered)
-    vocab_part = jnp.where(
-        is_first, found, jnp.concatenate([found[:, side:], found[:, :side]], 1)
+    count = vocab_table.shape[0] // lax.axis_size("section")
+    act, ing, tables, vocab_part, q_sum, qvb_sum, o_sum, u_sum, upb_sum, d_sum, rest = finished(
+        sums, slot_rows, all_ids, gathered, table_rows, act, ing, count, side
     )
-
-    parts = gathered.astype(F32)[:, : flat.shape[0]].reshape(4, -1)
-    partner = parts[jnp.where(half == 0, 1, 3)]
-    far_partner = parts[jnp.where(half == 0, 3, 1)]
-    edge_at = 2 * side + hidden_units
-    own = parts[0, :edge_at] + partner[edge_at : 2 * edge_at]
-    in_order = jnp.stack([parts[0] + partner, parts[2] + far_partner])[:, 2 * edge_at :]
-    by_layer = jnp.where(layer == 0, in_order, in_order[::-1])
-    small = (
-        by_layer[:, : 2 * width].reshape(2, 2, width),
-        by_layer[:, 2 * width : 6 * width].reshape(2, 4, width),
-        by_layer[0, 6 * width : 7 * width],
-        by_layer[0, 7 * width :],
-        own[: 2 * side].reshape(1, 2, side),
-        own[2 * side :].reshape(1, hidden_units),
-    )
-
-    out_first = output[:quarter].astype(BF)
-    out_second = output[quarter:].astype(BF)
-    act_a = routed(out_first, [(2, 0), (3, 2)])
-    act_b = routed(out_second, [(2, 1)])
-    grad_first = word_grad[:quarter].astype(BF)
-    grad_second = word_grad[quarter:].astype(BF)
-    ing_a = routed(grad_second, [(0, 1), (1, 3)])
-    ing_b = routed(grad_first, [(1, 2)])
-    activations = jnp.where(
-        section == 3,
-        output[quarter:],
-        jnp.where(section == 1, act_b, act_a).astype(F32),
-    )
-    input_grad = jnp.where(
-        section == 0,
-        word_grad[:quarter],
-        jnp.where(section == 2, ing_b, ing_a).astype(F32),
-    )
+    if table_part is None:
+        table_part = tables
+    gains_sum = rest[:, :4].reshape(2, 2, width)
+    shifts_sum = rest[:, 4:12].reshape(2, 4, width)
     return (
-        activations, input_grad, table_part, vocab_part, small[2], small[3],
-        sums[0],
-        small[4],
-        sums[1], sums[2],
-        small[5],
-        sums[3], small[0], small[1],
+        act, ing, table_part, vocab_part, rest[0, 12:14].reshape(width),
+        rest[0, 14:16].reshape(width), q_sum, qvb_sum, o_sum, u_sum, upb_sum, d_sum, gains_sum,
+        shifts_sum,
     )
 
 

time: 448 us -> 346 us (0.77); the launches traced: 442 us -> 345 us
  waiting for transfers between devices: 50.2 us -> 0.01 us
  Pallas kernels: 282 us -> 328 us
  other arithmetic: 27.1 us -> 3.19 us
  starting transfers between devices: 20.2 us -> 0.6 us
  matrix products: 16 us -> 0 us
  between operations: 15.8 us -> 0.72 us
  blocking collectives: 12.2 us -> 0 us
  local copies, waits for them, and re-layouts: 17.8 us -> 11.9 us
    reduce_scatter x1 -> x0, waiting for transfers between devices: 49.1 us -> none  [on_device(): lax.psum_scatter(matmul(picked, vocab_table).astype(BF), 'dp', scatter_di...]
    pallas_call x0 -> x2, Pallas kernels: none -> 46.1 us  [the longest x1 31.6 us: front(): pl.pallas_call(front_kernel, out_shape=(jax.ShapeDtypeStruct((page, width...]
    ppermute x11 -> x2, starting transfers between devices: 20.1 us -> 0.6 us  [routed(): return lax.ppermute(block, 'section', route)]
    dot_general x5 -> x0, matrix products: 16 us -> none  [the longest x4 13.4 us: matmul(): return jnp.dot(left, right, preferred_element_type=F32)]
    all_gather x1 -> x0, blocking collectives: 12.2 us -> none  [on_device(): asked = lax.all_gather(ids, 'dp', axis=0, tiled=True)]
    broadcast_in_dim x4 -> x0, other arithmetic: 9.54 us -> none  [on_device(): sums = [total.astype(F32)[None] for total in sums]]
    select_n x7 -> x0, other arithmetic: 8.62 us -> none  [the longest x1 3.13 us: on_device(): word_grad = jnp.where(marked[:, None], 0.0, grad_low.astype(F32))]
    unnamed x63 -> x8, local copies, waits for them, and re-layouts: 5.44 us -> 0.02 us
  transfers between devices with their start and end apart: 12 -> 2, of which waited for: 3 -> 0; matrix products, arithmetic and copies ran while one was open for 9% -> 3% of each run, Pallas kernels for 0% -> 9%
where the time goes in v3:
time: 346 us; the launch traced here: 345 us
  Pallas kernels  328 us (95%)
  local copies, waits for them, and re-layouts  11.9 us (3%)
    pallas_call x1, Pallas kernels, reduced(): pl.pallas_call(functools.partial(reduce_kernel, counts), out_shape=tuple(...  164 us
    pallas_call x1, Pallas kernels, layered(): pl.pallas_call(layer_kernel, out_shape=(jax.ShapeDtypeStruct((2, page, 2...  118 us
    pallas_call x1, Pallas kernels, front(): pl.pallas_call(front_kernel, out_shape=(jax.ShapeDtypeStruct((page, width...  31.6 us
    pallas_call x1, Pallas kernels, finished(): pl.pallas_call(functools.partial(finish_kernel, pieces), out_shape=outs,...  14.5 us
  transfers between devices with their start and end apart: 2, of which 0 were waited for; matrix products, arithmetic and copies ran while one was open for 3% of the time, Pallas kernels for 9%

profile of v3, /device:TPU:0, one launch (start us, length us, event | category | flops | bytes accessed | tf_op | source)
XLA Modules:
  0.0 344.6 jit_solution(7834740369112783471)
XLA Ops:
  0.6 0.0 copy-start
  0.7 0.5 collective-permute-start
  1.2 0.1 collective-permute-start.1
  1.3 1.4 select_bitcast_fusion.1
  2.7 1.3 dynamic-slice_bitcast_fusion.1.gains_ref
  4.0 0.0 copy-done
  4.0 0.6 dynamic-slice_bitcast_fusion.shifts_ref
  4.6 0.6 broadcast_select_fusion.box_ref
  5.2 0.7 fusion
  5.9 1.2 pad.8.ids_ref
  7.1 1.3 broadcast_in_dim.11.gain_ref.first_gain_ref
  8.4 1.3 broadcast_in_dim.12.shift_ref
  9.7 0.1 copy.31.listed_ref
  9.8 0.0 copy-start.1
  9.8 0.6 pad.9.listed_ref
  10.4 0.0 copy-done.1
  10.4 0.0 copy-start.3
  10.4 0.0 copy-start.2
  10.4 31.6 %embedded_rows.1 = (f32[512,768]{1,0:T(8,128)}, bf16[512,768]{1,0:T(8,128)(2,1)}, f32[512,768]{1,0:T(8,128)}, f32[2,512,1]{2,1,0:T(8,128)}, s32[8,2,128]{2,1,0:T(2,128)}) custom-call(bf16[256,768]{1,0:T(8,128)(2,1)} %words_ref.1, bf16[256,768]{1,0:T(8,128)(2,1)} %cot_ref.1, s32[2,128]{1,0:T(2,128)} %pad.8.ids_ref, s32[96,1]{1,0:T(8,128)} %copy-done.1, ...), custom_call_target="tpu_custom_call" | custom-call | tf_op jit(solution)/shard_map/embedded_rows/pallas_call | solution.py:1217
  42.0 0.0 collective-permute-done
  42.0 0.0 copy-done.3
  42.1 0.6 pad_maximum_fusion.1.qvb_ref
  42.6 0.0 collective-permute-done.1
  42.7 0.0 copy-done.2
  42.7 0.6 pad_maximum_fusion.upb_ref
  43.3 117.6 %layer_both_ways.1 = (bf16[2,512,3456]{2,1,0:T(8,128)(2,1)}, bf16[2,512,4224]{2,1,0:T(8,128)(2,1)}, bf16[2,512,384]{2,1,0:T(8,128)(2,1)}, bf16[512,768]{1,0:T(8,128)(2,1)}, f32[128,384]{1,0:T(8,128)}) custom-call(f32[512,768]{1,0:T(8,128)} %get-tuple-element.44.x_ref, bf16[512,768]{1,0:T(8,128)(2,1)} %get-tuple-element.45.given_ref, ...), custom_call_target="tpu_custom_call" | custom-call | flops 57982058496 | bytes 209715200 | tf_op jit(solution)/shard_map/layer_both_ways/pallas_call | solution.py:944
  160.9 164.4 %gradient_sums.1 = (bf16[768,1152]{1,0:T(8,128)(2,1)}, bf16[384,768]{1,0:T(8,128)(2,1)}, bf16[768,1536]{1,0:T(8,128)(2,1)}, bf16[1536,768]{1,0:T(8,128)(2,1)}, b...) custom-call(bf16[1024,3456]{1,0:T(8,128)(2,1)} %bitcast.17, ...), custom_call_target="tpu_custom_call" | custom-call | flops 7348420608 | bytes 419430400 | tf_op jit(solution)/shard_map/gradient_sums/pallas_call | solution.py:512
  325.3 14.5 %finished_outputs.1 = (f32[256,768]{1,0:T(8,128)}, f32[256,768]{1,0:T(8,128)}, f32[2,32,768]{2,1,0:T(8,128)}, f32[512,768]{1,0:T(8,128)}, f32[1,768,1152]{2,1,0:...) custom-call(bf16[768,1152]{1,0:T(8,128)(2,1)} %get-tuple-element.53., ...), custom_call_target="tpu_custom_call" | custom-call | tf_op jit(solution)/shard_map/finished_outputs/pallas_call | solution.py:1339
  339.8 0.8 fusion.1
  340.6 0.7 slice.30
  341.4 0.8 slice.31
  342.2 0.6 reshape_squeeze.7
  342.8 0.6 reshape_squeeze.6
  343.4 0.6 reshape.44
  344.0 0.6 reshape.43
  (3 shorter events, 0.1 us)
Async XLA Ops:
  0.6 3.3 copy-start
  0.7 41.4 %collective-permute-start = (f32[2,384]{1,0:T(2,128)}, f32[2,384]{1,0:T(2,128)S(1)}, u32[]{:S(2)}, u32[]{:S(2)}) collective-permute-start(f32[2,384]{1,0:T(2,128)} %bitcast.14), channel_id=1, source_target_pairs={{0,1},{1,0},{2,3},{3,2},{4,5},{5,4},{6,7},{7,6},{8,9},{9,8},{10,11... | collective-permute-start | bytes 9224 | tf_op jit(solution)/shard_map/ppermute | solution.py:19
  1.2 41.5 %collective-permute-start.1 = (f32[1,1536]{1,0:T(1,128)}, f32[1,1536]{1,0:T(1,128)S(1)}, u32[]{:S(2)}, u32[]{:S(2)}) collective-permute-start(f32[1,1536]{1,0:T(1,128)} %param.30), channel_id=1, source_target_pairs={{0,1},{1,0},{2,3},{3,2},{4,5},{5,4},{6,7},{7,6},{8,9},{9,8},{10,11... | collective-permute-start | bytes 18440 | tf_op jit(solution)/shard_map/ppermute | solution.py:19
  9.8 0.6 copy-start.1
  10.4 31.6 %copy-start.3 = (f32[1,2,384]{2,1,0:T(2,128)S(1)}, f32[1,2,384]{2,1,0:T(2,128)}, u32[]{:S(2)}) copy-start(f32[1,2,384]{2,1,0:T(2,128)} %param.27) | copy-start | bytes 9220
  10.4 32.2 %copy-start.2 = (f32[1,1536]{1,0:T(1,128)S(1)}, f32[1,1536]{1,0:T(1,128)}, u32[]{:S(2)}) copy-start(f32[1,1536]{1,0:T(1,128)} %param.30) | copy-start | bytes 18436

commit v4 on v3

--- a/solution.py
+++ b/solution.py
@@ -15,17 +15,6 @@
 F32 = jnp.float32
 
 
-def routed(block, route):
-    return lax.ppermute(block, "section", route)
-
-
-SWAP = [(0, 1), (1, 0), (2, 3), (3, 2)]
-
-
-def swapped(block):
-    return routed(block, SWAP)
-
-
 def matmul_left_t(left, right):
     return jnp.einsum("pa,pb->ab", left, right, preferred_element_type=F32)
 
@@ -57,7 +46,7 @@
 def reduce_kernel(
     counts, a_in, b_in, small_ref, edge_ref, mine_ref, box_ref, listed_ref,
     q_ref, o_ref, u_ref, d_ref, gathered_ref, rows_ref, table_ref, act_ref, ing_ref,
-    a_ref, b_ref, buf, total, gathered, edge, rows, table, piece,
+    a_ref, b_ref, square, buf, total, gathered, edge, rows, table, piece,
     send, recv, out_sem, g_send, g_recv, e_send, e_recv, r_send, r_recv, t_send, t_recv,
     f_send, f_recv, m_send, m_recv, last_sem, in_sem,
 ):
@@ -369,9 +358,13 @@
         @pl.when((c >= 0) & (c < GROUP) & (depth == DEPTH + 1 - level))
         def _():
             at = c * BLOCK + lax.broadcasted_iota(jnp.int32, (BLOCK, edge.shape[1]), 0)
+            reach = edge.shape[1]
             for part in range(2):
-                spots = box_ref[part]
-                ones = (at == spots[0:1]).astype(F32) + (at == spots[1:2]).astype(F32)
+                start = pl.multiple_of((half if part == 0 else 1 - half) * reach, reach)
+                spots = box_ref[:, pl.ds(start, reach)]
+                low_at = jnp.where(half == 0, spots[0:1], spots[1:2])
+                high_at = jnp.where(half == 0, spots[2:3], spots[3:4])
+                ones = (at == low_at).astype(F32) + (at == high_at).astype(F32)
                 term = jnp.dot(ones.astype(BF), edge[part], preferred_element_type=F32)
                 if part == 0:
                     total[...] = term
@@ -438,7 +431,12 @@
         edge_beside(edge.at[0]).start()
 
     edge_beside(edge.at[0]).wait_recv()
-    wanted = listed_ref[...] == lax.broadcasted_iota(jnp.int32, (slots, edge.shape[1]), 1)
+    used = listed_ref.shape[1]
+    listed = listed_ref[...].astype(F32)
+    square[...] = jnp.full_like(square, -1.0)
+    square[0:1, :used] = jnp.where(half == 0, listed[0:1], listed[1:2])
+    column = square[...].T[:, 0:1]
+    wanted = column == lax.broadcasted_iota(jnp.int32, (slots, edge.shape[1]), 1).astype(F32)
     rows[0, place] = jnp.dot(
         wanted.astype(F32).astype(BF), edge[0], preferred_element_type=F32
     ).astype(BF)
@@ -503,7 +501,7 @@
     chunks = 1 + sum(count[0] * count[1] for count in counts)
     n_sections = lax.axis_size("section")
     kept = 32
-    slots = listed.shape[0]
+    slots = BLOCK
     page = edge.shape[1]
     any_space = pl.BlockSpec(memory_space=pl.ANY)
     in_vmem = pl.BlockSpec(memory_space=pltpu.VMEM)
@@ -526,6 +524,7 @@
         scratch_shapes=[
             pltpu.VMEM(a.shape, BF),
             pltpu.VMEM(b.shape, BF),
+            pltpu.VMEM((BLOCK, BLOCK), F32),
             pltpu.VMEM((4, chunks, BLOCK, side), BF),
             pltpu.VMEM((BLOCK, side), F32),
             pltpu.VMEM((n_sections, kept, side), BF),
@@ -555,33 +554,72 @@
 ROWS = 256
 
 
-def layer_kernel(
-    x_ref, given_ref, norm_ref, column_ref, q_own, o_own, u_own, d_own, qvb_ref, upb_ref,
-    gains_ref, shifts_ref, first_gain_ref,
-    a_ref, b_ref, edge_ref, mine_ref, small_ref, sums_ref, upb_sum,
+def encoder_kernel(
+    words_ref, cot_ref, ids_ref, mask_ref, box_ref, vocab_ref, table_ref, gain_ref, shift_ref,
+    q_own, o_own, u_own, d_own, qvb_own, upb_own, gains_ref, shifts_ref,
+    a_ref, b_ref, ids_out, edge_ref, mine_ref, small_ref,
+    words, ids_all, ids_wide, vocab, spots, picks, land, other, square, norm_in, facts,
+    sums_ref, upb_sum, qvb_ref, upb_ref,
     wq, wo, wu, wd, wide, x_land, g_land, x_low, ctx, d_ctx, h_low, act, slope, qkv, d_qkv,
-    da_low, df_low, probs, n_one, n_two, r_one, r_two, z, sent_low, columns,
-    w_local, w_send, w_recv, x_send, x_recv, g_send, g_recv, p_local, p_send, p_recv, io_sem,
+    da_low, df_low, probs, n_one, n_two, r_one, r_two, z, sent_low,
+    o_w_send, o_w_recv, c_send, c_recv, i_send, i_recv, s_send, s_recv, o_send, o_recv, local,
+    w_local, w_send, w_recv, x_send, x_recv, g_send, g_recv, p_local, p_send, p_recv,
 ):
     me = lax.axis_index("dp")
     section = lax.axis_index("section")
     n_sections = lax.axis_size("section")
+    n_dp = ids_all.shape[0]
     layer = section // 2
     half = section % 2
-    beside = (me, section + 1 - 2 * half)
-    across = (me, (section + 2) % n_sections)
     mesh_id = pl.DeviceIdType.MESH
+    quarter = words_ref.shape[0]
     page, width = x_low.shape
-    side = ctx.shape[2]
     units = act.shape[2]
     blocks = page // ROWS
     tile = 512
     scale = HEAD_DIM ** (-0.5)
+    beside = (me, section + 1 - 2 * half)
+    across = (me, (section + 2) % n_sections)
+    slots = picks.shape[1]
+    side = picks.shape[2]
+    held = vocab.shape[0]
+
+    vocab_copy = pltpu.make_async_copy(
+        vocab_ref.at[:, pl.ds(pl.multiple_of(layer * side, side), side)], vocab, local.at[0]
+    )
+    vocab_copy.start()
+    table_copies = [
+        pltpu.make_async_copy(
+            table_ref.at[kind, pl.ds(part * page, page)],
+            act.at[kind, :, pl.ds(part * width, width)],
+            local.at[2 + 2 * kind + part],
+        )
+        for kind in range(2)
+        for part in range(2)
+    ]
+
+    @pl.when(layer == 0)
+    def _():
+        for copy in table_copies:
+            copy.start()
+
+    ids_wide[...] = jnp.full_like(ids_wide, -1)
+    ids_wide[:, :slots] = ids_ref[...]
 
     barrier = pltpu.get_barrier_semaphore()
-    for device in (beside, across):
-        pl.semaphore_signal(barrier, inc=1, device_id=device, device_id_type=mesh_id)
-    pl.semaphore_wait(barrier, 2)
+
+    def greet(step, carry):
+        pl.semaphore_signal(
+            barrier, inc=1, device_id=((me + step) % n_dp, section), device_id_type=mesh_id
+        )
+        return carry
+
+    lax.fori_loop(1, n_dp, greet, 0)
+    for step in range(1, n_sections):
+        pl.semaphore_signal(
+            barrier, inc=1, device_id=(me, (section + step) % n_sections), device_id_type=mesh_id
+        )
+    pl.semaphore_wait(barrier, n_dp - 1 + n_sections - 1)
 
     def remote(source, target, sent, got, device):
         return pltpu.make_async_remote_copy(
@@ -590,8 +628,8 @@
         )
 
     def weight_copies(i):
-        source = (q_own, o_own, u_own, d_own)[i].at[0]
-        target = (wq, wo, wu, wd)[i]
+        source = (q_own, o_own, u_own, d_own, qvb_own, upb_own)[i].at[0]
+        target = (wq, wo, wu, wd, qvb_ref, upb_ref)[i]
         return (
             pltpu.make_async_copy(source, target.at[0], w_local.at[i]),
             remote(source, target.at[1], w_send.at[i], w_recv.at[i], beside),
@@ -602,21 +640,169 @@
         near.wait()
         far.wait_recv()
 
-    x_copy = pltpu.make_async_copy(x_ref, wide, io_sem.at[0])
-    given_copy = pltpu.make_async_copy(given_ref, g_land, io_sem.at[1])
-
-    @pl.when(layer == 0)
-    def _():
-        x_copy.start()
-
-    @pl.when(layer == 1)
-    def _():
-        given_copy.start()
-
-    for i in range(4):
+    def ids_move(step):
+        return remote(
+            ids_wide, ids_all.at[me], i_send.at[step], i_recv.at[me], ((me + step) % n_dp, section)
+        )
+
+    def ids_got(step):
+        source = (me + step) % n_dp
+        return remote(
+            ids_wide, ids_all.at[source], i_send.at[0], i_recv.at[source],
+            (me, (section + 1) % n_sections),
+        )
+
+    loop(1, n_dp, lambda step: ids_move(step).start())
+    ids_all[me] = ids_wide[...]
+
+    words_move = remote(
+        words_ref, words.at[half], o_w_send, o_w_recv.at[half], (me, layer)
+    )
+    given_part = g_land.at[pl.ds(pl.multiple_of(half * quarter, quarter), quarter)]
+    given_move = remote(cot_ref, given_part, c_send, c_recv.at[half], (me, 2 + layer))
+    given_keep = pltpu.make_async_copy(cot_ref, given_part, c_send)
+
+    @pl.when(section != 0)
+    def _():
+        words_move.start()
+
+    @pl.when(section == 0)
+    def _():
+        words[0] = words_ref[...]
+
+    @pl.when(section != 3)
+    def _():
+        given_move.start()
+
+    @pl.when(section == 3)
+    def _():
+        given_keep.start()
+
+    for i in (0, 4, 5, 1, 2, 3):
         near, far = weight_copies(i)
         far.start()
         near.start()
+
+    loop(1, n_dp, lambda step: ids_got(step).wait_recv())
+    lists = ids_all[...].astype(F32)
+    lists = jnp.where(half == 0, lists[:, 0], lists[:, 1])
+    square[...] = jnp.zeros_like(square)
+    square[0:n_dp] = lists
+    listed = mask_ref[...].astype(F32)
+    square[n_dp : n_dp + 1, :slots] = jnp.where(half == 0, listed[0:1], listed[1:2])
+    turned = square[...].T
+    at = (me * held + lax.broadcasted_iota(jnp.int32, (slots, held), 1)).astype(F32)
+    for origin in range(n_dp):
+        spots[origin * slots : (origin + 1) * slots] = (
+            at == turned[:slots, origin : origin + 1]
+        ).astype(F32).astype(BF)
+    vocab_copy.wait()
+    found = jnp.dot(spots[...], vocab[...], preferred_element_type=F32).astype(BF)
+    for origin in range(n_dp):
+        picks[origin] = found[origin * slots : (origin + 1) * slots]
+
+    def slots_move(step):
+        to = (me + step) % n_dp
+        return remote(
+            picks.at[to], land.at[me], s_send.at[step], s_recv.at[me], (to, section)
+        )
+
+    def slots_got(step):
+        source = (me + step) % n_dp
+        return remote(
+            picks.at[0], land.at[source], s_send.at[0], s_recv.at[source],
+            (me, (section + 1) % n_sections),
+        )
+
+    loop(1, n_dp, lambda step: slots_move(step).start())
+    land[me] = picks[me]
+
+    @pl.when(layer == 0)
+    def _():
+        for copy in table_copies:
+            copy.wait()
+        coords = lax.broadcasted_iota(jnp.int32, (page, page), 0)
+        for kind in range(2):
+            low_at, high_at = (
+                box_ref[i : i + 1, pl.ds(pl.multiple_of(half * page, page), page)]
+                for i in (kind, kind + 2)
+            )
+            for part in range(2):
+                at = coords + part * page
+                ones = (at == low_at).astype(F32) + (at == high_at).astype(F32)
+                term = lax.dot_general(
+                    ones.astype(BF), act[kind, :, pl.ds(part * width, width)],
+                    (((0,), (0,)), ((), ())), preferred_element_type=F32,
+                )
+                if kind + part == 0:
+                    wide[...] = term
+                else:
+                    wide[...] += term
+
+    loop(1, n_dp, lambda step: slots_got(step).wait_recv())
+    mine = land[0]
+    for origin in range(1, n_dp):
+        mine = mine + land[origin]
+    other[1] = mine
+    other_move = remote(other.at[1], other.at[0], o_send, o_recv, (me, half))
+
+    @pl.when(layer == 1)
+    def _():
+        other_move.start()
+
+    @pl.when(layer == 0)
+    def _():
+        for r in range(2):
+
+            @pl.when(section + r > 0)
+            def _():
+                remote(
+                    words_ref, words.at[r], o_w_send, o_w_recv.at[r], (me, section + 1)
+                ).wait_recv()
+
+        places = lax.broadcasted_iota(jnp.int32, (slots, page), 1).astype(F32)
+        chosen = (turned[:slots, n_dp : n_dp + 1] == places).astype(F32).astype(BF)
+
+        def spread_out(right):
+            return lax.dot_general(
+                chosen, right, (((0,), (0,)), ((), ())), preferred_element_type=F32
+            )
+
+        marked = spread_out(jnp.ones((slots, BLOCK), BF))[:, 0:1]
+        facts[1] = 1.0 - marked
+        other_move.wait_recv()
+        for part, values in ((0, other[1]), (1, other[0])):
+            columns = pl.ds(part * side, side)
+            wide[:, columns] += spread_out(values)
+        for r in range(2):
+            rows = pl.ds(r * quarter, quarter)
+            kept = facts[1, rows]
+            summed = wide[rows] + words[r].astype(F32) * kept
+            center = summed - jnp.mean(summed, -1, keepdims=True)
+            spread = jnp.mean(center * center, -1, keepdims=True)
+            inverse = lax.rsqrt(spread + EPS)
+            normed = center * inverse
+            norm_in[rows] = normed
+            facts[0, rows] = inverse
+            wide[rows] = normed * gain_ref[...][None] + shift_ref[...][None]
+
+    ids_copy = pltpu.make_async_copy(ids_all, ids_out, local.at[1])
+    ids_copy.start()
+
+    @pl.when(layer == 1)
+    def _():
+        for r in range(2):
+
+            @pl.when(section + r < 4)
+            def _():
+                remote(
+                    cot_ref, g_land.at[pl.ds(r * quarter, quarter)], c_send, c_recv.at[r],
+                    (me, section - 1),
+                ).wait_recv()
+
+    @pl.when(section == 3)
+    def _():
+        given_keep.wait()
 
     def rows_of(block):
         return pl.ds(pl.multiple_of(block * ROWS, ROWS), ROWS)
@@ -691,11 +877,8 @@
     sums_ref[...] = jnp.zeros_like(sums_ref)
     upb_sum[...] = jnp.zeros_like(upb_sum)
 
-    weights_here(0)
-
-    @pl.when(layer == 0)
-    def _():
-        x_copy.wait()
+    for i in (0, 4, 5):
+        weights_here(i)
 
     def project(block):
         rows = rows_of(block)
@@ -753,12 +936,12 @@
         attended = (
             jnp.dot(ctx[0, rows], wo[0], preferred_element_type=F32)
             + jnp.dot(ctx[1, rows], wo[1], preferred_element_type=F32)
-            + shifts_ref[0:1]
+            + shifts_ref[layer, 0:1]
         )
         normed, inverse = centred(wide[rows] + attended)
         n_one[rows] = normed
         r_one[rows] = inverse
-        hidden = normed * gains_ref[0:1] + shifts_ref[1:2]
+        hidden = normed * gains_ref[layer, 0:1] + shifts_ref[layer, 1:2]
         z[rows] = hidden
         h_low[rows] = hidden.astype(BF)
         for slot in range(2):
@@ -766,7 +949,7 @@
                 part = pl.ds(c * tile, tile)
                 upper = (
                     jnp.dot(h_low[rows], wu[slot, :, part], preferred_element_type=F32)
-                    + upb_ref[slot : slot + 1, part]
+                    + upb_ref[slot, :, part]
                 )
                 below = 0.5 * (1.0 + lax.erf(upper * ROOT_HALF))
                 act[slot, rows, part] = (upper * below).astype(BF)
@@ -776,12 +959,12 @@
         mixed = (
             jnp.dot(act[0, rows], wd[0], preferred_element_type=F32)
             + jnp.dot(act[1, rows], wd[1], preferred_element_type=F32)
-            + shifts_ref[2:3]
+            + shifts_ref[layer, 2:3]
         )
         normed, inverse = centred(z[rows] + mixed)
         n_two[rows] = normed
         r_two[rows] = inverse
-        output = normed * gains_ref[1:2] + shifts_ref[3:4]
+        output = normed * gains_ref[layer, 1:2] + shifts_ref[layer, 3:4]
         sent_low[rows] = output.astype(BF)
 
         @pl.when(layer == 0)
@@ -794,10 +977,6 @@
 
     loop(0, blocks, feed)
     hand_out(2, 3)
-
-    @pl.when(layer == 1)
-    def _():
-        given_copy.wait()
 
     def feed_back(block):
         rows = rows_of(block)
@@ -810,7 +989,7 @@
         normed = n_two[rows]
         add_sum(1, grad * normed)
         add_sum(5, grad)
-        grad = pulled(grad, normed, r_two[rows], gains_ref[1:2])
+        grad = pulled(grad, normed, r_two[rows], gains_ref[layer, 1:2])
         z[rows] = grad
         low = grad.astype(BF)
         df_low[rows] = low
@@ -826,7 +1005,7 @@
         normed = n_one[rows]
         add_sum(0, grad * normed)
         add_sum(3, grad)
-        grad = pulled(grad, normed, r_one[rows], gains_ref[0:1])
+        grad = pulled(grad, normed, r_one[rows], gains_ref[layer, 0:1])
         z[rows] = grad
         low = grad.astype(BF)
         da_low[rows] = low
@@ -836,13 +1015,6 @@
 
     loop(0, blocks, feed_back)
     hand_out(5, 6, 7)
-    norm_copy = pltpu.make_async_copy(norm_ref, n_two, io_sem.at[2])
-    column_copy = pltpu.make_async_copy(column_ref, columns, io_sem.at[3])
-
-    @pl.when(layer == 0)
-    def _():
-        norm_copy.start()
-        column_copy.start()
 
     def attend_back(i):
         slot = i // pairs
@@ -868,11 +1040,6 @@
     loop(0, 2 * pairs, attend_back)
     hand_out(4)
 
-    @pl.when(layer == 0)
-    def _():
-        norm_copy.wait()
-        column_copy.wait()
-
     def leave(block):
         rows = rows_of(block)
         grad = z[rows] + nt(d_qkv[0, rows], wq[0]) + nt(d_qkv[1, rows], wq[1])
@@ -886,13 +1053,13 @@
         @pl.when(layer == 0)
         def _():
             grad = z[rows]
-            normed = n_two[rows]
+            normed = norm_in[rows]
             add_sum(6, grad * normed)
             add_sum(7, grad)
-            low = pulled(grad, normed, columns[0, rows], first_gain_ref[...]).astype(BF)
+            low = pulled(grad, normed, facts[0, rows], gain_ref[...][None]).astype(BF)
             edge_ref[0, rows] = low[:, :side]
             edge_ref[1, rows] = low[:, side:]
-            mine_ref[rows] = (low.astype(F32) * columns[1, rows]).astype(BF)
+            mine_ref[rows] = (low.astype(F32) * facts[1, rows]).astype(BF)
 
     loop(0, blocks, leave)
     small_ref[...] = jnp.zeros_like(small_ref)
@@ -921,7 +1088,7 @@
         def _():
             g_move(block).wait_send()
 
-    for i in range(4):
+    for i in range(6):
         weight_copies(i)[1].wait_send()
     for i in range(8):
         near, far = piece_copies(i)
@@ -929,31 +1096,62 @@
         far.wait()
 
 
-def layered(x, given, norm, columns, weights, qvb, upb, gains, shifts, first_gain):
-    page, width = x.shape
-    qkv_weight, out_weight, up_weight, down_weight = weights
-    side = out_weight.shape[1]
-    units = down_weight.shape[1]
+    @pl.when(layer == 1)
+    def _():
+        other_move.wait_send()
+
+    @pl.when(section != 0)
+    def _():
+        words_move.wait_send()
+
+    @pl.when(section != 3)
+    def _():
+        given_move.wait_send()
+
+    loop(1, n_dp, lambda step: ids_move(step).wait_send())
+    loop(1, n_dp, lambda step: slots_move(step).wait_send())
+    ids_copy.wait()
+
+
+def encoded(
+    words, cot, ids, mask, boxes, vocab, table, gain, shift, weights, qvb, upb, gains, shifts
+):
+    quarter, width = words.shape
+    page = 2 * quarter
+    n_dp = lax.axis_size("dp")
+    slots = ids.shape[1]
+    held = vocab.shape[0]
+    side = width // 2
+    units = weights[3].shape[1]
     blocks = page // ROWS
-    heads = 2 * side // HEAD_DIM
+    heads = width // HEAD_DIM
     any_space = pl.BlockSpec(memory_space=pl.ANY)
     in_vmem = pl.BlockSpec(memory_space=pltpu.VMEM)
     dma = pltpu.SemaphoreType.DMA
     vmem = pltpu.VMEM
     flops = 8 * page * width * (4 * width + 4 * units) * 2
     return pl.pallas_call(
-        layer_kernel,
+        encoder_kernel,
         out_shape=(
             jax.ShapeDtypeStruct((2, page, 2 * width + side + units), BF),
             jax.ShapeDtypeStruct((2, page, 3 * side + 2 * width + units), BF),
+            jax.ShapeDtypeStruct((n_dp, 2, BLOCK), jnp.int32),
             jax.ShapeDtypeStruct((2, page, side), BF),
             jax.ShapeDtypeStruct((page, width), BF),
             jax.ShapeDtypeStruct((BLOCK, side), F32),
         ),
-        in_specs=[any_space] * 8 + [in_vmem] * 5,
-        out_specs=(any_space,) * 2 + (in_vmem,) * 3,
+        in_specs=[in_vmem, any_space] + [in_vmem] * 3 + [any_space] * 2 + [in_vmem] * 2
+        + [any_space] * 6 + [in_vmem] * 2,
+        out_specs=(any_space,) * 3 + (in_vmem,) * 3,
         scratch_shapes=[
+            vmem((2, quarter, width), BF), vmem((n_dp, 2, BLOCK), jnp.int32),
+            vmem((2, BLOCK), jnp.int32),
+            vmem((held, side), BF), vmem((n_dp * slots, held), BF),
+            vmem((n_dp, slots, side), BF), vmem((n_dp, slots, side), BF),
+            vmem((2, slots, side), BF), vmem((BLOCK, BLOCK), F32),
+            vmem((page, width), F32), vmem((2, page, 1), F32),
             vmem((8, width), F32), vmem((2, units), F32),
+            vmem((2, 2, side), F32), vmem((2, 1, units), F32),
             vmem((2, width, 3 * side), BF), vmem((2, side, width), BF),
             vmem((2, width, units), BF), vmem((2, units, width), BF),
             vmem((page, width), F32), vmem((page, width), BF), vmem((page, width), BF),
@@ -963,287 +1161,27 @@
             vmem((page, width), BF), vmem((page, width), BF), vmem((heads, page, page), BF),
             vmem((page, width), F32), vmem((page, width), F32),
             vmem((page, 1), F32), vmem((page, 1), F32),
-            vmem((page, width), F32), vmem((page, width), BF), vmem((2, page, 1), F32),
-            dma((4,)), dma((4,)), dma((4,)),
+            vmem((page, width), F32), vmem((page, width), BF),
+            dma, dma((2,)), dma, dma((2,)), dma((n_dp,)), dma((n_dp,)),
+            dma((n_dp,)), dma((n_dp,)), dma, dma, dma((6,)),
+            dma((6,)), dma((6,)), dma((6,)),
             dma((blocks,)), dma((blocks,)), dma((blocks,)), dma((blocks,)),
-            dma((8,)), dma((8,)), dma((8,)), dma((4,)),
+            dma((8,)), dma((8,)), dma((8,)),
         ],
         compiler_params=pltpu.CompilerParams(
-            collective_id=1, has_side_effects=True, vmem_limit_bytes=62 << 20
+            collective_id=1, has_side_effects=True, vmem_limit_bytes=63 << 20
         ),
         cost_estimate=pl.CostEstimate(
             flops=flops, bytes_accessed=200 << 20, transcendentals=0
         ),
-        name="layer_both_ways",
-    )(x, given, norm, columns, *weights, qvb, upb, gains, shifts, first_gain)
-
-
-def front_kernel(
-    words_ref, cot_ref, ids_ref, listed_ref, box_ref, vocab_ref, table_ref, gain_ref, shift_ref,
-    x_ref, given_ref, norm_ref, column_ref, ids_out,
-    words, ids_all, vocab, spots, picks, land, other, sum_scratch, x_s, norm_s, column_s,
-    w_send, w_recv, c_send, c_recv, i_send, i_recv, s_send, s_recv, o_send, o_recv, local,
-):
-    me = lax.axis_index("dp")
-    section = lax.axis_index("section")
-    n_sections = lax.axis_size("section")
-    n_dp = ids_all.shape[0]
-    layer = section // 2
-    half = section % 2
-    mesh_id = pl.DeviceIdType.MESH
-    quarter = words_ref.shape[0]
-    page, width = x_s.shape
-    slots = picks.shape[1]
-    side = picks.shape[2]
-    held = vocab.shape[0]
-
-    vocab_copy = pltpu.make_async_copy(
-        vocab_ref.at[:, pl.ds(pl.multiple_of(layer * side, side), side)], vocab, local.at[0]
-    )
-    vocab_copy.start()
-
-    barrier = pltpu.get_barrier_semaphore()
-
-    def greet(step, carry):
-        pl.semaphore_signal(
-            barrier, inc=1, device_id=((me + step) % n_dp, section), device_id_type=mesh_id
-        )
-        return carry
-
-    lax.fori_loop(1, n_dp, greet, 0)
-    for step in range(1, n_sections):
-        pl.semaphore_signal(
-            barrier, inc=1, device_id=(me, (section + step) % n_sections), device_id_type=mesh_id
-        )
-    pl.semaphore_wait(barrier, n_dp - 1 + n_sections - 1)
-
-    def remote(source, target, sent, got, device):
-        return pltpu.make_async_remote_copy(
-            src_ref=source, dst_ref=target, send_sem=sent, recv_sem=got, device_id=device,
-            device_id_type=mesh_id,
-        )
-
-    def ids_move(step):
-        return remote(
-            ids_ref, ids_all.at[me], i_send.at[step], i_recv.at[me], ((me + step) % n_dp, section)
-        )
-
-    def ids_got(step):
-        source = (me + step) % n_dp
-        return remote(
-            ids_ref, ids_all.at[source], i_send.at[0], i_recv.at[source],
-            (me, (section + 1) % n_sections),
-        )
-
-    loop(1, n_dp, lambda step: ids_move(step).start())
-    ids_all[me] = ids_ref[...]
-
-    words_move = remote(
-        words_ref, words.at[half], w_send, w_recv.at[half], (me, layer)
-    )
-    given_part = given_ref.at[pl.ds(pl.multiple_of(half * quarter, quarter), quarter)]
-    given_move = remote(cot_ref, given_part, c_send, c_recv.at[half], (me, 2 + layer))
-    given_keep = pltpu.make_async_copy(cot_ref, given_part, c_send)
-
-    @pl.when(section != 0)
-    def _():
-        words_move.start()
-
-    @pl.when(section == 0)
-    def _():
-        words[0] = words_ref[...]
-
-    @pl.when(section != 3)
-    def _():
-        given_move.start()
-
-    @pl.when(section == 3)
-    def _():
-        given_keep.start()
-
-    loop(1, n_dp, lambda step: ids_got(step).wait_recv())
-    lists = ids_all[...].astype(F32)
-    lists = jnp.where(half == 0, lists[:, 0], lists[:, 1])
-    sum_scratch[...] = jnp.zeros_like(sum_scratch)
-    sum_scratch[0:n_dp] = lists
-    across = sum_scratch[...].T
-    at = (me * held + lax.broadcasted_iota(jnp.int32, (slots, held), 1)).astype(F32)
-    for origin in range(n_dp):
-        spots[origin * slots : (origin + 1) * slots] = (
-            at == across[:slots, origin : origin + 1]
-        ).astype(F32).astype(BF)
-    vocab_copy.wait()
-    found = jnp.dot(spots[...], vocab[...], preferred_element_type=F32).astype(BF)
-    for origin in range(n_dp):
-        picks[origin] = found[origin * slots : (origin + 1) * slots]
-
-    def slots_move(step):
-        to = (me + step) % n_dp
-        return remote(
-            picks.at[to], land.at[me], s_send.at[step], s_recv.at[me], (to, section)
-        )
-
-    def slots_got(step):
-        source = (me + step) % n_dp
-        return remote(
-            picks.at[0], land.at[source], s_send.at[0], s_recv.at[source],
-            (me, (section + 1) % n_sections),
-        )
-
-    loop(1, n_dp, lambda step: slots_move(step).start())
-    land[me] = picks[me]
-
-    @pl.when(layer == 0)
-    def _():
-        coords = lax.broadcasted_iota(jnp.int32, (table_ref.shape[1], page), 0)
-        for kind in range(2):
-            ones = (coords == box_ref[kind : kind + 1]).astype(F32) + (
-                coords == box_ref[kind + 2 : kind + 3]
-            ).astype(F32)
-            term = lax.dot_general(
-                ones.astype(BF), table_ref[kind], (((0,), (0,)), ((), ())),
-                preferred_element_type=F32,
-            )
-            if kind == 0:
-                x_s[...] = term
-            else:
-                x_s[...] += term
-
-    loop(1, n_dp, lambda step: slots_got(step).wait_recv())
-    mine = land[0]
-    for origin in range(1, n_dp):
-        mine = mine + land[origin]
-    other[1] = mine
-    other_move = remote(other.at[1], other.at[0], o_send, o_recv, (me, half))
-
-    @pl.when(layer == 1)
-    def _():
-        other_move.start()
-
-    @pl.when(layer == 0)
-    def _():
-        for r in range(2):
-
-            @pl.when(section + r > 0)
-            def _():
-                remote(
-                    words_ref, words.at[r], w_send, w_recv.at[r], (me, section + 1)
-                ).wait_recv()
-
-        chosen = (listed_ref[...] == lax.broadcasted_iota(jnp.int32, (slots, page), 1))
-        chosen = chosen.astype(F32).astype(BF)
-
-        def tn(right):
-            return lax.dot_general(
-                chosen, right, (((0,), (0,)), ((), ())), preferred_element_type=F32
-            )
-
-        marked = tn(jnp.ones((slots, BLOCK), BF))[:, 0:1]
-        column_s[1] = 1.0 - marked
-        other_move.wait_recv()
-        for part, values in ((0, other[1]), (1, other[0])):
-            columns = pl.ds(part * side, side)
-            x_s[:, columns] += tn(values)
-        for r in range(2):
-            rows = pl.ds(r * quarter, quarter)
-            kept = column_s[1, rows]
-            summed = x_s[rows] + words[r].astype(F32) * kept
-            center = summed - jnp.mean(summed, -1, keepdims=True)
-            spread = jnp.mean(center * center, -1, keepdims=True)
-            inverse = lax.rsqrt(spread + EPS)
-            normed = center * inverse
-            norm_s[rows] = normed
-            column_s[0, rows] = inverse
-            x_s[rows] = normed * gain_ref[...] + shift_ref[...]
-
-    outs = (
-        pltpu.make_async_copy(x_s, x_ref, local.at[1]),
-        pltpu.make_async_copy(norm_s, norm_ref, local.at[2]),
-        pltpu.make_async_copy(column_s, column_ref, local.at[3]),
-    )
-    ids_copy = pltpu.make_async_copy(ids_all, ids_out, local.at[4])
-    ids_copy.start()
-
-    @pl.when(layer == 0)
-    def _():
-        for copy in outs:
-            copy.start()
-
-    @pl.when(layer == 1)
-    def _():
-        other_move.wait_send()
-        for r in range(2):
-
-            @pl.when(section + r < 4)
-            def _():
-                remote(
-                    cot_ref, given_ref.at[pl.ds(r * quarter, quarter)], c_send, c_recv.at[r],
-                    (me, section - 1),
-                ).wait_recv()
-
-    @pl.when(section != 0)
-    def _():
-        words_move.wait_send()
-
-    @pl.when(section != 3)
-    def _():
-        given_move.wait_send()
-
-    @pl.when(section == 3)
-    def _():
-        given_keep.wait()
-
-    loop(1, n_dp, lambda step: ids_move(step).wait_send())
-    loop(1, n_dp, lambda step: slots_move(step).wait_send())
-    ids_copy.wait()
-
-    @pl.when(layer == 0)
-    def _():
-        for copy in outs:
-            copy.wait()
-
-
-def front(words, cot, ids, listed, boxes, vocab, table, gain, shift):
-    quarter, width = words.shape
-    page = 2 * quarter
-    n_dp = lax.axis_size("dp")
-    slots = listed.shape[0]
-    held = vocab.shape[0]
-    side = width // 2
-    any_space = pl.BlockSpec(memory_space=pl.ANY)
-    in_vmem = pl.BlockSpec(memory_space=pltpu.VMEM)
-    dma = pltpu.SemaphoreType.DMA
-    vmem = pltpu.VMEM
-    return pl.pallas_call(
-        front_kernel,
-        out_shape=(
-            jax.ShapeDtypeStruct((page, width), F32),
-            jax.ShapeDtypeStruct((page, width), BF),
-            jax.ShapeDtypeStruct((page, width), F32),
-            jax.ShapeDtypeStruct((2, page, 1), F32),
-            jax.ShapeDtypeStruct((n_dp, 2, BLOCK), jnp.int32),
-        ),
-        in_specs=[in_vmem, any_space, in_vmem, in_vmem, in_vmem, any_space] + [in_vmem] * 3,
-        out_specs=(any_space,) * 5,
-        scratch_shapes=[
-            vmem((2, quarter, width), BF), vmem((n_dp, 2, BLOCK), jnp.int32),
-            vmem((held, side), BF), vmem((n_dp * slots, held), BF),
-            vmem((n_dp, slots, side), BF), vmem((n_dp, slots, side), BF),
-            vmem((2, slots, side), BF), vmem((BLOCK, BLOCK), F32),
-            vmem((page, width), F32), vmem((page, width), F32), vmem((2, page, 1), F32),
-            dma, dma((2,)), dma, dma((2,)), dma((n_dp,)), dma((n_dp,)),
-            dma((n_dp,)), dma((n_dp,)), dma, dma, dma((5,)),
-        ],
-        compiler_params=pltpu.CompilerParams(
-            collective_id=2, has_side_effects=True, vmem_limit_bytes=60 << 20
-        ),
-        name="embedded_rows",
-    )(words, cot, ids, listed, boxes, vocab, table, gain, shift)
+        name="encoder_both_ways",
+    )(words, cot, ids, mask, boxes, vocab, table, gain, shift, *weights, qvb, upb, gains, shifts)
 
 
 def finish_kernel(
     pieces, q_in, o_in, u_in, d_in, rows_in, ids_ref, small_ref, table_ref, act_in, ing_in,
-    act_ref, ing_ref, tab_ref, voc_ref, q_ref, qvb_ref, o_ref, u_ref, upb_ref, d_ref, own_ref,
+    act_ref, ing_ref, tab_ref, voc_ref, q_ref, qvb_ref, o_ref, u_ref, upb_ref, d_ref, gains_ref,
+    shifts_ref, eg_ref, es_ref,
     q_s, o_s, u_s, d_s, q_f, o_f, u_f, d_f, rows_s, in_sem, out_sem, rows_sem,
 ):
     section = lax.axis_index("section")
@@ -1279,8 +1217,18 @@
         upb_ref[0:1, pl.ds(i * side, side)] = own[2 + i : 3 + i]
     here = (parts[0] + partner)[2 * kept : 2 * kept + 16]
     there = (parts[2] + far_partner)[2 * kept : 2 * kept + 16]
-    own_ref[0] = jnp.where(layer == 0, here, there)
-    own_ref[1] = jnp.where(layer == 0, there, here)
+    in_order = (jnp.where(layer == 0, here, there), jnp.where(layer == 0, there, here))
+    for j in range(2):
+        columns = pl.ds(j * side, side)
+        for l in range(2):
+            for i in range(2):
+                at = 2 * i + j
+                gains_ref[l, i : i + 1, columns] = in_order[l][at : at + 1]
+            for i in range(4):
+                at = 4 + 2 * i + j
+                shifts_ref[l, i : i + 1, columns] = in_order[l][at : at + 1]
+        eg_ref[columns] = in_order[0][12 + j]
+        es_ref[columns] = in_order[0][14 + j]
     for l in range(2):
         for h in range(2):
             tab_ref[h, :, pl.ds(l * side, side)] = table_ref[2 * l + h].astype(F32)
@@ -1332,10 +1280,10 @@
         for shape in (
             act.shape, ing.shape, (2, tables.shape[1], width), (count, width), (1, *shapes[0]),
             (1, 2, side), (1, *shapes[1]), (1, *shapes[2]), (1, units), (1, *shapes[3]),
-            (2, 16, side),
+            (2, 2, width), (2, 4, width), (width,), (width,),
         )
     ]
-    specs = [in_vmem] * 4 + [any_space, in_vmem, any_space, any_space, in_vmem, any_space, in_vmem]
+    specs = [in_vmem] * 4 + [any_space, in_vmem, any_space, any_space, in_vmem, any_space] + [in_vmem] * 4
     return pl.pallas_call(
         functools.partial(finish_kernel, pieces),
         out_shape=outs,
@@ -1362,23 +1310,10 @@
     side = qkv_weight.shape[2] // 3
     units = up_bias.shape[1]
 
-    qvb = jnp.stack([qv_bias[0], swapped(qv_bias[0])])
-    upb = jnp.concatenate([up_bias, swapped(up_bias)])
-    gains = lax.dynamic_index_in_dim(layer_gains, layer, 0, keepdims=False)
-    shifts = lax.dynamic_index_in_dim(layer_biases, layer, 0, keepdims=False)
-    slots = mask_pos.shape[1]
-    listed = lax.dynamic_index_in_dim(mask_pos, half, 0, keepdims=False)[:, None]
-    listed_wide = jnp.pad(listed, ((0, BLOCK - slots), (0, 0)), constant_values=-1)
-    ids = jnp.pad(replace_ids, ((0, 0), (0, BLOCK - slots)), constant_values=-1)
-    page_boxes = lax.dynamic_slice_in_dim(boxes, half * page, page, 1)
-
-    hidden_in, given, norm_in, columns, all_ids = front(
-        word_embed, cotangent, ids, listed, page_boxes, vocab_table, layout_table,
-        embed_gain[None], embed_shift[None],
-    )
-    left, right, edge, mine, small = layered(
-        hidden_in, given, norm_in, columns, (qkv_weight, out_weight, up_weight, down_weight),
-        qvb, upb, gains, shifts, embed_gain[None],
+    left, right, all_ids, edge, mine, small = encoded(
+        word_embed, cotangent, replace_ids, mask_pos, boxes, vocab_table, layout_table,
+        embed_gain, embed_shift, (qkv_weight, out_weight, up_weight, down_weight), qv_bias,
+        up_bias[:, None], layer_gains, layer_biases,
     )
     left, right = (array.reshape(2 * page, -1) for array in (left, right))
     counts = (
@@ -1387,11 +1322,8 @@
         (width // BLOCK, units // side),
         (units // BLOCK, width // side),
     )
-    first, second = boxes[:, :page], boxes[:, page:]
-    pair = jnp.stack([jnp.where(half == 0, first, second), jnp.where(half == 0, second, first)])
-    pair = jnp.where(half == 0, pair[:, 0::2], pair[:, 1::2])
     *sums, gathered, slot_rows, table_rows, act, ing = reduced(
-        left, right, small, edge, mine, pair, listed_wide, counts, side
+        left, right, small, edge, mine, boxes, mask_pos, counts, side
     )
     outer = lax.axis_size("dp") // GROUP
     table_part = None
@@ -1400,6 +1332,7 @@
         *sums, gathered = lax.psum((*sums, gathered), "dp", axis_index_groups=groups)
         slot_rows = lax.all_gather(slot_rows, "dp", axis_index_groups=groups, axis=1, tiled=True)
         coords = jnp.arange(layout_table.shape[1], dtype=jnp.int32)
+        page_boxes = lax.dynamic_slice_in_dim(boxes, half * page, page, 1)
         grad_low = jnp.concatenate([edge[0], edge[1]], 1)
         grad_low = jnp.where(layer == 0, grad_low, jnp.zeros_like(grad_low))
         table_grad = jnp.stack(
@@ -1416,17 +1349,14 @@
             table_grad.astype(BF), ("dp", "section"), scatter_dimension=1, tiled=True
         ).astype(F32)
     count = vocab_table.shape[0] // lax.axis_size("section")
-    act, ing, tables, vocab_part, q_sum, qvb_sum, o_sum, u_sum, upb_sum, d_sum, rest = finished(
+    act, ing, tables, vocab_part, *rest = finished(
         sums, slot_rows, all_ids, gathered, table_rows, act, ing, count, side
     )
     if table_part is None:
         table_part = tables
-    gains_sum = rest[:, :4].reshape(2, 2, width)
-    shifts_sum = rest[:, 4:12].reshape(2, 4, width)
+    *layer_sums, gains_sum, shifts_sum, gain_sum, shift_sum = rest
     return (
-        act, ing, table_part, vocab_part, rest[0, 12:14].reshape(width),
-        rest[0, 14:16].reshape(width), q_sum, qvb_sum, o_sum, u_sum, upb_sum, d_sum, gains_sum,
-        shifts_sum,
+        act, ing, table_part, vocab_part, gain_sum, shift_sum, *layer_sums, gains_sum, shifts_sum,
     )
 
 

time: 346 us -> 316 us (0.913)
  Pallas kernels: 328 us -> 313 us
  local copies, waits for them, and re-layouts: 11.9 us -> 0 us
    pallas_call x2 -> x1, Pallas kernels: 149 us -> 128 us  [encoded(): pl.pallas_call(encoder_kernel, out_shape=(jax.ShapeDtypeStruct((2, page,...]
    pallas_call x1, Pallas kernels: 164 us -> 171 us  [reduced(): pl.pallas_call(functools.partial(reduce_kernel, counts), out_shape=tuple(...]
  transfers between devices with their start and end apart: 2 -> 0, of which waited for: 0 -> 0; matrix products, arithmetic and copies ran while one was open for 3% -> 0% of each run, Pallas kernels for 9% -> 0%
where the time goes in v4:
time: 316 us; the launch traced here: 314 us
  Pallas kernels  313 us (99%)
    pallas_call x1, Pallas kernels, reduced(): pl.pallas_call(functools.partial(reduce_kernel, counts), out_shape=tuple(...  171 us
    pallas_call x1, Pallas kernels, encoded(): pl.pallas_call(encoder_kernel, out_shape=(jax.ShapeDtypeStruct((2, page,...  128 us
    pallas_call x1, Pallas kernels, finished(): pl.pallas_call(functools.partial(finish_kernel, pieces), out_shape=outs,...  14.4 us

profile of v4, /device:TPU:0, one launch (start us, length us, event | category | flops | bytes accessed | tf_op | source)
XLA Modules:
  0.0 313.5 jit_solution(2196533645852788520)
XLA Ops:
  0.7 127.6 %encoder_both_ways.1 = (bf16[2,512,3456]{2,1,0:T(8,128)(2,1)}, bf16[2,512,4224]{2,1,0:T(8,128)(2,1)}, s32[8,2,128]{2,1,0:T(2,128)}, bf16[2,512,384]{2,1,0:T(8,12...) custom-call(bf16[256,768]{1,0:T(8,128)(2,1)} %words_ref.1, bf16[256,768]{1,0:T(8,128)(2,1)} %cot_ref.1, ...), custom_call_target="tpu_custom_call" | custom-call | flops 57982058496 | bytes 209715200 | tf_op jit(solution)/shard_map/encoder_both_ways/pallas_call | solution.py:1133
  128.3 170.6 %gradient_sums.1 = (bf16[768,1152]{1,0:T(8,128)(2,1)}, bf16[384,768]{1,0:T(8,128)(2,1)}, bf16[768,1536]{1,0:T(8,128)(2,1)}, bf16[1536,768]{1,0:T(8,128)(2,1)}, b...) custom-call(bf16[1024,3456]{1,0:T(8,128)(2,1)} %bitcast.5, ...), custom_call_target="tpu_custom_call" | custom-call | flops 7348420608 | bytes 419430400 | tf_op jit(solution)/shard_map/gradient_sums/pallas_call | solution.py:510
  298.9 14.4 %finished_outputs.1 = (f32[256,768]{1,0:T(8,128)}, f32[256,768]{1,0:T(8,128)}, f32[2,32,768]{2,1,0:T(8,128)}, f32[512,768]{1,0:T(8,128)}, f32[1,768,1152]{2,1,0:...) custom-call(bf16[768,1152]{1,0:T(8,128)(2,1)} %get-tuple-element.48., ...), custom_call_target="tpu_custom_call" | custom-call | tf_op jit(solution)/shard_map/finished_outputs/pallas_call | solution.py:1287

commit v5 on v4

--- a/solution.py
+++ b/solution.py
@@ -23,7 +23,9 @@
 BLOCK = 128
 HOP = 4
 DEPTH = 3
-EXTRA = 20
+FIRST = 20
+EXTRA = 36
+GUESTS = 6
 
 
 def tree_of(k):
@@ -44,16 +46,26 @@
 
 
 def reduce_kernel(
-    counts, a_in, b_in, small_ref, edge_ref, mine_ref, box_ref, listed_ref,
-    q_ref, o_ref, u_ref, d_ref, gathered_ref, rows_ref, table_ref, act_ref, ing_ref,
+    counts, a_in, b_in, small_ref, edge_ref, mine_ref, box_ref, listed_ref, ids_ref,
+    q_ref, o_ref, u_ref, d_ref, gathered_ref, rows_ref, table_ref, act_ref, ing_ref, voc_ref,
     a_ref, b_ref, square, buf, total, gathered, edge, rows, table, piece,
     send, recv, out_sem, g_send, g_recv, e_send, e_recv, r_send, r_recv, t_send, t_recv,
-    f_send, f_recv, m_send, m_recv, last_sem, in_sem,
+    f_send, f_recv, m_send, m_recv, last_sem, in_sem, voc, entered,
+    away_send, away_recv, back_send, back_recv,
 ):
-    loads = (
-        pltpu.make_async_copy(a_in, a_ref, in_sem.at[0]),
-        pltpu.make_async_copy(b_in, b_ref, in_sem.at[1]),
-    )
+    a_cut = a_ref.shape[1] - counts[3][0] * BLOCK
+    b_cut = b_ref.shape[1] - counts[3][1] * buf.shape[3]
+    loads = []
+    for columns_a, columns_b in (
+        (pl.ds(a_cut, a_ref.shape[1] - a_cut), pl.ds(b_cut, b_ref.shape[1] - b_cut)),
+        (pl.ds(0, a_cut), pl.ds(0, b_cut)),
+    ):
+        for source, target, columns in ((a_in, a_ref, columns_a), (b_in, b_ref, columns_b)):
+            loads.append(
+                pltpu.make_async_copy(
+                    source.at[:, columns], target.at[:, columns], in_sem.at[len(loads)]
+                )
+            )
     for copy in loads:
         copy.start()
     me = lax.axis_index("dp")
@@ -66,7 +78,8 @@
     place = me % GROUP
     z = place // 2
     y = place % 2
-    chunks = buf.shape[1]
+    chunks = buf.shape[1] - GUESTS
+    limit = jnp.where(layer == 0, chunks - GUESTS, chunks + GUESTS)
     side = buf.shape[3]
     slots = rows.shape[2]
     n_q, n_o, n_u, n_d = counts
@@ -86,14 +99,20 @@
                 barrier, inc=1, device_id=(me + deltas[d], section), device_id_type=mesh_id
             )
 
-    for step in range(1, n_sections):
-        pl.semaphore_signal(
-            barrier, inc=1, device_id=(me, (section + step) % n_sections), device_id_type=mesh_id
-        )
-    pl.semaphore_wait(
-        barrier,
-        n_sections + jnp.where(exists[0], 1, 0) + jnp.where(exists[1], 1, 0),
-    )
+    pl.semaphore_signal(barrier, inc=1, device_id=(me, other_core), device_id_type=mesh_id)
+
+    @pl.when(layer == 1)
+    def _():
+        for h in range(2):
+            pl.semaphore_signal(barrier, inc=1, device_id=(me, h), device_id_type=mesh_id)
+
+    around = 2 + jnp.where(exists[0], 1, 0) + jnp.where(exists[1], 1, 0)
+    pl.semaphore_wait(barrier, around + jnp.where(layer == 0, 2, 0))
+
+    @pl.when(layer == 0)
+    def _():
+        for h in range(2):
+            pl.semaphore_signal(entered, inc=1, device_id=(me, 2 + h), device_id_type=mesh_id)
 
     def remote(source, target, sent, got, device):
         return pltpu.make_async_remote_copy(
@@ -114,8 +133,8 @@
             mine_ref.at[pl.ds(r * quarter, quarter)], target, m_send.at[r]
         )
 
-    for r in range(2):
-        for kind, target in ((0, ing_ref), (1, act_ref)):
+    def spread_all(kind, target):
+        for r in range(2):
 
             @pl.when((layer == kind) & (section != 2 * half + r))
             def _():
@@ -226,18 +245,54 @@
             left, right, (((0,), (0,)), ((), ())), preferred_element_type=F32
         )
 
+    def away(g):
+        return remote(
+            buf.at[3, chunks - GUESTS + g], buf.at[3, chunks + g], away_send.at[g],
+            away_recv.at[g], (me, other_layer),
+        )
+
+    def back(g, source):
+        return remote(
+            buf.at[source, chunks + g], buf.at[0, chunks - GUESTS + g], back_send.at[g],
+            back_recv.at[g], (me, other_layer),
+        )
+
+    def finish(k, source):
+        @pl.when(k < chunks)
+        def _():
+            put(k, source)
+
+        @pl.when(k >= chunks)
+        def _():
+            back(k - chunks, source).start()
+
+    def send_away(g):
+        k = chunks - GUESTS + g
+        product(k)
+        buf[3, k] = total[...].astype(BF)
+        away(g).start()
+
+    def receive_back(g):
+        back(g, 3).wait_recv()
+        put(chunks - GUESTS + g, 0)
+
     def climb(k, level):
         child, parent, depth = roles(tree_of(k))
 
-        @pl.when((k >= 0) & (k < chunks) & (depth == DEPTH - level))
+        @pl.when((k >= 0) & (k < limit) & (depth == DEPTH - level))
         def _():
             @pl.when(k == 0)
             def _():
                 total[...] = small_ref[...]
 
-            @pl.when(k > 0)
+            @pl.when((k > 0) & (k < chunks))
             def _():
                 product(k)
+
+            @pl.when(k >= chunks)
+            def _():
+                away(k - chunks).wait_recv()
+                total[...] = buf[3, k].astype(F32)
 
             if level > 0:
                 for d in range(3):
@@ -257,12 +312,12 @@
                     def _():
                         transfer(k, d, 3).start()
 
-                put(k, 3)
+                finish(k, 3)
 
     def descend(k, level):
         child, parent, depth = roles(tree_of(k))
 
-        @pl.when((k >= 0) & (k < chunks) & (depth == level))
+        @pl.when((k >= 0) & (k < limit) & (depth == level))
         def _():
             arrived(k, parent)
             for d in range(3):
@@ -271,7 +326,7 @@
                 def _():
                     transfer(k, d, parent).start()
 
-            put(k, parent)
+            finish(k, parent)
 
     def settle(k):
         child, parent, depth = roles(tree_of(k))
@@ -281,7 +336,7 @@
             def _():
                 transfer(k, d, 3).wait_send()
 
-        @pl.when(k > 0)
+        @pl.when((k > 0) & (k < chunks))
         def _():
             pltpu.make_async_copy(
                 buf.at[3, k], d_ref.at[pl.ds(0, BLOCK), pl.ds(0, side)], out_sem.at[k]
@@ -292,6 +347,13 @@
             climb(t - level * HOP, level)
         for level in range(1, DEPTH + 1):
             descend(t - (DEPTH + level) * HOP, level)
+
+    def settle_away(g):
+        pltpu.make_async_copy(
+            buf.at[0, chunks - GUESTS + g], d_ref.at[pl.ds(0, BLOCK), pl.ds(0, side)],
+            out_sem.at[chunks - GUESTS + g],
+        ).wait()
+        away(g).wait_send()
 
     def slots_down(c, d):
         return remote(
@@ -413,7 +475,29 @@
         slots_across(c).wait_send()
         for kind in range(2):
             slots_beside(c, kind).wait_send()
-            slots_got(c, 2 + kind)
+
+    count = voc.shape[0]
+    base = (me * n_sections + section) * count
+
+    def tokens(n):
+        at = base + lax.broadcasted_iota(jnp.int32, (count, BLOCK), 0)
+        first = lax.rem(half + n // 2, 2) == 0
+        spots = []
+        for origin in range(GROUP):
+            row = ids_ref[origin]
+            spots.append((at == jnp.where(first, row[0:1], row[1:2])).astype(F32).astype(BF))
+        spots = jnp.concatenate(spots, 1)
+        held = rows[n].reshape(GROUP * slots, side)
+        term = jnp.dot(spots, held, preferred_element_type=F32)
+        columns = pl.ds(pl.multiple_of(lax.rem(layer + n, 2) * side, side), side)
+
+        @pl.when(n < 2)
+        def _():
+            voc[:, columns] = term
+
+        @pl.when(n >= 2)
+        def _():
+            voc[:, columns] += term
 
     def handed(step):
         return remote(
@@ -421,15 +505,26 @@
             (me, (section + n_sections - step) % n_sections),
         )
 
-    for copy in loads:
+    for copy in loads[:2]:
         copy.wait()
-    loop(0, EXTRA, advance)
+    loop(0, FIRST, advance)
+    for copy in loads[2:]:
+        copy.wait()
+
+    @pl.when(layer == 0)
+    def _():
+        loop(0, GUESTS, send_away)
+
+    spread_all(0, ing_ref)
+    loop(FIRST, EXTRA, advance)
 
     @pl.when(layer == 1)
     def _():
+        pl.semaphore_wait(entered, 2)
         edge_across().wait_recv()
         edge_beside(edge.at[0]).start()
 
+    spread_all(1, act_ref)
     edge_beside(edge.at[0]).wait_recv()
     used = listed_ref.shape[1]
     listed = listed_ref[...].astype(F32)
@@ -452,7 +547,19 @@
     gathered[0] = buf[mine, 0, :kept_small]
     for step in range(1, n_sections):
         handed(step).start()
-    loop(middle, chunks + 2 * DEPTH * HOP, advance)
+    for c in range(GROUP):
+        for kind in range(2):
+            slots_got(c, 2 + kind)
+
+    def late(t):
+        advance(t)
+        n = t - middle - 2
+
+        @pl.when((n >= 0) & (n < 4))
+        def _():
+            tokens(n)
+
+    loop(middle, limit + 2 * DEPTH * HOP, late)
     loop(0, GROUP, settle_extras)
     for step in range(1, n_sections):
         handed(step).wait()
@@ -466,6 +573,7 @@
         pltpu.make_async_copy(gathered, gathered_ref, last_sem.at[0]),
         pltpu.make_async_copy(rows, rows_ref, last_sem.at[1]),
         pltpu.make_async_copy(table, table_ref, last_sem.at[2]),
+        pltpu.make_async_copy(voc, voc_ref, last_sem.at[3]),
     )
     for copy in outs:
         copy.start()
@@ -492,12 +600,22 @@
         edge_across().wait_send()
 
     edge_beside(edge.at[0]).wait_send()
-    loop(0, chunks, settle)
+    loop(0, limit, settle)
+
+    @pl.when(layer == 0)
+    def _():
+        loop(0, GUESTS, receive_back)
+        loop(0, GUESTS, settle_away)
+
+    @pl.when(layer == 1)
+    def _():
+        loop(0, GUESTS, lambda g: back(g, 3).wait_send())
+
     for copy in outs:
         copy.wait()
 
 
-def reduced(a, b, small, edge, mine, boxes, listed, counts, side):
+def reduced(a, b, small, edge, mine, boxes, listed, ids, count, counts, side):
     chunks = 1 + sum(count[0] * count[1] for count in counts)
     n_sections = lax.axis_size("section")
     kept = 32
@@ -518,28 +636,32 @@
             jax.ShapeDtypeStruct((n_sections, BLOCK // n_sections, side), BF),
             jax.ShapeDtypeStruct((mine.shape[0] // 2, mine.shape[1]), BF),
             jax.ShapeDtypeStruct((mine.shape[0] // 2, mine.shape[1]), BF),
+            jax.ShapeDtypeStruct((count, mine.shape[1]), F32),
         ),
-        in_specs=[any_space] * 2 + [in_vmem] * 2 + [any_space] + [in_vmem] * 2,
-        out_specs=(any_space,) * 9,
+        in_specs=[any_space] * 2 + [in_vmem] * 2 + [any_space] + [in_vmem] * 3,
+        out_specs=(any_space,) * 10,
         scratch_shapes=[
             pltpu.VMEM(a.shape, BF),
             pltpu.VMEM(b.shape, BF),
             pltpu.VMEM((BLOCK, BLOCK), F32),
-            pltpu.VMEM((4, chunks, BLOCK, side), BF),
+            pltpu.VMEM((4, chunks + GUESTS, BLOCK, side), BF),
             pltpu.VMEM((BLOCK, side), F32),
             pltpu.VMEM((n_sections, kept, side), BF),
             pltpu.VMEM((2, page, side), BF),
             pltpu.VMEM((4, GROUP, slots, side), BF),
             pltpu.VMEM((n_sections, BLOCK // n_sections, side), BF),
             pltpu.VMEM((4, GROUP, BLOCK, side), BF),
-            dma((3, chunks)), dma((3, chunks)), dma((chunks,)),
+            dma((3, chunks + GUESTS)), dma((3, chunks + GUESTS)), dma((chunks,)),
             dma((n_sections,)), dma((n_sections,)),
             dma((2,)), dma((2,)),
             dma((6, GROUP)), dma((4, GROUP)),
             dma((3, GROUP)), dma((3, GROUP)),
             dma((n_sections,)), dma((n_sections,)),
             dma((2,)), dma((2,)),
-            dma((3,)), dma((2,)),
+            dma((4,)), dma((4,)),
+            pltpu.VMEM((count, mine.shape[1]), F32),
+            pltpu.SemaphoreType.REGULAR,
+            dma((GUESTS,)), dma((GUESTS,)), dma((GUESTS,)), dma((GUESTS,)),
         ],
         compiler_params=pltpu.CompilerParams(
             collective_id=0, has_side_effects=True, vmem_limit_bytes=60 << 20
@@ -548,7 +670,7 @@
             flops=flops, bytes_accessed=400 << 20, transcendentals=0
         ),
         name="gradient_sums",
-    )(a, b, small, edge, mine, boxes, listed)
+    )(a, b, small, edge, mine, boxes, listed, ids)
 
 
 ROWS = 256
@@ -1179,18 +1301,17 @@
 
 
 def finish_kernel(
-    pieces, q_in, o_in, u_in, d_in, rows_in, ids_ref, small_ref, table_ref, act_in, ing_in,
+    pieces, q_in, o_in, u_in, d_in, voc_in, small_ref, table_ref, act_in, ing_in,
     act_ref, ing_ref, tab_ref, voc_ref, q_ref, qvb_ref, o_ref, u_ref, upb_ref, d_ref, gains_ref,
     shifts_ref, eg_ref, es_ref,
-    q_s, o_s, u_s, d_s, q_f, o_f, u_f, d_f, rows_s, in_sem, out_sem, rows_sem,
+    q_s, o_s, u_s, d_s, q_f, o_f, u_f, d_f, in_sem, out_sem, voc_s, voc_sem,
 ):
     section = lax.axis_index("section")
     layer = section // 2
     half = section % 2
-    side = rows_s.shape[3]
-    n_dp = rows_s.shape[1]
-    rows_copy = pltpu.make_async_copy(rows_in, rows_s, rows_sem)
-    rows_copy.start()
+    side = table_ref.shape[2]
+    voc_copy = pltpu.make_async_copy(voc_in, voc_s, voc_sem.at[0])
+    voc_copy.start()
     moves = []
     for source, low, wide, target in (
         (d_in, d_s, d_f, d_ref), (u_in, u_s, u_f, u_ref), (q_in, q_s, q_f, q_ref),
@@ -1203,6 +1324,9 @@
     for i, (source, low, wide, target) in enumerate(moves):
         pltpu.make_async_copy(source, low, in_sem.at[i]).start()
 
+    voc_copy.wait()
+    voc_out = pltpu.make_async_copy(voc_s, voc_ref, voc_sem.at[1])
+    voc_out.start()
     act_ref[...] = act_in[...].astype(F32)
     ing_ref[...] = ing_in[...].astype(F32)
 
@@ -1238,35 +1362,12 @@
         wide[...] = low[...].astype(F32)
         pltpu.make_async_copy(wide, target, out_sem.at[i]).start()
 
-    count = voc_ref.shape[0]
-    base = (lax.axis_index("dp") * lax.axis_size("section") + section) * count
-    rows_copy.wait()
-    at = base + lax.broadcasted_iota(jnp.int32, (count, BLOCK), 0)
-    for h in range(2):
-        list_at = jnp.where(half == 0, h, 1 - h)
-        for group in range(n_dp // 4):
-            spots = []
-            for origin in range(group * 4, group * 4 + 4):
-                row = ids_ref[origin]
-                row = jnp.where(list_at == 0, row[0:1], row[1:2])
-                spots.append((at == row).astype(F32).astype(BF))
-            spots = jnp.concatenate(spots, 1)
-            for l in range(2):
-                rows = rows_s[2 * h + l, group * 4 : group * 4 + 4].reshape(4 * BLOCK, side)
-                term = jnp.dot(spots, rows, preferred_element_type=F32)
-                columns = pl.ds(
-                    pl.multiple_of(jnp.where(layer == 0, l, 1 - l) * side, side), side
-                )
-                if h == 0 and group == 0:
-                    voc_ref[:, columns] = term
-                else:
-                    voc_ref[:, columns] += term
-
     for i, (source, low, wide, target) in enumerate(moves):
         pltpu.make_async_copy(wide, target, out_sem.at[i]).wait()
-
-
-def finished(sums, rows, ids, small, tables, act, ing, count, side):
+    voc_out.wait()
+
+
+def finished(sums, voc, small, tables, act, ing, side):
     any_space = pl.BlockSpec(memory_space=pl.ANY)
     in_vmem = pl.BlockSpec(memory_space=pltpu.VMEM)
     dma = pltpu.SemaphoreType.DMA
@@ -1278,23 +1379,23 @@
     outs = [
         jax.ShapeDtypeStruct(shape, F32)
         for shape in (
-            act.shape, ing.shape, (2, tables.shape[1], width), (count, width), (1, *shapes[0]),
+            act.shape, ing.shape, (2, tables.shape[1], width), voc.shape, (1, *shapes[0]),
             (1, 2, side), (1, *shapes[1]), (1, *shapes[2]), (1, units), (1, *shapes[3]),
             (2, 2, width), (2, 4, width), (width,), (width,),
         )
     ]
-    specs = [in_vmem] * 4 + [any_space, in_vmem, any_space, any_space, in_vmem, any_space] + [in_vmem] * 4
+    specs = [in_vmem] * 3 + [any_space] * 2 + [in_vmem, any_space, any_space, in_vmem, any_space] + [in_vmem] * 4
     return pl.pallas_call(
         functools.partial(finish_kernel, pieces),
         out_shape=outs,
-        in_specs=[any_space] * 5 + [in_vmem] * 5,
+        in_specs=[any_space] * 5 + [in_vmem] * 4,
         out_specs=specs,
         scratch_shapes=[vmem(shape, BF) for shape in shapes]
         + [vmem(shape, F32) for shape in shapes]
-        + [vmem(rows.shape, BF), dma((4 * pieces,)), dma((4 * pieces,)), dma],
+        + [dma((4 * pieces,)), dma((4 * pieces,)), vmem(voc.shape, F32), dma((2,))],
         compiler_params=pltpu.CompilerParams(vmem_limit_bytes=60 << 20),
         name="finished_outputs",
-    )(*sums, rows, ids, small, tables, act, ing)
+    )(*sums, voc, small, tables, act, ing)
 
 
 def on_device(
@@ -1322,8 +1423,9 @@
         (width // BLOCK, units // side),
         (units // BLOCK, width // side),
     )
-    *sums, gathered, slot_rows, table_rows, act, ing = reduced(
-        left, right, small, edge, mine, boxes, mask_pos, counts, side
+    count = vocab_table.shape[0] // lax.axis_size("section")
+    *sums, gathered, slot_rows, table_rows, act, ing, voc = reduced(
+        left, right, small, edge, mine, boxes, mask_pos, all_ids, count, counts, side
     )
     outer = lax.axis_size("dp") // GROUP
     table_part = None
@@ -1331,6 +1433,15 @@
         groups = [[i + GROUP * g for g in range(outer)] for i in range(GROUP)]
         *sums, gathered = lax.psum((*sums, gathered), "dp", axis_index_groups=groups)
         slot_rows = lax.all_gather(slot_rows, "dp", axis_index_groups=groups, axis=1, tiled=True)
+        here = jnp.arange(count, dtype=jnp.int32)
+        here = here + (lax.axis_index("dp") * lax.axis_size("section") + section) * count
+        ordered_ids = jnp.where(half == 0, all_ids, all_ids[:, ::-1])
+        ordered_ids = ordered_ids.transpose(1, 0, 2).reshape(-1)
+        held = slot_rows.reshape(2, 2, -1, side).transpose(0, 2, 1, 3).reshape(-1, width)
+        voc = jnp.dot(
+            (here[:, None] == ordered_ids[None]).astype(BF), held, preferred_element_type=F32
+        )
+        voc = jnp.where(layer == 0, voc, jnp.roll(voc, side, 1))
         coords = jnp.arange(layout_table.shape[1], dtype=jnp.int32)
         page_boxes = lax.dynamic_slice_in_dim(boxes, half * page, page, 1)
         grad_low = jnp.concatenate([edge[0], edge[1]], 1)
@@ -1348,9 +1459,8 @@
         table_part = lax.psum_scatter(
             table_grad.astype(BF), ("dp", "section"), scatter_dimension=1, tiled=True
         ).astype(F32)
-    count = vocab_table.shape[0] // lax.axis_size("section")
     act, ing, tables, vocab_part, *rest = finished(
-        sums, slot_rows, all_ids, gathered, table_rows, act, ing, count, side
+        sums, voc, gathered, table_rows, act, ing, side
     )
     if table_part is None:
         table_part = tables

time: 316 us -> 305 us (0.965)
  Pallas kernels: 313 us -> 304 us
    pallas_call x1, Pallas kernels: 171 us -> 165 us  [reduced(): pl.pallas_call(functools.partial(reduce_kernel, counts), out_shape=tuple(...]
where the time goes in v5:
time: 305 us
  Pallas kernels  304 us (100%)
    pallas_call x1, Pallas kernels, reduced(): pl.pallas_call(functools.partial(reduce_kernel, counts), out_shape=tuple(...  165 us
    pallas_call x1, Pallas kernels, encoded(): pl.pallas_call(encoder_kernel, out_shape=(jax.ShapeDtypeStruct((2, page,...  128 us
    pallas_call x1, Pallas kernels, finished(): pl.pallas_call(functools.partial(finish_kernel, pieces), out_shape=outs,...  11.9 us

profile of v5, /device:TPU:0, one launch (start us, length us, event | category | flops | bytes accessed | tf_op | source)
XLA Modules:
  0.0 305.0 jit_solution(13201146349422529140)
XLA Ops:
  0.7 127.6 %encoder_both_ways.1 = (bf16[2,512,3456]{2,1,0:T(8,128)(2,1)}, bf16[2,512,4224]{2,1,0:T(8,128)(2,1)}, s32[8,2,128]{2,1,0:T(2,128)}, bf16[2,512,384]{2,1,0:T(8,12...) custom-call(bf16[256,768]{1,0:T(8,128)(2,1)} %words_ref.1, bf16[256,768]{1,0:T(8,128)(2,1)} %cot_ref.1, ...), custom_call_target="tpu_custom_call" | custom-call | flops 57982058496 | bytes 209715200 | tf_op jit(solution)/shard_map/encoder_both_ways/pallas_call | solution.py:1255
  128.3 164.7 %gradient_sums.1 = (bf16[768,1152]{1,0:T(8,128)(2,1)}, bf16[384,768]{1,0:T(8,128)(2,1)}, bf16[768,1536]{1,0:T(8,128)(2,1)}, bf16[1536,768]{1,0:T(8,128)(2,1)}, b...) custom-call(bf16[1024,3456]{1,0:T(8,128)(2,1)} %bitcast.5, ...), custom_call_target="tpu_custom_call" | custom-call | flops 7348420608 | bytes 419430400 | tf_op jit(solution)/shard_map/gradient_sums/pallas_call | solution.py:628
  293.0 11.9 %finished_outputs.1 = (f32[256,768]{1,0:T(8,128)}, f32[256,768]{1,0:T(8,128)}, f32[2,32,768]{2,1,0:T(8,128)}, f32[512,768]{1,0:T(8,128)}, f32[1,768,1152]{2,1,0:...) custom-call(bf16[768,1152]{1,0:T(8,128)(2,1)} %get-tuple-element.49., ...), custom_call_target="tpu_custom_call" | custom-call | tf_op jit(solution)/shard_map/finished_outputs/pallas_call | solution.py:1388

commit v6 on v5

--- a/solution.py
+++ b/solution.py
@@ -21,20 +21,27 @@
 
 GROUP = 8
 BLOCK = 128
-HOP = 4
-DEPTH = 3
+HOP = 5
+DEPTH = 4
 FIRST = 20
 EXTRA = 36
 GUESTS = 6
+SETTLED = 9
 
 
 def tree_of(k):
-    turn = k % 8
-    return turn < 4, 1 + turn % 2, (turn // 2) % 2
+    lines = lax.div(4 * k, 10)
+    comb = lax.rem(4 * k, 10) < 6
+    pick = jnp.where(comb, k - lines, lines)
+    root_z = 3 * lax.rem(pick, 2)
+    near = lax.rem(lax.div(pick, 4), 2)
+    rung = jnp.where(comb, root_z, jnp.where(root_z == 0, near, 3 - near))
+    return comb, root_z, lax.rem(lax.div(pick, 2), 2), rung
 
 
 def rooted_at(c):
-    return (c // 2) % 2 == 0, c // 2, c % 2
+    line = lax.div(c, 2)
+    return lax.rem(line, 2) == 0, line, lax.rem(c, 2), line
 
 
 def loop(low, high, body):
@@ -159,19 +166,27 @@
         edge[0] = edge_ref[0]
 
     def roles(tree):
-        comb, root_z, root_y = tree
+        comb, root_z, root_y, rung = tree
         along = jnp.logical_or(jnp.logical_not(comb), y == root_y)
-        across = jnp.logical_or(comb, z == root_z)
+        across = jnp.logical_or(comb, z == rung)
+        pivot = jnp.where(y == root_y, root_z, rung)
         child = (
-            exists[0] & along & (z <= root_z),
-            exists[1] & along & (z >= root_z),
+            exists[0] & along & (z <= pivot),
+            exists[1] & along & (z >= pivot),
             across & (y == root_y),
         )
-        up_z = along & (z != root_z)
+        up_z = along & (z != pivot)
         up_y = across & (y != root_y)
-        parent = jnp.where(up_z, jnp.where(z < root_z, 1, 0), jnp.where(up_y, 2, 3))
-        depth = jnp.abs(z - root_z) + jnp.abs(y - root_y)
-        return child, parent, depth
+        parent = jnp.where(up_z, jnp.where(z < pivot, 1, 0), jnp.where(up_y, 2, 3))
+        return child, parent
+
+    def depth_of(k):
+        comb, root_z, root_y, rung = tree_of(jnp.maximum(k, 0))
+        beyond = jnp.abs(z - rung) + 1 + jnp.abs(rung - root_z)
+        return jnp.where(y == root_y, jnp.abs(z - root_z), beyond)
+
+    def depth_from(c):
+        return jnp.abs(z - lax.div(c, 2)) + jnp.abs(y - lax.rem(c, 2))
 
     def neighbour(d):
         return me + jnp.where(d == 0, deltas[0], jnp.where(d == 1, deltas[1], deltas[2]))
@@ -276,33 +291,35 @@
         back(g, 3).wait_recv()
         put(chunks - GUESTS + g, 0)
 
+    def prepare(k):
+        @pl.when((k > 0) & (k < jnp.minimum(limit, chunks)))
+        def _():
+            product(k)
+            buf[3, k] = total[...].astype(BF)
+
     def climb(k, level):
-        child, parent, depth = roles(tree_of(k))
-
-        @pl.when((k >= 0) & (k < limit) & (depth == DEPTH - level))
-        def _():
-            @pl.when(k == 0)
-            def _():
-                total[...] = small_ref[...]
-
-            @pl.when((k > 0) & (k < chunks))
-            def _():
-                product(k)
+        @pl.when((k >= 0) & (k < limit) & (depth_of(k) == DEPTH - level))
+        def _():
+            child, parent = roles(tree_of(k))
 
             @pl.when(k >= chunks)
             def _():
                 away(k - chunks).wait_recv()
-                total[...] = buf[3, k].astype(F32)
 
             if level > 0:
-                for d in range(3):
-
-                    @pl.when(child[d])
-                    def _():
-                        arrived(k, d)
-                        total[...] += buf[d, k].astype(F32)
-
-            buf[3, k] = total[...].astype(BF)
+
+                @pl.when(child[0] | child[1] | child[2])
+                def _():
+                    total[...] = buf[3, k].astype(F32)
+                    for d in range(3):
+
+                        @pl.when(child[d])
+                        def _():
+                            arrived(k, d)
+                            total[...] += buf[d, k].astype(F32)
+
+                    buf[3, k] = total[...].astype(BF)
+
             if level < DEPTH:
                 transfer(k, parent, 3).start()
             else:
@@ -315,10 +332,9 @@
                 finish(k, 3)
 
     def descend(k, level):
-        child, parent, depth = roles(tree_of(k))
-
-        @pl.when((k >= 0) & (k < limit) & (depth == level))
-        def _():
+        @pl.when((k >= 0) & (k < limit) & (depth_of(k) == level))
+        def _():
+            child, parent = roles(tree_of(k))
             arrived(k, parent)
             for d in range(3):
 
@@ -329,7 +345,7 @@
             finish(k, parent)
 
     def settle(k):
-        child, parent, depth = roles(tree_of(k))
+        child, parent = roles(tree_of(k))
         for d in range(3):
 
             @pl.when(child[d] | (parent == d))
@@ -343,10 +359,17 @@
             ).wait()
 
     def advance(t):
+        old = t - SETTLED * HOP
+
+        @pl.when((old >= 0) & (old < limit))
+        def _():
+            settle(old)
+
         for level in range(DEPTH + 1):
             climb(t - level * HOP, level)
         for level in range(1, DEPTH + 1):
             descend(t - (DEPTH + level) * HOP, level)
+        prepare(t + 1)
 
     def settle_away(g):
         pltpu.make_async_copy(
@@ -379,10 +402,9 @@
         ).wait_recv()
 
     def share_slots(c, level):
-        child, parent, depth = roles(rooted_at(c))
-
-        @pl.when((c >= 0) & (c < GROUP) & (depth == level))
-        def _():
+        @pl.when((c >= 0) & (c < GROUP) & (depth_from(c) == level))
+        def _():
+            child, parent = roles(rooted_at(c))
             if level > 0:
                 slots_got(c, 0)
             for d in range(3):
@@ -415,10 +437,9 @@
         )
 
     def table_climb(c, level):
-        child, parent, depth = roles(rooted_at(c))
-
-        @pl.when((c >= 0) & (c < GROUP) & (depth == DEPTH + 1 - level))
-        def _():
+        @pl.when((c >= 0) & (c < GROUP) & (depth_from(c) == DEPTH - level))
+        def _():
+            child, parent = roles(rooted_at(c))
             at = c * BLOCK + lax.broadcasted_iota(jnp.int32, (BLOCK, edge.shape[1]), 0)
             reach = edge.shape[1]
             for part in range(2):
@@ -444,7 +465,7 @@
                         total[...] += piece[d, c].astype(F32)
 
             piece[3, c] = total[...].astype(BF)
-            if level < DEPTH + 1:
+            if level < DEPTH:
                 table_up(c, parent).start()
             else:
                 for step in range(1, n_sections):
@@ -454,14 +475,14 @@
 
     def extras(t):
         c = t - EXTRA
-        for level in range(DEPTH + 2):
+        for level in range(DEPTH + 1):
             share_slots(c - level * HOP, level)
-        relay_slots(c - (DEPTH + 3) * HOP)
-        for level in range(DEPTH + 2):
+        relay_slots(c - (DEPTH + 2) * HOP)
+        for level in range(DEPTH + 1):
             table_climb(c - GROUP - level * HOP, level)
 
     def settle_extras(c):
-        child, parent, depth = roles(rooted_at(c))
+        child, parent = roles(rooted_at(c))
         for d in range(3):
 
             @pl.when(child[d])
@@ -507,6 +528,7 @@
 
     for copy in loads[:2]:
         copy.wait()
+    buf[3, 0] = small_ref[...].astype(BF)
     loop(0, FIRST, advance)
     for copy in loads[2:]:
         copy.wait()
@@ -540,7 +562,7 @@
         advance(t)
         extras(t)
 
-    middle = EXTRA + 2 * GROUP + (DEPTH + 3) * HOP
+    middle = EXTRA + 2 * GROUP + (DEPTH + 2) * HOP
     loop(EXTRA, middle, both)
     mine = roles(tree_of(0))[1]
     kept_small = gathered.shape[1]
@@ -559,8 +581,11 @@
         def _():
             tokens(n)
 
+        @pl.when((n >= 4) & (n < 4 + GROUP))
+        def _():
+            settle_extras(n - 4)
+
     loop(middle, limit + 2 * DEPTH * HOP, late)
-    loop(0, GROUP, settle_extras)
     for step in range(1, n_sections):
         handed(step).wait()
         table_out(place, step).wait_send()
@@ -600,7 +625,7 @@
         edge_across().wait_send()
 
     edge_beside(edge.at[0]).wait_send()
-    loop(0, limit, settle)
+    loop(limit - (SETTLED - 2 * DEPTH) * HOP, limit, settle)
 
     @pl.when(layer == 0)
     def _():
@@ -823,21 +848,41 @@
     for origin in range(n_dp):
         picks[origin] = found[origin * slots : (origin + 1) * slots]
 
-    def slots_move(step):
-        to = (me + step) % n_dp
-        return remote(
-            picks.at[to], land.at[me], s_send.at[step], s_recv.at[me], (to, section)
+    lines = n_dp // 2
+    line, lane_of = me // 2, me % 2
+
+    def slots_beside(at):
+        return remote(
+            picks.at[2 * at + 1 - lane_of], land.at[at], s_send.at[at], s_recv.at[at],
+            (me + 1 - 2 * lane_of, section),
+        )
+
+    def slots_along(step):
+        to = (line + step) % lines
+        return remote(
+            picks.at[2 * to + lane_of], land.at[lines + line], s_send.at[lines + to],
+            s_recv.at[lines + line], (2 * to + lane_of, section),
         )
 
     def slots_got(step):
-        source = (me + step) % n_dp
-        return remote(
-            picks.at[0], land.at[source], s_send.at[0], s_recv.at[source],
+        source = (line + step) % lines
+        return remote(
+            picks.at[0], land.at[lines + source], s_send.at[0], s_recv.at[lines + source],
             (me, (section + 1) % n_sections),
         )
 
-    loop(1, n_dp, lambda step: slots_move(step).start())
-    land[me] = picks[me]
+    def pass_on(step):
+        to = (line + step) % lines
+        slots_beside(to).wait_recv()
+        picks[2 * to + lane_of] = picks[2 * to + lane_of] + land[to]
+
+        @pl.when(step < lines)
+        def _():
+            slots_along(step).start()
+
+    loop(1, lines + 1, lambda step: slots_beside((line + step) % lines).start())
+    loop(1, lines + 1, pass_on)
+    land[lines + line] = picks[me]
 
     @pl.when(layer == 0)
     def _():
@@ -861,10 +906,10 @@
                 else:
                     wide[...] += term
 
-    loop(1, n_dp, lambda step: slots_got(step).wait_recv())
-    mine = land[0]
-    for origin in range(1, n_dp):
-        mine = mine + land[origin]
+    loop(1, lines, lambda step: slots_got(step).wait_recv())
+    mine = land[lines]
+    for origin in range(1, lines):
+        mine = mine + land[lines + origin]
     other[1] = mine
     other_move = remote(other.at[1], other.at[0], o_send, o_recv, (me, half))
 
@@ -1231,7 +1276,8 @@
         given_move.wait_send()
 
     loop(1, n_dp, lambda step: ids_move(step).wait_send())
-    loop(1, n_dp, lambda step: slots_move(step).wait_send())
+    loop(0, lines, lambda at: slots_beside(at).wait_send())
+    loop(1, lines, lambda step: slots_along(step).wait_send())
     ids_copy.wait()
 
 
@@ -1304,7 +1350,7 @@
     pieces, q_in, o_in, u_in, d_in, voc_in, small_ref, table_ref, act_in, ing_in,
     act_ref, ing_ref, tab_ref, voc_ref, q_ref, qvb_ref, o_ref, u_ref, upb_ref, d_ref, gains_ref,
     shifts_ref, eg_ref, es_ref,
-    q_s, o_s, u_s, d_s, q_f, o_f, u_f, d_f, in_sem, out_sem, voc_s, voc_sem,
+    q_s, o_s, u_s, d_s, q_f, o_f, u_f, d_f, act_s, ing_s, act_f, ing_f, in_sem, out_sem, voc_s, voc_sem,
 ):
     section = lax.axis_index("section")
     layer = section // 2
@@ -1321,14 +1367,11 @@
         for i in range(pieces):
             rows = pl.ds(i * count, count)
             moves.append((source.at[rows], low.at[rows], wide.at[rows], target.at[0, rows]))
+    moves.append((act_in, act_s, act_f, act_ref))
+    moves.append((ing_in, ing_s, ing_f, ing_ref))
     for i, (source, low, wide, target) in enumerate(moves):
         pltpu.make_async_copy(source, low, in_sem.at[i]).start()
 
-    voc_copy.wait()
-    voc_out = pltpu.make_async_copy(voc_s, voc_ref, voc_sem.at[1])
-    voc_out.start()
-    act_ref[...] = act_in[...].astype(F32)
-    ing_ref[...] = ing_in[...].astype(F32)
 
     parts = small_ref[...].astype(F32)
     partner = jnp.where(half == 0, parts[1], parts[3])
@@ -1357,6 +1400,9 @@
         for h in range(2):
             tab_ref[h, :, pl.ds(l * side, side)] = table_ref[2 * l + h].astype(F32)
 
+    voc_copy.wait()
+    voc_out = pltpu.make_async_copy(voc_s, voc_ref, voc_sem.at[1])
+    voc_out.start()
     for i, (source, low, wide, target) in enumerate(moves):
         pltpu.make_async_copy(source, low, in_sem.at[i]).wait()
         wide[...] = low[...].astype(F32)
@@ -1384,15 +1430,17 @@
             (2, 2, width), (2, 4, width), (width,), (width,),
         )
     ]
-    specs = [in_vmem] * 3 + [any_space] * 2 + [in_vmem, any_space, any_space, in_vmem, any_space] + [in_vmem] * 4
+    specs = [any_space] * 2 + [in_vmem] + [any_space] * 2 + [in_vmem, any_space, any_space, in_vmem, any_space] + [in_vmem] * 4
     return pl.pallas_call(
         functools.partial(finish_kernel, pieces),
         out_shape=outs,
-        in_specs=[any_space] * 5 + [in_vmem] * 4,
+        in_specs=[any_space] * 5 + [in_vmem] * 2 + [any_space] * 2,
         out_specs=specs,
         scratch_shapes=[vmem(shape, BF) for shape in shapes]
         + [vmem(shape, F32) for shape in shapes]
-        + [dma((4 * pieces,)), dma((4 * pieces,)), vmem(voc.shape, F32), dma((2,))],
+        + [vmem(act.shape, BF)] * 2
+        + [vmem(act.shape, F32)] * 2
+        + [dma((4 * pieces + 2,)), dma((4 * pieces + 2,)), vmem(voc.shape, F32), dma((2,))],
         compiler_params=pltpu.CompilerParams(vmem_limit_bytes=60 << 20),
         name="finished_outputs",
     )(*sums, voc, small, tables, act, ing)

time: 305 us -> 298 us (0.977)
  Pallas kernels: 304 us -> 297 us
    pallas_call x1, Pallas kernels: 165 us -> 153 us  [reduced(): pl.pallas_call(functools.partial(reduce_kernel, counts), out_shape=tuple(...]
    pallas_call x1, Pallas kernels: 128 us -> 132 us  [encoded(): pl.pallas_call(encoder_kernel, out_shape=(jax.ShapeDtypeStruct((2, page,...]
where the time goes in v6:
time: 298 us
  Pallas kernels  297 us (100%)
    pallas_call x1, Pallas kernels, reduced(): pl.pallas_call(functools.partial(reduce_kernel, counts), out_shape=tuple(...  153 us
    pallas_call x1, Pallas kernels, encoded(): pl.pallas_call(encoder_kernel, out_shape=(jax.ShapeDtypeStruct((2, page,...  132 us
    pallas_call x1, Pallas kernels, finished(): pl.pallas_call(functools.partial(finish_kernel, pieces), out_shape=outs,...  11.9 us

profile of v6, /device:TPU:0, one launch (start us, length us, event | category | flops | bytes accessed | tf_op | source)
XLA Modules:
  0.0 297.9 jit_solution(16953955312338822250)
XLA Ops:
  0.7 132.5 %encoder_both_ways.1 = (bf16[2,512,3456]{2,1,0:T(8,128)(2,1)}, bf16[2,512,4224]{2,1,0:T(8,128)(2,1)}, s32[8,2,128]{2,1,0:T(2,128)}, bf16[2,512,384]{2,1,0:T(8,12...) custom-call(bf16[256,768]{1,0:T(8,128)(2,1)} %words_ref.1, bf16[256,768]{1,0:T(8,128)(2,1)} %cot_ref.1, ...), custom_call_target="tpu_custom_call" | custom-call | flops 57982058496 | bytes 209715200 | tf_op jit(solution)/shard_map/encoder_both_ways/pallas_call | solution.py:1301
  133.1 152.7 %gradient_sums.1 = (bf16[768,1152]{1,0:T(8,128)(2,1)}, bf16[384,768]{1,0:T(8,128)(2,1)}, bf16[768,1536]{1,0:T(8,128)(2,1)}, bf16[1536,768]{1,0:T(8,128)(2,1)}, b...) custom-call(bf16[1024,3456]{1,0:T(8,128)(2,1)} %bitcast.5, ...), custom_call_target="tpu_custom_call" | custom-call | flops 7348420608 | bytes 419430400 | tf_op jit(solution)/shard_map/gradient_sums/pallas_call | solution.py:653
  285.8 11.9 %finished_outputs.1 = (f32[256,768]{1,0:T(8,128)}, f32[256,768]{1,0:T(8,128)}, f32[2,32,768]{2,1,0:T(8,128)}, f32[512,768]{1,0:T(8,128)}, f32[1,768,1152]{2,1,0:...) custom-call(bf16[768,1152]{1,0:T(8,128)(2,1)} %get-tuple-element.49., ...), custom_call_target="tpu_custom_call" | custom-call | tf_op jit(solution)/shard_map/finished_outputs/pallas_call | solution.py:1434

commit v7 on v6

--- a/solution.py
+++ b/solution.py
@@ -378,26 +378,30 @@
         ).wait()
         away(g).wait_send()
 
+    used = listed_ref.shape[1]
+
+    def filled(kind, c):
+        return rows.at[kind, c, pl.ds(0, used)]
+
     def slots_down(c, d):
         return remote(
-            rows.at[0, c], rows.at[0, c], r_send.at[d, c], r_recv.at[0, c],
-            (neighbour(d), section),
+            filled(0, c), filled(0, c), r_send.at[d, c], r_recv.at[0, c], (neighbour(d), section)
         )
 
     def slots_across(c):
         return remote(
-            rows.at[0, c], rows.at[1, c], r_send.at[3, c], r_recv.at[1, c], (me, other_layer)
+            filled(0, c), filled(1, c), r_send.at[3, c], r_recv.at[1, c], (me, other_layer)
         )
 
     def slots_beside(c, kind):
         return remote(
-            rows.at[kind, c], rows.at[2 + kind, c], r_send.at[4 + kind, c],
-            r_recv.at[2 + kind, c], (me, other_core),
+            filled(kind, c), filled(2 + kind, c), r_send.at[4 + kind, c], r_recv.at[2 + kind, c],
+            (me, other_core),
         )
 
     def slots_got(c, kind):
         remote(
-            rows.at[kind, c], rows.at[kind, c], r_send.at[0, c], r_recv.at[kind, c],
+            filled(kind, c), filled(kind, c), r_send.at[0, c], r_recv.at[kind, c],
             (me, other_core),
         ).wait_recv()
 
@@ -548,15 +552,16 @@
 
     spread_all(1, act_ref)
     edge_beside(edge.at[0]).wait_recv()
-    used = listed_ref.shape[1]
     listed = listed_ref[...].astype(F32)
     square[...] = jnp.full_like(square, -1.0)
     square[0:1, :used] = jnp.where(half == 0, listed[0:1], listed[1:2])
     column = square[...].T[:, 0:1]
     wanted = column == lax.broadcasted_iota(jnp.int32, (slots, edge.shape[1]), 1).astype(F32)
-    rows[0, place] = jnp.dot(
-        wanted.astype(F32).astype(BF), edge[0], preferred_element_type=F32
-    ).astype(BF)
+    for kind in range(4):
+        for c in range(GROUP):
+            rows[kind, c, used:] = jnp.zeros((slots - used, side), BF)
+    found = jnp.dot(wanted.astype(F32).astype(BF), edge[0], preferred_element_type=F32)
+    rows[0, place, :used] = found[:used].astype(BF)
 
     def both(t):
         advance(t)
@@ -1418,7 +1423,7 @@
     in_vmem = pl.BlockSpec(memory_space=pltpu.VMEM)
     dma = pltpu.SemaphoreType.DMA
     vmem = pltpu.VMEM
-    pieces = 6
+    pieces = 4
     width = act.shape[1]
     units = sums[3].shape[0]
     shapes = [array.shape for array in sums]

time: 298 us -> 296 us (level)
  no operation moved by 1% of the time
where the time goes in v7:
time: 296 us
  Pallas kernels  295 us (100%)
    pallas_call x1, Pallas kernels, reduced(): pl.pallas_call(functools.partial(reduce_kernel, counts), out_shape=tuple(...  151 us
    pallas_call x1, Pallas kernels, encoded(): pl.pallas_call(encoder_kernel, out_shape=(jax.ShapeDtypeStruct((2, page,...  132 us
    pallas_call x1, Pallas kernels, finished(): pl.pallas_call(functools.partial(finish_kernel, pieces), out_shape=outs,...  11.7 us

profile of v7, /device:TPU:0, one launch (start us, length us, event | category | flops | bytes accessed | tf_op | source)
XLA Modules:
  0.0 295.9 jit_solution(16438443060437756573)
XLA Ops:
  0.7 132.5 %encoder_both_ways.1 = (bf16[2,512,3456]{2,1,0:T(8,128)(2,1)}, bf16[2,512,4224]{2,1,0:T(8,128)(2,1)}, s32[8,2,128]{2,1,0:T(2,128)}, bf16[2,512,384]{2,1,0:T(8,12...) custom-call(bf16[256,768]{1,0:T(8,128)(2,1)} %words_ref.1, bf16[256,768]{1,0:T(8,128)(2,1)} %cot_ref.1, ...), custom_call_target="tpu_custom_call" | custom-call | flops 57982058496 | bytes 209715200 | tf_op jit(solution)/shard_map/encoder_both_ways/pallas_call | solution.py:1306
  133.1 150.9 %gradient_sums.1 = (bf16[768,1152]{1,0:T(8,128)(2,1)}, bf16[384,768]{1,0:T(8,128)(2,1)}, bf16[768,1536]{1,0:T(8,128)(2,1)}, bf16[1536,768]{1,0:T(8,128)(2,1)}, b...) custom-call(bf16[1024,3456]{1,0:T(8,128)(2,1)} %bitcast.5, ...), custom_call_target="tpu_custom_call" | custom-call | flops 7348420608 | bytes 419430400 | tf_op jit(solution)/shard_map/gradient_sums/pallas_call | solution.py:658
  284.0 11.7 %finished_outputs.1 = (f32[256,768]{1,0:T(8,128)}, f32[256,768]{1,0:T(8,128)}, f32[2,32,768]{2,1,0:T(8,128)}, f32[512,768]{1,0:T(8,128)}, f32[1,768,1152]{2,1,0:...) custom-call(bf16[768,1152]{1,0:T(8,128)(2,1)} %get-tuple-element.49., ...), custom_call_target="tpu_custom_call" | custom-call | tf_op jit(solution)/shard_map/finished_outputs/pallas_call | solution.py:1439

commit v8 on v7

--- a/solution.py
+++ b/solution.py
@@ -25,7 +25,7 @@
 DEPTH = 4
 FIRST = 20
 EXTRA = 36
-GUESTS = 6
+GUESTS = 7
 SETTLED = 9
 
 

time: 296 us -> 298 us (level)
  no operation moved by 1% of the time
where the time goes in v8:
time: 298 us
  Pallas kernels  297 us (100%)
    pallas_call x1, Pallas kernels, reduced(): pl.pallas_call(functools.partial(reduce_kernel, counts), out_shape=tuple(...  153 us
    pallas_call x1, Pallas kernels, encoded(): pl.pallas_call(encoder_kernel, out_shape=(jax.ShapeDtypeStruct((2, page,...  132 us
    pallas_call x1, Pallas kernels, finished(): pl.pallas_call(functools.partial(finish_kernel, pieces), out_shape=outs,...  11.7 us

profile of v8, /device:TPU:0, one launch (start us, length us, event | category | flops | bytes accessed | tf_op | source)
XLA Modules:
  0.0 297.9 jit_solution(842003878734005635)
XLA Ops:
  0.7 132.5 %encoder_both_ways.1 = (bf16[2,512,3456]{2,1,0:T(8,128)(2,1)}, bf16[2,512,4224]{2,1,0:T(8,128)(2,1)}, s32[8,2,128]{2,1,0:T(2,128)}, bf16[2,512,384]{2,1,0:T(8,12...) custom-call(bf16[256,768]{1,0:T(8,128)(2,1)} %words_ref.1, bf16[256,768]{1,0:T(8,128)(2,1)} %cot_ref.1, ...), custom_call_target="tpu_custom_call" | custom-call | flops 57982058496 | bytes 209715200 | tf_op jit(solution)/shard_map/encoder_both_ways/pallas_call | solution.py:1306
  133.1 152.8 %gradient_sums.1 = (bf16[768,1152]{1,0:T(8,128)(2,1)}, bf16[384,768]{1,0:T(8,128)(2,1)}, bf16[768,1536]{1,0:T(8,128)(2,1)}, bf16[1536,768]{1,0:T(8,128)(2,1)}, b...) custom-call(bf16[1024,3456]{1,0:T(8,128)(2,1)} %bitcast.5, ...), custom_call_target="tpu_custom_call" | custom-call | flops 7348420608 | bytes 419430400 | tf_op jit(solution)/shard_map/gradient_sums/pallas_call | solution.py:658
  286.0 11.7 %finished_outputs.1 = (f32[256,768]{1,0:T(8,128)}, f32[256,768]{1,0:T(8,128)}, f32[2,32,768]{2,1,0:T(8,128)}, f32[512,768]{1,0:T(8,128)}, f32[1,768,1152]{2,1,0:...) custom-call(bf16[768,1152]{1,0:T(8,128)(2,1)} %get-tuple-element.49., ...), custom_call_target="tpu_custom_call" | custom-call | tf_op jit(solution)/shard_map/finished_outputs/pallas_call | solution.py:1439
